TPU v7x, 512 devices: a whole 4x8x8 slice. The times are simulated.
512 devices in a mesh: blk: 8 (over z_lo, core), grp: 64 (over y, z_hi, x).
Axes of the slice: x: 4, y: 8, z: 8 (z_hi: 2, z_lo: 4; z = z_hi * 4 + z_lo), core: 2. Of those that a mesh axis runs over, the one named last changes fastest.
Arguments:
- picture_inputs: bfloat16 [65536, 768], P(('blk', 'grp')), may hold values from -6 to 6
- caption_inputs: bfloat16 [65536, 768], P(('blk', 'grp')), may hold values from -6 to 6
- picture_mapping: bfloat16 [768, 768], P('grp'), may hold values from -0.21875 to 0.21875
- caption_mapping: bfloat16 [768, 768], P('grp'), may hold values from -0.21875 to 0.21875
- similarity_multiplier: float32 [1], replicated, may hold values from 2 to 8
- score_constant: float32 [1], replicated, may hold values from -6 to -3
Outputs:
- img_proj_grad: float32 [768, 768], P('grp')
- txt_proj_grad: float32 [768, 768], P('grp')
- img_norms: float32 [65536], P(('blk', 'grp'))
- txt_norms: float32 [65536], P(('blk', 'grp'))
All inputs are finite; a program needn't handle non-finite values.
Results may differ from a plain program's by a relative error of at most 0.0036.
Values may be sent and summed in bfloat16 or wider, within the bound.
No kernel may reach another device: no remote copies, remote signals or barrier semaphores. Data moves between devices by JAX's collectives and lax.ppermute only.
A program may use at most 64 MiB of HBM per device.

v0:
```python
import jax
import jax.numpy as jnp
from jax import lax
from jax.sharding import PartitionSpec as P


def shifted(value, axis, by):
    devices = lax.axis_size(axis)
    return lax.ppermute(value, axis, [(i, (i + by) % devices) for i in range(devices)])


def unit_rows(projected):
    radius = jnp.sqrt(jnp.sum(projected * projected, axis=-1, keepdims=True) + 1e-06)
    return (projected / radius, radius)


def through_norm(unit, radius, upstream):
    return (upstream - unit * jnp.sum(unit * upstream, axis=-1, keepdims=True)) / radius


def on_device(
    picture_inputs,
    caption_inputs,
    picture_mapping,
    caption_mapping,
    similarity_multiplier,
    score_constant,
):
    own_rows = picture_inputs.shape[0]
    full_img_proj, full_txt_proj = (
        lax.all_gather(picture_mapping, "grp", axis=0, tiled=True),
        lax.all_gather(caption_mapping, "grp", axis=0, tiled=True),
    )
    img_out = jnp.dot(picture_inputs, full_img_proj, preferred_element_type=jnp.float32)
    txt_out = jnp.dot(caption_inputs, full_txt_proj, preferred_element_type=jnp.float32)
    img_unit, img_radius = unit_rows(img_out)
    txt_unit, txt_radius = unit_rows(txt_out)
    img_half = img_unit.astype(jnp.bfloat16)
    text_half = txt_unit.astype(jnp.bfloat16)
    multiplier_amount = similarity_multiplier[0]
    set_offset = score_constant[0]
    group_size = lax.axis_size("grp")
    loop_size = lax.axis_size("blk")
    my_group = lax.axis_index("blk")
    member_ids = jnp.arange(own_rows, dtype=jnp.int32)
    text_ids = my_group * own_rows + member_ids
    shifted_text = img_half
    carried = jnp.zeros(img_out.shape, jnp.float32)
    txt_grad = jnp.zeros(txt_out.shape, jnp.float32)
    img_grad = carried
    for turn_index in range(loop_size):
        source = (my_group - turn_index) % loop_size
        image_ids = source * own_rows + member_ids
        pair_logits = (
            multiplier_amount
            * jnp.dot(shifted_text, text_half.T, preferred_element_type=jnp.float32)
            + set_offset
        )
        pair_label_sign = jnp.where(image_ids[:, None] == text_ids[None, :], 1.0, -1.0).astype(
            jnp.float32
        )
        weight_matrices = (
            -multiplier_amount * pair_label_sign * jax.nn.sigmoid(-pair_label_sign * pair_logits)
        ).astype(jnp.bfloat16)
        img_part = jnp.dot(weight_matrices, text_half, preferred_element_type=jnp.float32)
        txt_part = lax.dot_general(
            weight_matrices,
            shifted_text,
            (((0,), (0,)), ((), ())),
            preferred_element_type=jnp.float32,
        )
        img_part, txt_part = (img_part, txt_part)
        txt_grad = txt_grad + txt_part
        carried = carried + img_part
        if turn_index + 1 < loop_size:
            shifted_text, carried = (
                shifted(shifted_text.astype(jnp.float32), "blk", 1).astype(shifted_text.dtype),
                shifted(carried, "blk", 1),
            )
        else:
            img_grad = shifted(carried, "blk", 1)
    img_pre = through_norm(img_unit, img_radius, img_grad)
    txt_pre = through_norm(txt_unit, txt_radius, txt_grad)
    img_rounded = img_pre.astype(jnp.bfloat16)
    txt_rounded = txt_pre.astype(jnp.bfloat16)
    contract = (((0,), (0,)), ((), ()))
    img_local = lax.dot_general(
        picture_inputs, img_rounded, contract, preferred_element_type=jnp.float32
    )
    txt_local = lax.dot_general(
        caption_inputs, txt_rounded, contract, preferred_element_type=jnp.float32
    )
    img_pieces, txt_pieces = (
        lax.all_to_all(img_local, "grp", split_axis=0, concat_axis=0, tiled=True),
        lax.all_to_all(txt_local, "grp", split_axis=0, concat_axis=0, tiled=True),
    )
    share = img_local.shape[0] // group_size
    img_share = jnp.sum(img_pieces.reshape(group_size, share, img_local.shape[1]), axis=0)
    txt_share = jnp.sum(txt_pieces.reshape(group_size, share, txt_local.shape[1]), axis=0)
    img_proj_grad, txt_proj_grad = lax.psum((img_share, txt_share), "blk")
    img_wide = picture_inputs.astype(jnp.float32)
    txt_wide = caption_inputs.astype(jnp.float32)
    img_norms = jnp.sqrt(jnp.sum(img_wide * img_wide, axis=-1)) * jnp.sqrt(
        jnp.sum(img_pre * img_pre, axis=-1)
    )
    txt_norms = jnp.sqrt(jnp.sum(txt_wide * txt_wide, axis=-1)) * jnp.sqrt(
        jnp.sum(txt_pre * txt_pre, axis=-1)
    )
    return (img_proj_grad, txt_proj_grad, img_norms, txt_norms)


def solution(mesh):
    in_specs = (
        P(("blk", "grp"), None),
        P(("blk", "grp"), None),
        P("grp", None),
        P("grp", None),
        P(),
        P(),
    )
    out_specs = (P("grp", None), P("grp", None), P(("blk", "grp")), P(("blk", "grp")))
    return jax.shard_map(
        on_device, mesh=mesh, in_specs=in_specs, out_specs=out_specs, check_vma=False
    )
```

profile of v0, /device:TPU:1, one launch (start us, length us, event | category | flops | bytes accessed | tf_op | source)
XLA Modules:
  0.0 666.0 jit_solution(5211288276455161907)
XLA Ops:
  7.2 0.7 all-gather.5.cloned.1.call-update
  8.0 0.7 all-gather.7.cloned.1.call-update
  10.2 137.7 %all-gather.5.cloned.1.call-done = bf16[64,12,768]{2,1,0:T(8,128)(2,1)} async-done(((bf16[1,12,768]{2,1,0:T(8,128)(2,1)}), bf16[64,12,768]{2,1,0:T(8,128)(2,1)}) %all-gather.5.cloned.1.call-update) | async-done | bytes 1179664 | tf_op jit(solution)/shard_map/all_gather | solution.py:31
  147.9 2.2 reshape.67
  150.1 0.4 multiply_reduce_fusion.7
  150.6 128.7 %all-gather.7.cloned.1.call-done = bf16[64,12,768]{2,1,0:T(8,128)(2,1)} async-done(((bf16[1,12,768]{2,1,0:T(8,128)(2,1)}), bf16[64,12,768]{2,1,0:T(8,128)(2,1)}) %all-gather.7.cloned.1.call-update) | async-done | bytes 1179664 | tf_op jit(solution)/shard_map/all_gather | solution.py:32
  279.3 2.2 reshape.69
  281.6 0.4 multiply_reduce_fusion.6
  282.2 6.2 collective-permute-start.1
  288.5 0.3 fusion.68
  288.8 0.3 fusion.90
  289.0 1.9 collective-permute-done.1
  291.0 4.4 collective-permute-start.3
  295.4 0.2 fusion.67
  295.6 0.2 convolution_add_fusion.1
  295.9 2.1 collective-permute-done.3
  298.0 4.4 collective-permute-start.5
  302.3 0.2 fusion.66
  302.6 4.2 collective-permute-done.5
  306.7 2.6 collective-permute-start.7
  309.8 5.7 collective-permute-done.7
  315.5 1.9 collective-permute-start.9
  317.4 0.2 fusion.64
  317.9 6.3 collective-permute-done.9
  324.3 1.9 collective-permute-start.11
  326.7 6.4 collective-permute-done.11
  333.1 1.9 collective-permute-start.13
  335.5 6.4 collective-permute-done.13
  342.1 0.6 copy-done.7
  342.9 0.4 multiply_reduce_fusion.4
  343.3 0.2 multiply_reduce_fusion
  343.6 0.5 convolution_bitcast_fusion
  344.1 1.8 all_to_all.14
  345.9 7.2 %all-to-all-start.1 = ((f32[64,12,768]{2,1,0:T(8,128)}), f32[64,12,768]{2,1,0:T(8,128)S(1)}, u32[]{:S(2)}, u32[]{:S(2)}) async-start(f32[64,12,768]{2,1,0:T(8,128)} %all_to_all.14), calls=%async_computation.1 | async-start | bytes 6291456 | tf_op jit(solution)/shard_map/all_to_all | solution.py:95
  353.1 1.0 fusion.94
  354.1 1.9 collective-permute-start
  356.0 70.5 %collective-permute-done = f32[128,768]{1,0:T(8,128)S(1)} collective-permute-done((f32[128,768]{1,0:T(8,128)S(1)}, f32[128,768]{1,0:T(8,128)S(1)}, u32[]{:S(2)}, u32[]{:S(2)}) %collective-permute-start) | collective-permute-done | bytes 393248 | tf_op jit(solution)/shard_map/ppermute | solution.py:9
  426.5 0.9 convolution_add_fusion.2
  427.4 4.4 collective-permute-start.2
  432.0 4.5 collective-permute-done.2
  436.6 4.4 collective-permute-start.4
  441.2 4.5 collective-permute-done.4
  445.7 4.4 collective-permute-start.6
  450.3 4.5 collective-permute-done.6
  454.9 4.4 collective-permute-start.8
  459.5 4.5 collective-permute-done.8
  464.0 4.4 collective-permute-start.10
  468.6 4.8 collective-permute-done.10
  473.5 4.1 collective-permute-start.12
  477.8 6.6 collective-permute-done.12
  484.4 2.3 collective-permute-start.14
  486.7 8.6 %collective-permute-done.14 = f32[128,768]{1,0:T(8,128)S(1)} collective-permute-done((f32[128,768]{1,0:T(8,128)S(1)}, f32[128,768]{1,0:T(8,128)S(1)}, u32[]{:S(2)}, u32[]{:S(2)}) %collective-permute-start.14) | collective-permute-done | bytes 393248 | tf_op jit(solution)/shard_map/ppermute | solution.py:9
  495.5 0.2 multiply_reduce_fusion.2
  495.8 2.0 convolution_bitcast_fusion.1
  497.8 3.6 all_to_all.12
  501.3 10.7 %all-to-all-start = ((f32[64,12,768]{2,1,0:T(8,128)}), f32[64,12,768]{2,1,0:T(8,128)}, u32[]{:S(2)}, u32[]{:S(2)}) async-start(f32[64,12,768]{2,1,0:T(8,128)} %all_to_all.12), calls=%async_computation | async-start | bytes 6291456 | tf_op jit(solution)/shard_map/all_to_all | solution.py:94
  512.3 0.5 sqrt_multiply_fusion
  512.9 0.8 reduce_sum.95
  513.7 64.5 %all-to-all-done = f32[64,12,768]{2,1,0:T(8,128)} async-done(((f32[64,12,768]{2,1,0:T(8,128)}), f32[64,12,768]{2,1,0:T(8,128)}, u32[]{:S(2)}, u32[]{:S(2)}) %all-to-all-start) | async-done | bytes 2359328 | tf_op jit(solution)/shard_map/all_to_all | solution.py:94
  578.1 2.7 reduce_sum.93
  580.9 0.5 sqrt_multiply_fusion.1
  581.4 75.2 %all-reduce.3.cloned.1.call-done = (f32[12,768]{1,0:T(8,128)}, f32[12,768]{1,0:T(8,128)}) async-done(((f32[12,768]{1,0:T(8,128)}, f32[12,768]{1,0:T(8,128)}), (f32[12,768]{1,0:T(8,128)}, f32[12,768]{1,0:T(8,128)})) %all-reduce.3.cloned.1.call-update) | async-done | bytes 73744 | tf_op jit(solution)/shard_map/psum | solution.py:100
  656.6 1.4 copy.14
  658.0 1.4 copy.15
  (78 shorter events, 4.4 us)
Async XLA Ops:
  7.2 143.0 %copy-start.2 = (bf16[128,768]{1,0:T(8,128)(2,1)S(1)}, bf16[128,768]{1,0:T(8,128)(2,1)}, u32[]{:S(2)}) copy-start(bf16[128,768]{1,0:T(8,128)(2,1)} %param.6) | copy-start | bytes 589828
  7.2 140.7 %all-gather.5.cloned.1.call-start = ((), (), s32[]{:S(2)}) async-start(), calls=%async_computation.2 | async-start | bytes 1597440 | tf_op jit(solution)/shard_map/all_gather | solution.py:31
  7.9 271.4 %all-gather.7.cloned.1.call-start = ((), (), s32[]{:S(2)}) async-start(), calls=%async_computation.3 | async-start | bytes 1597440 | tf_op jit(solution)/shard_map/all_gather | solution.py:32
  150.6 138.2 %copy-start = (f32[128,768]{1,0:T(8,128)}, f32[128,768]{1,0:T(8,128)S(1)}, u32[]{:S(2)}) copy-start(f32[128,768]{1,0:T(8,128)S(1)} %get-tuple-element.13) | copy-start | bytes 1179652
  150.6 131.0 %copy-start.3 = (bf16[128,768]{1,0:T(8,128)(2,1)S(1)}, bf16[128,768]{1,0:T(8,128)(2,1)}, u32[]{:S(2)}) copy-start(bf16[128,768]{1,0:T(8,128)(2,1)} %param.7) | copy-start | bytes 589828
  282.2 8.8 %collective-permute-start.1 = (bf16[128,768]{1,0:T(8,128)(2,1)S(1)}, bf16[128,768]{1,0:T(8,128)(2,1)S(1)}, u32[]{:S(2)}, u32[]{:S(2)}) collective-permute-start(bf16[128,768]{1,0:T(8,128)(2,1)S(1)} %convert_convert_fusion.6), channel_id=1, source_target_pairs={{0,64},{64,128},{128,192},{192,256},{256,320},{320,384},{384,448},... | collective-permute-start | bytes 589832 | tf_op jit(solution)/shard_map/ppermute | solution.py:9
  288.8 6.6 copy-start.18
  291.0 7.0 %collective-permute-start.3 = (bf16[128,768]{1,0:T(8,128)(2,1)S(1)}, bf16[128,768]{1,0:T(8,128)(2,1)S(1)}, u32[]{:S(2)}, u32[]{:S(2)}) collective-permute-start(bf16[128,768]{1,0:T(8,128)(2,1)S(1)} %collective-permute-done.1), channel_id=1, source_target_pairs={{0,64},{64,128},{128,192},{192,256},{256,320},{320,384},{384,448},... | collective-permute-start | bytes 589832 | tf_op jit(solution)/shard_map/ppermute | solution.py:9
  295.6 22.1 %copy-start.13 = (bf16[128,128]{1,0:T(8,128)(2,1)}, bf16[128,128]{1,0:T(8,128)(2,1)S(1)}, u32[]{:S(2)}) copy-start(bf16[128,128]{1,0:T(8,128)(2,1)S(1)} %fusion.67) | copy-start | bytes 98308
  298.0 8.8 %collective-permute-start.5 = (bf16[128,768]{1,0:T(8,128)(2,1)S(1)}, bf16[128,768]{1,0:T(8,128)(2,1)S(1)}, u32[]{:S(2)}, u32[]{:S(2)}) collective-permute-start(bf16[128,768]{1,0:T(8,128)(2,1)S(1)} %collective-permute-done.3), channel_id=1, source_target_pairs={{0,64},{64,128},{128,192},{192,256},{256,320},{320,384},{384,448},... | collective-permute-start | bytes 589832 | tf_op jit(solution)/shard_map/ppermute | solution.py:9
  302.6 40.4 %copy-start.5 = (bf16[128,128]{1,0:T(8,128)(2,1)}, bf16[128,128]{1,0:T(8,128)(2,1)S(1)}, u32[]{:S(2)}) copy-start(bf16[128,128]{1,0:T(8,128)(2,1)S(1)} %fusion.66) | copy-start | bytes 98308
  306.7 8.8 %collective-permute-start.7 = (bf16[128,768]{1,0:T(8,128)(2,1)S(1)}, bf16[128,768]{1,0:T(8,128)(2,1)S(1)}, u32[]{:S(2)}, u32[]{:S(2)}) collective-permute-start(bf16[128,768]{1,0:T(8,128)(2,1)S(1)} %collective-permute-done.5), channel_id=1, source_target_pairs={{0,64},{64,128},{128,192},{192,256},{256,320},{320,384},{384,448},... | collective-permute-start | bytes 589832 | tf_op jit(solution)/shard_map/ppermute | solution.py:9
  309.5 7.9 %copy-start.16 = (bf16[128,128]{1,0:T(8,128)(2,1)}, bf16[128,128]{1,0:T(8,128)(2,1)S(1)}, u32[]{:S(2)}) copy-start(bf16[128,128]{1,0:T(8,128)(2,1)S(1)} %fusion.65) | copy-start | bytes 98308
  315.5 8.8 %collective-permute-start.9 = (bf16[128,768]{1,0:T(8,128)(2,1)S(1)}, bf16[128,768]{1,0:T(8,128)(2,1)S(1)}, u32[]{:S(2)}, u32[]{:S(2)}) collective-permute-start(bf16[128,768]{1,0:T(8,128)(2,1)S(1)} %collective-permute-done.7), channel_id=1, source_target_pairs={{0,64},{64,128},{128,192},{192,256},{256,320},{320,384},{384,448},... | collective-permute-start | bytes 589832 | tf_op jit(solution)/shard_map/ppermute | solution.py:9
  317.7 8.5 %copy-start.14 = (bf16[128,128]{1,0:T(8,128)(2,1)}, bf16[128,128]{1,0:T(8,128)(2,1)S(1)}, u32[]{:S(2)}) copy-start(bf16[128,128]{1,0:T(8,128)(2,1)S(1)} %fusion.64) | copy-start | bytes 98308
  324.3 8.8 %collective-permute-start.11 = (bf16[128,768]{1,0:T(8,128)(2,1)S(1)}, bf16[128,768]{1,0:T(8,128)(2,1)S(1)}, u32[]{:S(2)}, u32[]{:S(2)}) collective-permute-start(bf16[128,768]{1,0:T(8,128)(2,1)S(1)} %collective-permute-done.9), channel_id=1, source_target_pairs={{0,64},{64,128},{128,192},{192,256},{256,320},{320,384},{384,448},... | collective-permute-start | bytes 589832 | tf_op jit(solution)/shard_map/ppermute | solution.py:9
  326.5 8.5 %copy-start.11 = (bf16[128,128]{1,0:T(8,128)(2,1)}, bf16[128,128]{1,0:T(8,128)(2,1)S(1)}, u32[]{:S(2)}) copy-start(bf16[128,128]{1,0:T(8,128)(2,1)S(1)} %fusion.63) | copy-start | bytes 98308
  333.1 8.8 %collective-permute-start.13 = (bf16[128,768]{1,0:T(8,128)(2,1)S(1)}, bf16[128,768]{1,0:T(8,128)(2,1)S(1)}, u32[]{:S(2)}, u32[]{:S(2)}) collective-permute-start(bf16[128,768]{1,0:T(8,128)(2,1)S(1)} %collective-permute-done.11), channel_id=1, source_target_pairs={{0,64},{64,128},{128,192},{192,256},{256,320},{320,384},{384,448},... | collective-permute-start | bytes 589832 | tf_op jit(solution)/shard_map/ppermute | solution.py:9
  335.2 6.6 copy-start.9
  342.1 0.6 copy-start.7
  345.9 155.4 %all-to-all-start.1 = ((f32[64,12,768]{2,1,0:T(8,128)}), f32[64,12,768]{2,1,0:T(8,128)S(1)}, u32[]{:S(2)}, u32[]{:S(2)}) async-start(f32[64,12,768]{2,1,0:T(8,128)} %all_to_all.14), calls=%async_computation.1 | async-start | bytes 6291456 | tf_op jit(solution)/shard_map/all_to_all | solution.py:95
  353.1 78.7 %copy-start.6 = (bf16[128,128]{1,0:T(8,128)(2,1)S(1)}, bf16[128,128]{1,0:T(8,128)(2,1)}, u32[]{:S(2)}) copy-start(bf16[128,128]{1,0:T(8,128)(2,1)} %copy-done.5) | copy-start | bytes 98308
  353.1 87.9 %copy-start.17 = (bf16[128,128]{1,0:T(8,128)(2,1)S(1)}, bf16[128,128]{1,0:T(8,128)(2,1)}, u32[]{:S(2)}) copy-start(bf16[128,128]{1,0:T(8,128)(2,1)} %copy-done.16) | copy-start | bytes 98308
  354.1 72.4 %collective-permute-start = (f32[128,768]{1,0:T(8,128)S(1)}, f32[128,768]{1,0:T(8,128)S(1)}, u32[]{:S(2)}, u32[]{:S(2)}) collective-permute-start(f32[128,768]{1,0:T(8,128)S(1)} %fusion.94), channel_id=1, source_target_pairs={{0,64},{64,128},{128,192},{192,256},{256,320},{320,384},{384,448},... | collective-permute-start | bytes 1179656 | tf_op jit(solution)/shard_map/ppermute | solution.py:9
  427.4 9.1 %collective-permute-start.2 = (f32[128,768]{1,0:T(8,128)S(1)}, f32[128,768]{1,0:T(8,128)S(1)}, u32[]{:S(2)}, u32[]{:S(2)}) collective-permute-start(f32[128,768]{1,0:T(8,128)S(1)} %convolution_add_fusion.2), channel_id=1, source_target_pairs={{0,64},{64,128},{128,192},{192,256},{256,320},{320,384},{384,448},... | collective-permute-start | bytes 1179656 | tf_op jit(solution)/shard_map/ppermute | solution.py:9
  432.0 18.1 %copy-start.15 = (bf16[128,128]{1,0:T(8,128)(2,1)S(1)}, bf16[128,128]{1,0:T(8,128)(2,1)}, u32[]{:S(2)}) copy-start(bf16[128,128]{1,0:T(8,128)(2,1)} %copy-done.14) | copy-start | bytes 98308
  436.6 9.1 %collective-permute-start.4 = (f32[128,768]{1,0:T(8,128)S(1)}, f32[128,768]{1,0:T(8,128)S(1)}, u32[]{:S(2)}, u32[]{:S(2)}) collective-permute-start(f32[128,768]{1,0:T(8,128)S(1)} %add.263), channel_id=1, source_target_pairs={{0,64},{64,128},{128,192},{192,256},{256,320},{320,384},{384,448},... | collective-permute-start | bytes 1179656 | tf_op jit(solution)/shard_map/ppermute | solution.py:9
  441.2 18.1 %copy-start.12 = (bf16[128,128]{1,0:T(8,128)(2,1)S(1)}, bf16[128,128]{1,0:T(8,128)(2,1)}, u32[]{:S(2)}) copy-start(bf16[128,128]{1,0:T(8,128)(2,1)} %copy-done.11) | copy-start | bytes 98308
  445.7 9.1 %collective-permute-start.6 = (f32[128,768]{1,0:T(8,128)S(1)}, f32[128,768]{1,0:T(8,128)S(1)}, u32[]{:S(2)}, u32[]{:S(2)}) collective-permute-start(f32[128,768]{1,0:T(8,128)S(1)} %add.269), channel_id=1, source_target_pairs={{0,64},{64,128},{128,192},{192,256},{256,320},{320,384},{384,448},... | collective-permute-start | bytes 1179656 | tf_op jit(solution)/shard_map/ppermute | solution.py:9
  450.3 18.1 %copy-start.10 = (bf16[128,128]{1,0:T(8,128)(2,1)S(1)}, bf16[128,128]{1,0:T(8,128)(2,1)}, u32[]{:S(2)}) copy-start(bf16[128,128]{1,0:T(8,128)(2,1)} %copy-done.9) | copy-start | bytes 98308
  454.9 9.1 %collective-permute-start.8 = (f32[128,768]{1,0:T(8,128)S(1)}, f32[128,768]{1,0:T(8,128)S(1)}, u32[]{:S(2)}, u32[]{:S(2)}) collective-permute-start(f32[128,768]{1,0:T(8,128)S(1)} %add.275), channel_id=1, source_target_pairs={{0,64},{64,128},{128,192},{192,256},{256,320},{320,384},{384,448},... | collective-permute-start | bytes 1179656 | tf_op jit(solution)/shard_map/ppermute | solution.py:9
  459.5 18.1 %copy-start.8 = (bf16[128,128]{1,0:T(8,128)(2,1)S(1)}, bf16[128,128]{1,0:T(8,128)(2,1)}, u32[]{:S(2)}) copy-start(bf16[128,128]{1,0:T(8,128)(2,1)} %copy-done.7) | copy-start | bytes 98308
  464.0 9.4 %collective-permute-start.10 = (f32[128,768]{1,0:T(8,128)S(1)}, f32[128,768]{1,0:T(8,128)S(1)}, u32[]{:S(2)}, u32[]{:S(2)}) collective-permute-start(f32[128,768]{1,0:T(8,128)S(1)} %add.281), channel_id=1, source_target_pairs={{0,64},{64,128},{128,192},{192,256},{256,320},{320,384},{384,448},... | collective-permute-start | bytes 1179656 | tf_op jit(solution)/shard_map/ppermute | solution.py:9
  468.6 26.7 %copy-start.1 = (f32[128,768]{1,0:T(8,128)S(1)}, f32[128,768]{1,0:T(8,128)}, u32[]{:S(2)}) copy-start(f32[128,768]{1,0:T(8,128)} %copy-done) | copy-start | bytes 1179652
  473.5 10.9 %collective-permute-start.12 = (f32[128,768]{1,0:T(8,128)S(1)}, f32[128,768]{1,0:T(8,128)S(1)}, u32[]{:S(2)}, u32[]{:S(2)}) collective-permute-start(f32[128,768]{1,0:T(8,128)S(1)} %add.287), channel_id=1, source_target_pairs={{0,64},{64,128},{128,192},{192,256},{256,320},{320,384},{384,448},... | collective-permute-start | bytes 1179656 | tf_op jit(solution)/shard_map/ppermute | solution.py:9
  484.4 10.9 %collective-permute-start.14 = (f32[128,768]{1,0:T(8,128)S(1)}, f32[128,768]{1,0:T(8,128)S(1)}, u32[]{:S(2)}, u32[]{:S(2)}) collective-permute-start(f32[128,768]{1,0:T(8,128)S(1)} %add.293), channel_id=1, source_target_pairs={{0,64},{64,128},{128,192},{192,256},{256,320},{320,384},{384,448},... | collective-permute-start | bytes 1179656 | tf_op jit(solution)/shard_map/ppermute | solution.py:9
  501.3 10.9 %copy-start.4 = (bf16[128,768]{1,0:T(8,128)(2,1)S(1)}, bf16[128,768]{1,0:T(8,128)(2,1)}, u32[]{:S(2)}) copy-start(bf16[128,768]{1,0:T(8,128)(2,1)} %param.7) | copy-start | bytes 589828
  501.3 76.8 %all-to-all-start = ((f32[64,12,768]{2,1,0:T(8,128)}), f32[64,12,768]{2,1,0:T(8,128)}, u32[]{:S(2)}, u32[]{:S(2)}) async-start(f32[64,12,768]{2,1,0:T(8,128)} %all_to_all.12), calls=%async_computation | async-start | bytes 6291456 | tf_op jit(solution)/shard_map/all_to_all | solution.py:94
  512.0 144.6 %all-reduce.3.cloned.1.call-start = ((), (), s32[]{:S(2)}) async-start(), calls=%async_computation.4 | async-start | bytes 196608 | tf_op jit(solution)/shard_map/psum | solution.py:100
Sparse Core Ops, SparseCore 0:
  12.4 135.4 all-gather.4
  152.3 127.0 all-gather.6
  581.0 75.5 all-reduce.2
where the time goes:
time: 668 us; the launch traced here: 666 us
  waiting for transfers between devices  549 us (82%)
  starting transfers between devices  71.4 us (11%)
  between operations  15.9 us (2%)
  local copies, waits for them, and re-layouts  13.4 us (2%)
  matrix products  10.3 us (2%)
    ppermute x15, waiting for transfers between devices, shifted(): lax.ppermute(value, axis, [(i, (i + by) % devices) for i in range(devices)])  141 us
    all_gather x1, waiting for transfers between devices, on_device(): lax.all_gather(picture_mapping, 'grp', axis=0, tiled=True)  138 us
    all_gather x1, waiting for transfers between devices, on_device(): lax.all_gather(caption_mapping, 'grp', axis=0, tiled=True)  129 us
    psum x1, waiting for transfers between devices, on_device(): img_proj_grad, txt_proj_grad = lax.psum((img_share, txt_share), 'blk')  75.2 us
    all_to_all x1, waiting for transfers between devices, on_device(): lax.all_to_all(img_local, 'grp', split_axis=0, concat_axis=0, tiled=True)  64.5 us
    ppermute x15, starting transfers between devices, shifted(): lax.ppermute(value, axis, [(i, (i + by) % devices) for i in range(devices)])  53.4 us
  transfers between devices with their start and end apart: 20, of which 19 were waited for; matrix products, arithmetic and copies ran while one was open for 2% of the time, Pallas kernels for 0%

commit v1 on v0

v1 whole, which is shorter than its diff:
```python
import jax
import jax.numpy as jnp
from jax import lax
from jax.sharding import Mesh, PartitionSpec as P

EVERY = ("zlo", "core", "y", "zhi", "x")
SWAP = [(0, 1), (1, 0)]


def turned(value, axis, by):
    count = lax.axis_size(axis)
    return lax.ppermute(value, axis, [(i, (i + by) % count) for i in range(count)])


def spread(value, axis):
    count = lax.axis_size(axis)
    copies = jnp.broadcast_to(value[None], (count,) + value.shape)
    return lax.all_to_all(copies, axis, split_axis=0, concat_axis=0)


def on_device(
    picture_inputs,
    caption_inputs,
    picture_mapping,
    caption_mapping,
    similarity_multiplier,
    score_constant,
):
    own, width = picture_inputs.shape
    embed = picture_mapping.shape[1]
    share = picture_mapping.shape[0]
    first = lax.axis_index("core") == 0
    chips = lax.axis_size("zlo")
    n_y, n_zhi, n_x = lax.axis_size("y"), lax.axis_size("zhi"), lax.axis_size("x")
    mine = jnp.where(first, picture_inputs, caption_inputs)
    sent = jnp.where(first, caption_inputs, picture_inputs)
    chunk = jnp.concatenate([mine, lax.ppermute(sent, "core", SWAP)], axis=0)
    from_1, from_3 = turned(chunk, "zlo", 1), turned(chunk, "zlo", 3)
    from_2 = turned(chunk, "zlo", 2)
    piece = jnp.where(first, picture_mapping, caption_mapping)
    paired = jnp.concatenate([piece, lax.ppermute(piece, "zhi", SWAP)], axis=0)
    near = spread(paired, "y").reshape(n_y * n_zhi * share, embed)
    after = jnp.minimum(jnp.abs(from_1[0, 0]), 0) + jnp.minimum(jnp.abs(from_3[0, 0]), 0)
    gathered = spread(near + after, "x").reshape(width, embed)
    rows = jnp.concatenate([chunk, from_1, from_2, from_3], axis=0)
    at = jnp.arange(width, dtype=jnp.int32)
    owner, row = at // share, at % share
    at_half = (owner // n_x) % n_zhi
    at_half = jnp.where(lax.axis_index("zhi") == 0, at_half, 1 - at_half)
    place = (((owner % n_x) * n_y + owner // (n_x * n_zhi)) * n_zhi + at_half) * share + row
    order = (place[:, None] == at[None, :]).astype(jnp.bfloat16)
    mapping = jnp.dot(order, gathered, preferred_element_type=jnp.float32).astype(jnp.bfloat16)
    out = jnp.dot(rows, mapping, preferred_element_type=jnp.float32)
    radius = jnp.sqrt(jnp.sum(out * out, axis=-1, keepdims=True) + 1e-06)
    unit = out / radius
    half = unit.astype(jnp.bfloat16)
    partner = lax.ppermute(half, "core", SWAP)
    multiplier_amount = similarity_multiplier[0]
    logits = (
        multiplier_amount * jnp.dot(half, partner.T, preferred_element_type=jnp.float32)
        + score_constant[0]
    )
    ids = jnp.arange(rows.shape[0], dtype=jnp.int32)
    other_ids = ids + own - 2 * own * ((ids // own) % 2)
    sign = jnp.where(ids[:, None] == other_ids[None, :], 1.0, -1.0).astype(jnp.float32)
    weights = (-multiplier_amount * sign * jax.nn.sigmoid(-sign * logits)).astype(jnp.bfloat16)
    grad = jnp.dot(weights, partner, preferred_element_type=jnp.float32)
    pre = (grad - unit * jnp.sum(unit * grad, axis=-1, keepdims=True)) / radius
    columns = embed // chips
    part = lax.dynamic_slice_in_dim(pre, lax.axis_index("zlo") * columns, columns, axis=1)
    local = lax.dot_general(
        rows,
        part.astype(jnp.bfloat16),
        (((0,), (0,)), ((), ())),
        preferred_element_type=jnp.float32,
    )
    pieces = lax.all_to_all(
        local.astype(jnp.bfloat16).reshape(width // share, share, columns),
        ("y", "zhi", "x"),
        split_axis=0,
        concat_axis=0,
        tiled=True,
    )
    total = jnp.sum(pieces.astype(jnp.float32), axis=0)
    whole = spread(total, ("zlo", "core")).reshape(chips, 2, share, columns)
    whole = whole.transpose(1, 2, 0, 3).reshape(2, share, embed)
    wide = chunk.astype(jnp.float32)
    pre_chunk = pre[: 2 * own]
    norms = jnp.sqrt(jnp.sum(wide * wide, axis=-1)) * jnp.sqrt(
        jnp.sum(pre_chunk * pre_chunk, axis=-1)
    )
    own_norms = norms[:own]
    their_norms = lax.ppermute(norms[own:], "core", SWAP)
    img_norms = jnp.where(first, own_norms, their_norms)
    txt_norms = jnp.where(first, their_norms, own_norms)
    return (whole[0], whole[1], img_norms, txt_norms)


def solution(mesh):
    fine = Mesh(mesh.devices.reshape(4, 2, 8, 2, 4), EVERY)
    grp = ("y", "zhi", "x")
    in_specs = (P(EVERY, None), P(EVERY, None), P(grp, None), P(grp, None), P(), P())
    out_specs = (P(grp, None), P(grp, None), P(EVERY), P(EVERY))
    return jax.shard_map(
        on_device, mesh=fine, in_specs=in_specs, out_specs=out_specs, check_vma=False
    )
```

time: 668 us -> 159 us (0.24)
  waiting for transfers between devices: 549 us -> 55.8 us
  between operations: 15.9 us -> 3.51 us
  starting transfers between devices: 71.4 us -> 64 us
    all_gather x2 -> x0, waiting for transfers between devices: 266 us -> none  [the longest x1 138 us: on_device(): lax.all_gather(picture_mapping, 'grp', axis=0, tiled=True)]
    ppermute x15 -> x7, waiting for transfers between devices: 141 us -> 36.2 us  [the longest x3 31 us: turned(): lax.ppermute(value, axis, [(i, (i + by) % count) for i in range(count)])]
    psum x1 -> x0, waiting for transfers between devices: 75.2 us -> none  [on_device(): img_proj_grad, txt_proj_grad = lax.psum((img_share, txt_share), 'blk')]
    all_to_all x2 -> x4, waiting for transfers between devices: 64.5 us -> 19.5 us  [the longest x1 14.2 us: on_device(): lax.all_to_all(local.astype(jnp.bfloat16).reshape(width // share, share,...]
    ppermute x15 -> x7, starting transfers between devices: 53.4 us -> 31.2 us  [the longest x3 11.3 us: turned(): lax.ppermute(value, axis, [(i, (i + by) % count) for i in range(count)])]
    all_to_all x2 -> x4, starting transfers between devices: 17.9 us -> 32.7 us  [the longest x3 17.7 us: spread(): return lax.all_to_all(copies, axis, split_axis=0, concat_axis=0)]
    dot_general x28 -> x3, matrix products: 10.3 us -> 13.8 us  [the longest x1 8.07 us: on_device(): grad = jnp.dot(weights, partner, preferred_element_type=jnp.float32)]
  transfers between devices with their start and end apart: 20 -> 11, of which waited for: 19 -> 7; matrix products, arithmetic and copies ran while one was open for 2% -> 5% of each run, Pallas kernels for 0% -> 0%
where the time goes in v1:
time: 159 us; the launch traced here: 158 us
  starting transfers between devices  64 us (40%)
  waiting for transfers between devices  55.8 us (35%)
  matrix products  13.8 us (9%)
  local copies, waits for them, and re-layouts  12.3 us (8%)
  other arithmetic  8.39 us (5%)
  between operations  3.51 us (2%)
    ppermute x3, waiting for transfers between devices, turned(): lax.ppermute(value, axis, [(i, (i + by) % count) for i in range(count)])  31 us
    all_to_all x3, starting transfers between devices, spread(): return lax.all_to_all(copies, axis, split_axis=0, concat_axis=0)  17.7 us
    all_to_all x1, starting transfers between devices, on_device(): lax.all_to_all(local.astype(jnp.bfloat16).reshape(width // share, share,...  15 us
    all_to_all x1, waiting for transfers between devices, on_device(): lax.all_to_all(local.astype(jnp.bfloat16).reshape(width // share, share,...  14.2 us
    ppermute x3, starting transfers between devices, turned(): lax.ppermute(value, axis, [(i, (i + by) % count) for i in range(count)])  11.3 us
    ppermute x1, starting transfers between devices, on_device(): chunk = jnp.concatenate([mine, lax.ppermute(sent, 'core', SWAP)], axis=0)  8.79 us
    dot_general x1, matrix products, on_device(): grad = jnp.dot(weights, partner, preferred_element_type=jnp.float32)  8.07 us
    unnamed x15, local copies, waits for them, and re-layouts  5.87 us
  transfers between devices with their start and end apart: 11, of which 7 were waited for; matrix products, arithmetic and copies ran while one was open for 5% of the time, Pallas kernels for 0%

profile of v1, /device:TPU:1, one launch (start us, length us, event | category | flops | bytes accessed | tf_op | source)
XLA Modules:
  0.0 157.7 jit_solution(2281759307767632900)
XLA Ops:
  0.6 1.1 constant_dynamic-update-slice_fusion.4
  1.7 8.8 %collective-permute-start = (bf16[128,768]{1,0:T(8,128)(2,1)S(1)}, bf16[128,768]{1,0:T(8,128)(2,1)S(1)}, u32[]{:S(2)}, u32[]{:S(2)}) collective-permute-start(bf16[128,768]{1,0:T(8,128)(2,1)S(1)} %get-tuple-element.8), channel_id=1, source_target_pairs={{0,64},{64,0},{1,65},{65,1},{2,66},{66,2},{3,67},{67,3},{4,68},{68... | collective-permute-start | bytes 589832 | tf_op jit(solution)/shard_map/ppermute | solution.py:37
  10.5 0.8 broadcast_select_fusion.2
  11.3 5.3 %collective-permute-start.4 = (bf16[12,768]{1,0:T(8,128)(2,1)S(1)}, bf16[12,768]{1,0:T(8,128)(2,1)S(1)}, u32[]{:S(2)}, u32[]{:S(2)}) collective-permute-start(bf16[12,768]{1,0:T(8,128)(2,1)S(1)} %broadcast_select_fusion.2), channel_id=1, source_target_pairs={{0,4},{4,0},{1,5},{5,1},{2,6},{6,2},{3,7},{7,3},{8,12},{12,8},{9,1... | collective-permute-start | bytes 55304 | tf_op jit(solution)/shard_map/ppermute | solution.py:41
  16.5 3.2 %collective-permute-done.4 = bf16[12,768]{1,0:T(8,128)(2,1)S(1)} collective-permute-done((bf16[12,768]{1,0:T(8,128)(2,1)S(1)}, bf16[12,768]{1,0:T(8,128)(2,1)S(1)}, u32[]{:S(2)}, u32[]{:S(2)}) %collective-permute-start.4) | collective-permute-done | bytes 18464 | tf_op jit(solution)/shard_map/ppermute | solution.py:41
  19.8 0.7 broadcast_in_dim.14
  20.5 5.2 %all-to-all-start = ((bf16[8,24,768]{2,1,0:T(8,128)(2,1)}), bf16[8,24,768]{2,1,0:T(8,128)(2,1)S(1)}, u32[]{:S(2)}, u32[]{:S(2)}) async-start(bf16[8,24,768]{2,1,0:T(8,128)(2,1)} %broadcast_in_dim.14), calls=%async_computation | async-start | bytes 589824 | tf_op jit(solution)/shard_map/all_to_all | solution.py:18
  25.7 0.0 collective-permute-done
  25.7 0.0 copy-start.4
  25.7 4.9 %collective-permute-start.3 = (bf16[256,768]{1,0:T(8,128)(2,1)S(1)}, bf16[256,768]{1,0:T(8,128)(2,1)S(1)}, u32[]{:S(2)}, u32[]{:S(2)}) collective-permute-start(bf16[256,768]{1,0:T(8,128)(2,1)S(1)} %pad_maximum_fusion), channel_id=1, source_target_pairs={{0,384},{128,0},{256,128},{384,256},{1,385},{129,1},{257,129},{385... | collective-permute-start | bytes 1179656 | tf_op jit(solution)/shard_map/ppermute | solution.py:12
  30.7 1.9 %collective-permute-start.1 = (bf16[256,768]{1,0:T(8,128)(2,1)S(1)}, bf16[256,768]{1,0:T(8,128)(2,1)S(1)}, u32[]{:S(2)}, u32[]{:S(2)}) collective-permute-start(bf16[256,768]{1,0:T(8,128)(2,1)S(1)} %pad_maximum_fusion), channel_id=1, source_target_pairs={{0,128},{128,256},{256,384},{384,0},{1,129},{129,257},{257,385},{3... | collective-permute-start | bytes 1179656 | tf_op jit(solution)/shard_map/ppermute | solution.py:12
  32.6 5.7 %collective-permute-done.3 = bf16[256,768]{1,0:T(8,128)(2,1)S(1)} collective-permute-done((bf16[256,768]{1,0:T(8,128)(2,1)S(1)}, bf16[256,768]{1,0:T(8,128)(2,1)S(1)}, u32[]{:S(2)}, u32[]{:S(2)}) %collective-permute-start.3) | collective-permute-done | bytes 393248 | tf_op jit(solution)/shard_map/ppermute | solution.py:12
  38.2 0.5 slice.31
  39.4 9.1 %collective-permute-done.1 = bf16[256,768]{1,0:T(8,128)(2,1)S(1)} collective-permute-done((bf16[256,768]{1,0:T(8,128)(2,1)S(1)}, bf16[256,768]{1,0:T(8,128)(2,1)S(1)}, u32[]{:S(2)}, u32[]{:S(2)}) %collective-permute-start.1) | collective-permute-done | bytes 393248 | tf_op jit(solution)/shard_map/ppermute | solution.py:12
  48.5 0.0 copy-start.5
  48.5 0.5 slice.30
  49.7 0.0 all-to-all-done
  49.8 1.1 broadcast_in_dim.17
  50.8 0.0 copy-done.4
  50.8 0.0 copy-done.5
  50.9 4.0 %all-to-all-start.1 = ((bf16[4,192,768]{2,1,0:T(8,128)(2,1)}), bf16[4,192,768]{2,1,0:T(8,128)(2,1)S(1)}, u32[]{:S(2)}, u32[]{:S(2)}) async-start(bf16[4,192,768]{2,1,0:T(8,128)(2,1)} %broadcast_in_dim.17), calls=%async_computation.1 | async-start | bytes 2359296 | tf_op jit(solution)/shard_map/all_to_all | solution.py:18
  54.9 4.4 %collective-permute-start.2 = (bf16[256,768]{1,0:T(8,128)(2,1)}, bf16[256,768]{1,0:T(8,128)(2,1)}, u32[]{:S(2)}, u32[]{:S(2)}) collective-permute-start(bf16[256,768]{1,0:T(8,128)(2,1)} %copy-done.4), channel_id=1, source_target_pairs={{0,256},{128,384},{256,0},{384,128},{1,257},{129,385},{257,1},{385... | collective-permute-start | bytes 1179656 | tf_op jit(solution)/shard_map/ppermute | solution.py:12
  59.3 1.0 constant_dynamic-update-slice_fusion.2
  60.4 16.3 %collective-permute-done.2 = bf16[256,768]{1,0:T(8,128)(2,1)} collective-permute-done((bf16[256,768]{1,0:T(8,128)(2,1)}, bf16[256,768]{1,0:T(8,128)(2,1)}, u32[]{:S(2)}, u32[]{:S(2)}) %collective-permute-start.2) | collective-permute-done | bytes 393248 | tf_op jit(solution)/shard_map/ppermute | solution.py:12
  76.6 1.0 constant_dynamic-update-slice_fusion.1
  77.7 0.0 copy-start.1
  77.7 0.0 all-to-all-done.1
  77.7 1.1 copy-done.1
  78.9 0.0 copy-start.3
  78.9 1.0 copy-done.3
  79.9 5.2 %multiply_reduce_fusion.1 = (f32[1024]{0:T(1024)S(1)}, f32[1024,768]{0,1:T(8,128)S(1)}) fusion(bf16[1024,768]{1,0:T(8,128)(2,1)} %copy-done.1, bf16[768,768]{1,0:T(8,128)(2,1)} %bitcast.17, s32[768]{0:T(1024)S(1)} %fusion.27), kind=kOutput, calls=%fused_computation.12 | convolution fusion | flops 2116680704 | bytes 5905408 | tf_op jit(solution)/shard_map/dot_general | solution.py:53
  85.1 1.6 %fusion.41 = bf16[1024,768]{0,1:T(8,128)(2,1)} fusion(f32[1024,768]{0,1:T(8,128)S(1)} %get-tuple-element.12, f32[1024]{0:T(1024)S(1)} %add_sqrt_fusion), kind=kLoop, calls=%fused_computation.97 | loop fusion | flops 1572864 | bytes 4722688 | tf_op jit(solution)/shard_map/convert_element_type | solution.py:56
  86.7 3.3 %collective-permute-start.5 = (bf16[1024,768]{0,1:T(8,128)(2,1)}, bf16[1024,768]{0,1:T(8,128)(2,1)}, u32[]{:S(2)}, u32[]{:S(2)}) collective-permute-start(bf16[1024,768]{0,1:T(8,128)(2,1)} %fusion.41), channel_id=1, source_target_pairs={{0,64},{64,0},{1,65},{65,1},{2,66},{66,2},{3,67},{67,3},{4,68},{68... | collective-permute-start | bytes 4718600 | tf_op jit(solution)/shard_map/ppermute | solution.py:57
  91.4 2.0 %collective-permute-done.5 = bf16[1024,768]{0,1:T(8,128)(2,1)} collective-permute-done((bf16[1024,768]{0,1:T(8,128)(2,1)}, bf16[1024,768]{0,1:T(8,128)(2,1)}, u32[]{:S(2)}, u32[]{:S(2)}) %collective-permute-start.5) | collective-permute-done | bytes 1572896 | tf_op jit(solution)/shard_map/ppermute | solution.py:57
  93.4 8.1 %multiply_reduce_fusion = (f32[1024]{0:T(1024)S(1)}, f32[1024,768]{0,1:T(8,128)}) fusion(f32[1024,768]{0,1:T(8,128)S(1)} %get-tuple-element.12, f32[1024]{0:T(1024)S(1)} %add_sqrt_fusion, bf16[1024,768]{0,1:T(8,128)(2,1)} %collective-permute-done.5, f32[]{:T(128)} %bitcast.16, f32[]{:T(128)} %bitcast.15, s32[1024]{0:T(1024)S(1)} %fusion.21, f32[]{:T(128)S(6)} %neg.9), kind=kOutput, calls=%fused_computation.11 | convolution fusion | flops 3237739520 | bytes 7876620 | tf_op jit(solution)/shard_map/dot_general | solution.py:67
  101.5 0.0 copy-start.2
  101.5 2.8 %subtract_divide_fusion = f32[1024,768]{0,1:T(8,128)S(1)} fusion(f32[1024,768]{0,1:T(8,128)} %get-tuple-element.14, f32[1024]{0:T(1024)S(1)} %get-tuple-element.13, f32[1024]{0:T(1024)S(1)} %add_sqrt_fusion, f32[1024,768]{0,1:T(8,128)S(1)} %get-tuple-element.12), kind=kLoop, calls=%fused_computation.10 | loop fusion | flops 3145728 | bytes 9445376 | tf_op jit(solution)/shard_map/div | solution.py:68
  104.2 0.0 copy-start
  104.3 1.6 %copy-done = f32[1024,768]{0,1:T(8,128)} copy-done((f32[1024,768]{0,1:T(8,128)}, f32[1024,768]{0,1:T(8,128)S(1)}, u32[]{:S(2)}) %copy-start) | copy-done | bytes 3145752
  105.9 0.0 copy-done.2
  105.9 0.5 convolution_convert_fusion
  106.4 0.2 copy.11
  106.6 0.9 reshape.147
  107.5 15.0 %all-to-all-start.2 = ((bf16[64,12,192]{2,1,0:T(8,128)(2,1)}), bf16[64,12,192]{2,1,0:T(8,128)(2,1)S(1)}, u32[]{:S(2)}, u32[]{:S(2)}) async-start(bf16[64,12,192]{2,1,0:T(8,128)(2,1)} %reshape.147), calls=%async_computation.2 | async-start | bytes 1048576 | tf_op jit(solution)/shard_map/all_to_all | solution.py:77
  122.5 0.2 multiply_reduce_fusion.2
  122.7 1.3 fusion.11
  124.0 2.6 %collective-permute-start.6 = (f32[128]{0:T(128)S(1)}, f32[128]{0:T(128)S(1)}, u32[]{:S(2)}, u32[]{:S(2)}) collective-permute-start(f32[128]{0:T(128)S(1)} %slice.29), channel_id=1, source_target_pairs={{0,64},{64,0},{1,65},{65,1},{2,66},{66,2},{3,67},{67,3},{4,68},{68... | collective-permute-start | bytes 1544 | tf_op jit(solution)/shard_map/ppermute | solution.py:93
  126.5 14.2 %all-to-all-done.2 = bf16[64,12,192]{2,1,0:T(8,128)(2,1)S(1)} async-done(((bf16[64,12,192]{2,1,0:T(8,128)(2,1)}), bf16[64,12,192]{2,1,0:T(8,128)(2,1)S(1)}, u32[]{:S(2)}, u32[]{:S(2)}) %all-to-all-start.2) | async-done | bytes 294944 | tf_op jit(solution)/shard_map/all_to_all | solution.py:77
  140.8 0.1 convert_reduce_fusion
  140.9 0.7 broadcast_in_dim.18
  141.6 8.5 %all-to-all-start.3 = ((f32[8,12,192]{2,1,0:T(8,128)}), f32[8,12,192]{2,1,0:T(8,128)S(1)}, u32[]{:S(2)}, u32[]{:S(2)}) async-start(f32[8,12,192]{2,1,0:T(8,128)} %broadcast_in_dim.18), calls=%async_computation.3 | async-start | bytes 262144 | tf_op jit(solution)/shard_map/all_to_all | solution.py:18
  150.1 0.0 collective-permute-done.6
  150.1 0.5 broadcast_select_fusion.3
  150.6 5.3 %all-to-all-done.3 = f32[8,12,192]{2,1,0:T(8,128)S(1)} async-done(((f32[8,12,192]{2,1,0:T(8,128)}), f32[8,12,192]{2,1,0:T(8,128)S(1)}, u32[]{:S(2)}, u32[]{:S(2)}) %all-to-all-start.3) | async-done | bytes 73760 | tf_op jit(solution)/shard_map/all_to_all | solution.py:18
  155.9 0.1 copy.15
  156.0 0.3 slice_reduce_fusion
  156.3 0.7 squeeze.17
  157.0 0.7 squeeze.16
  (10 shorter events, 0.2 us)
Async XLA Ops:
  1.7 23.9 %collective-permute-start = (bf16[128,768]{1,0:T(8,128)(2,1)S(1)}, bf16[128,768]{1,0:T(8,128)(2,1)S(1)}, u32[]{:S(2)}, u32[]{:S(2)}) collective-permute-start(bf16[128,768]{1,0:T(8,128)(2,1)S(1)} %get-tuple-element.8), channel_id=1, source_target_pairs={{0,64},{64,0},{1,65},{65,1},{2,66},{66,2},{3,67},{67,3},{4,68},{68... | collective-permute-start | bytes 589832 | tf_op jit(solution)/shard_map/ppermute | solution.py:37
  11.3 8.5 %collective-permute-start.4 = (bf16[12,768]{1,0:T(8,128)(2,1)S(1)}, bf16[12,768]{1,0:T(8,128)(2,1)S(1)}, u32[]{:S(2)}, u32[]{:S(2)}) collective-permute-start(bf16[12,768]{1,0:T(8,128)(2,1)S(1)} %broadcast_select_fusion.2), channel_id=1, source_target_pairs={{0,4},{4,0},{1,5},{5,1},{2,6},{6,2},{3,7},{7,3},{8,12},{12,8},{9,1... | collective-permute-start | bytes 55304 | tf_op jit(solution)/shard_map/ppermute | solution.py:41
  20.5 29.2 %all-to-all-start = ((bf16[8,24,768]{2,1,0:T(8,128)(2,1)}), bf16[8,24,768]{2,1,0:T(8,128)(2,1)S(1)}, u32[]{:S(2)}, u32[]{:S(2)}) async-start(bf16[8,24,768]{2,1,0:T(8,128)(2,1)} %broadcast_in_dim.14), calls=%async_computation | async-start | bytes 589824 | tf_op jit(solution)/shard_map/all_to_all | solution.py:18
  25.7 25.1 %copy-start.4 = (bf16[256,768]{1,0:T(8,128)(2,1)}, bf16[256,768]{1,0:T(8,128)(2,1)S(1)}, u32[]{:S(2)}) copy-start(bf16[256,768]{1,0:T(8,128)(2,1)S(1)} %pad_maximum_fusion) | copy-start | bytes 1179652
  25.7 12.5 %collective-permute-start.3 = (bf16[256,768]{1,0:T(8,128)(2,1)S(1)}, bf16[256,768]{1,0:T(8,128)(2,1)S(1)}, u32[]{:S(2)}, u32[]{:S(2)}) collective-permute-start(bf16[256,768]{1,0:T(8,128)(2,1)S(1)} %pad_maximum_fusion), channel_id=1, source_target_pairs={{0,384},{128,0},{256,128},{384,256},{1,385},{129,1},{257,129},{385... | collective-permute-start | bytes 1179656 | tf_op jit(solution)/shard_map/ppermute | solution.py:12
  30.7 17.8 %collective-permute-start.1 = (bf16[256,768]{1,0:T(8,128)(2,1)S(1)}, bf16[256,768]{1,0:T(8,128)(2,1)S(1)}, u32[]{:S(2)}, u32[]{:S(2)}) collective-permute-start(bf16[256,768]{1,0:T(8,128)(2,1)S(1)} %pad_maximum_fusion), channel_id=1, source_target_pairs={{0,128},{128,256},{256,384},{384,0},{1,129},{129,257},{257,385},{3... | collective-permute-start | bytes 1179656 | tf_op jit(solution)/shard_map/ppermute | solution.py:12
  48.5 2.4 %copy-start.5 = (bf16[256,768]{1,0:T(8,128)(2,1)}, bf16[256,768]{1,0:T(8,128)(2,1)S(1)}, u32[]{:S(2)}) copy-start(bf16[256,768]{1,0:T(8,128)(2,1)S(1)} %collective-permute-done.1) | copy-start | bytes 1179652
  50.9 26.9 %all-to-all-start.1 = ((bf16[4,192,768]{2,1,0:T(8,128)(2,1)}), bf16[4,192,768]{2,1,0:T(8,128)(2,1)S(1)}, u32[]{:S(2)}, u32[]{:S(2)}) async-start(bf16[4,192,768]{2,1,0:T(8,128)(2,1)} %broadcast_in_dim.17), calls=%async_computation.1 | async-start | bytes 2359296 | tf_op jit(solution)/shard_map/all_to_all | solution.py:18
  54.9 21.8 %collective-permute-start.2 = (bf16[256,768]{1,0:T(8,128)(2,1)}, bf16[256,768]{1,0:T(8,128)(2,1)}, u32[]{:S(2)}, u32[]{:S(2)}) collective-permute-start(bf16[256,768]{1,0:T(8,128)(2,1)} %copy-done.4), channel_id=1, source_target_pairs={{0,256},{128,384},{256,0},{384,128},{1,257},{129,385},{257,1},{385... | collective-permute-start | bytes 1179656 | tf_op jit(solution)/shard_map/ppermute | solution.py:12
  77.7 1.2 copy-start.1
  78.9 1.0 copy-start.3
  86.7 6.7 %collective-permute-start.5 = (bf16[1024,768]{0,1:T(8,128)(2,1)}, bf16[1024,768]{0,1:T(8,128)(2,1)}, u32[]{:S(2)}, u32[]{:S(2)}) collective-permute-start(bf16[1024,768]{0,1:T(8,128)(2,1)} %fusion.41), channel_id=1, source_target_pairs={{0,64},{64,0},{1,65},{65,1},{2,66},{66,2},{3,67},{67,3},{4,68},{68... | collective-permute-start | bytes 4718600 | tf_op jit(solution)/shard_map/ppermute | solution.py:57
  101.5 4.4 %copy-start.2 = (bf16[1024,768]{1,0:T(8,128)(2,1)S(1)}, bf16[1024,768]{1,0:T(8,128)(2,1)}, u32[]{:S(2)}) copy-start(bf16[1024,768]{1,0:T(8,128)(2,1)} %copy-done.1) | copy-start | bytes 4718596
  104.2 1.7 %copy-start = (f32[1024,768]{0,1:T(8,128)}, f32[1024,768]{0,1:T(8,128)S(1)}, u32[]{:S(2)}) copy-start(f32[1024,768]{0,1:T(8,128)S(1)} %subtract_divide_fusion) | copy-start | bytes 9437188
  107.5 33.3 %all-to-all-start.2 = ((bf16[64,12,192]{2,1,0:T(8,128)(2,1)}), bf16[64,12,192]{2,1,0:T(8,128)(2,1)S(1)}, u32[]{:S(2)}, u32[]{:S(2)}) async-start(bf16[64,12,192]{2,1,0:T(8,128)(2,1)} %reshape.147), calls=%async_computation.2 | async-start | bytes 1048576 | tf_op jit(solution)/shard_map/all_to_all | solution.py:77
  124.0 26.1 %collective-permute-start.6 = (f32[128]{0:T(128)S(1)}, f32[128]{0:T(128)S(1)}, u32[]{:S(2)}, u32[]{:S(2)}) collective-permute-start(f32[128]{0:T(128)S(1)} %slice.29), channel_id=1, source_target_pairs={{0,64},{64,0},{1,65},{65,1},{2,66},{66,2},{3,67},{67,3},{4,68},{68... | collective-permute-start | bytes 1544 | tf_op jit(solution)/shard_map/ppermute | solution.py:93
  141.6 14.3 %all-to-all-start.3 = ((f32[8,12,192]{2,1,0:T(8,128)}), f32[8,12,192]{2,1,0:T(8,128)S(1)}, u32[]{:S(2)}, u32[]{:S(2)}) async-start(f32[8,12,192]{2,1,0:T(8,128)} %broadcast_in_dim.18), calls=%async_computation.3 | async-start | bytes 262144 | tf_op jit(solution)/shard_map/all_to_all | solution.py:18

commit v2 on v1

v2 whole, which is shorter than its diff:
```python
import functools

import jax
import jax.numpy as jnp
from jax import lax
from jax.experimental import pallas as pl
from jax.experimental.pallas import tpu as pltpu
from jax.sharding import Mesh, PartitionSpec as P

EVERY = ("zlo", "core", "y", "zhi", "x")
GRP = ("y", "zhi", "x")
SWAP = [(0, 1), (1, 0)]
F32, BF16 = jnp.float32, jnp.bfloat16
VMEM = pl.BlockSpec(memory_space=pltpu.VMEM)
ANY = pl.BlockSpec(memory_space=pl.ANY)
SMEM = pl.BlockSpec(memory_space=pltpu.SMEM)
PARAMS = pltpu.CompilerParams(vmem_limit_bytes=40 * 1024 * 1024)


def passed_on(value, axis, by):
    count = lax.axis_size(axis)
    return lax.ppermute(value, axis, [(i, i + by) for i in range(count) if 0 <= i + by < count])


def spread(value, axis):
    count = lax.axis_size(axis)
    copies = jnp.broadcast_to(value[None], (count,) + value.shape)
    return lax.all_to_all(copies, axis, split_axis=0, concat_axis=0)


def copies_kernel(own_ref, other_ref, up_ref, down_ref, out_ref):
    share = own_ref.shape[0]
    for k in range(out_ref.shape[0]):
        out_ref[k, :share] = own_ref[...]
        out_ref[k, share:] = other_ref[...]


def spread_kernel(near_ref, up_ref, down_ref, out_ref):
    for k in range(out_ref.shape[0]):
        out_ref[k] = near_ref[...]


def embed_kernel(
    place, order_ref, gathered_ref, x0, up1, up2, up3, down1, down2, down3,
    half_ref, unit_ref, radius_ref, rows_ref, mapping,
):
    mapping[...] = jnp.dot(
        order_ref[...], gathered_ref[...], preferred_element_type=F32
    ).astype(BF16)
    blocks = ((x0, None), (up1, down3), (up2, down2), (up3, down1))
    for k, (low, high) in enumerate(blocks):
        rows = low.shape[0]
        at = pl.ds(k * rows, rows)
        block = low[...] if high is None else jnp.where(place[0] >= k, low[...], high[...])
        rows_ref[at, :] = block
        out = jnp.dot(block, mapping[...], preferred_element_type=F32)
        radius = jnp.sqrt(jnp.sum(out * out, axis=-1, keepdims=True) + 1e-06)
        unit = out / radius
        radius_ref[at, :] = radius
        unit_ref[at, :] = unit
        half_ref[at, :] = unit.astype(BF16)


def grad_kernel(
    own, scalars, place, half_ref, partner_ref, unit_ref, radius_ref, rows_ref,
    local_ref, norms_ref, pre_ref,
):
    multiplier, offset = scalars[0], scalars[1]
    columns = local_ref.shape[1]
    start = pl.multiple_of((3 * place[0]) // 2 * 128, 128)
    total = None
    rows = 2 * own
    for k in range(rows_ref.shape[0] // rows):
        at = pl.ds(k * rows, rows)
        logits = multiplier * lax.dot_general(
            half_ref[at, :], partner_ref[...], (((1,), (1,)), ((), ())), preferred_element_type=F32
        ) + offset
        i = lax.broadcasted_iota(jnp.int32, logits.shape, 0) + k * rows
        j = lax.broadcasted_iota(jnp.int32, logits.shape, 1)
        sign = jnp.where(j == jnp.where(i % rows < own, i + own, i - own), 1.0, -1.0)
        weights = (-multiplier * sign) * jax.nn.sigmoid(-sign * logits)
        grad = jnp.dot(weights.astype(BF16), partner_ref[...], preferred_element_type=F32)
        unit = unit_ref[at, :]
        pre = (grad - unit * jnp.sum(unit * grad, axis=-1, keepdims=True)) / radius_ref[at, :]
        pre_ref[...] = pre
        if k == 0:
            wide = rows_ref[at, :].astype(F32)
            norms_ref[...] = jnp.sqrt(jnp.sum(wide * wide, axis=-1, keepdims=True)) * jnp.sqrt(
                jnp.sum(pre * pre, axis=-1, keepdims=True)
            )
        part = lax.dot_general(
            rows_ref[at, :],
            pre_ref[:, pl.ds(start, 256)].astype(BF16),
            (((0,), (0,)), ((), ())),
            preferred_element_type=F32,
        )
        total = part if total is None else total + part
    odd = place[0] % 2 == 1
    local_ref[...] = jnp.where(odd, total[:, 256 - columns :], total[:, :columns]).astype(BF16)


def on_device(
    picture_inputs,
    caption_inputs,
    picture_mapping,
    caption_mapping,
    similarity_multiplier,
    score_constant,
):
    own, width = picture_inputs.shape
    share, embed = picture_mapping.shape
    first = lax.axis_index("core") == 0
    chips = lax.axis_size("zlo")
    n_y, n_zhi, n_x = (lax.axis_size(a) for a in GRP)
    piece = jnp.where(first, picture_mapping, caption_mapping)
    other = lax.ppermute(piece, "zhi", SWAP)
    mine = jnp.where(first, picture_inputs, caption_inputs)
    sent = jnp.where(first, caption_inputs, picture_inputs)
    chunk = jnp.concatenate([mine, lax.ppermute(sent, "core", SWAP)], axis=0)
    up, down = [chunk], [chunk]
    for _ in range(1, chips):
        up.append(passed_on(up[-1], "zlo", 1))
        down.append(passed_on(down[-1], "zlo", -1))
    at_chip = lax.axis_index("zlo").astype(jnp.int32).reshape(1)
    copies = pl.pallas_call(
        copies_kernel,
        out_shape=jax.ShapeDtypeStruct((n_y, n_zhi * share, embed), BF16),
        in_specs=[VMEM, VMEM, ANY, ANY],
        out_specs=VMEM,
        cost_estimate=pl.CostEstimate(flops=0, bytes_accessed=2**19, transcendentals=0),
    )(piece, other, up[1], down[1])
    near = lax.all_to_all(copies, "y", split_axis=0, concat_axis=0)
    near = near.reshape(n_y * n_zhi * share, embed)
    copies = pl.pallas_call(
        spread_kernel,
        out_shape=jax.ShapeDtypeStruct((n_x,) + near.shape, BF16),
        in_specs=[VMEM, ANY, ANY],
        out_specs=VMEM,
        cost_estimate=pl.CostEstimate(flops=0, bytes_accessed=2**21, transcendentals=0),
    )(near, up[2], down[2])
    gathered = lax.all_to_all(copies, "x", split_axis=0, concat_axis=0).reshape(width, embed)
    at = jnp.arange(width, dtype=jnp.int32)
    owner, row = at // share, at % share
    at_half = (owner // n_x) % n_zhi
    at_half = jnp.where(lax.axis_index("zhi") == 0, at_half, 1 - at_half)
    from_row = (((owner % n_x) * n_y + owner // (n_x * n_zhi)) * n_zhi + at_half) * share + row
    order = (from_row[:, None] == at[None, :]).astype(BF16)
    rows = chips * chunk.shape[0]
    half, unit, radius, set_rows = pl.pallas_call(
        embed_kernel,
        out_shape=(
            jax.ShapeDtypeStruct((rows, embed), BF16),
            jax.ShapeDtypeStruct((rows, embed), F32),
            jax.ShapeDtypeStruct((rows, 1), F32),
            jax.ShapeDtypeStruct((rows, width), BF16),
        ),
        in_specs=[SMEM] + [VMEM] * 9,
        out_specs=(VMEM,) * 4,
        scratch_shapes=[pltpu.VMEM((width, embed), BF16)],
        compiler_params=PARAMS,
        cost_estimate=pl.CostEstimate(
            flops=2 * (rows + width) * width * embed, bytes_accessed=8 * 2**20, transcendentals=0
        ),
    )(at_chip, order, gathered, *up, *down[1:])
    partner = lax.ppermute(half, "core", SWAP)
    columns = embed // chips
    local, norms = pl.pallas_call(
        functools.partial(grad_kernel, own),
        out_shape=(
            jax.ShapeDtypeStruct((width, columns), BF16),
            jax.ShapeDtypeStruct((2 * own, 1), F32),
        ),
        in_specs=[SMEM] * 2 + [VMEM] * 5,
        out_specs=(VMEM,) * 2,
        scratch_shapes=[pltpu.VMEM((2 * own, embed), F32)],
        compiler_params=PARAMS,
        cost_estimate=pl.CostEstimate(
            flops=4 * rows * rows * embed, bytes_accessed=8 * 2**20, transcendentals=rows * rows
        ),
    )(
        jnp.concatenate([similarity_multiplier, score_constant]),
        at_chip,
        half,
        partner,
        unit,
        radius,
        set_rows,
    )
    pieces = lax.all_to_all(
        local.reshape(width // share, share, columns), GRP, split_axis=0, concat_axis=0, tiled=True
    )
    total = jnp.sum(pieces.astype(F32), axis=0)
    whole = spread(total, ("zlo", "core")).reshape(chips, 2, share, columns)
    whole = whole.transpose(1, 2, 0, 3).reshape(2, share, embed)
    norms = norms.reshape(2 * own)
    own_norms = norms[:own]
    their_norms = lax.ppermute(norms[own:], "core", SWAP)
    img_norms = jnp.where(first, own_norms, their_norms)
    txt_norms = jnp.where(first, their_norms, own_norms)
    return (whole[0], whole[1], img_norms, txt_norms)


def build(fine):
    in_specs = (P(EVERY, None), P(EVERY, None), P(GRP, None), P(GRP, None), P(), P())
    out_specs = (P(GRP, None), P(GRP, None), P(EVERY), P(EVERY))
    return jax.shard_map(
        on_device, mesh=fine, in_specs=in_specs, out_specs=out_specs, check_vma=False
    )


def solution(mesh):
    return build(Mesh(mesh.devices.reshape(4, 2, 8, 2, 4), EVERY))
```

time: 159 us -> 138 us (0.87)
  matrix products: 13.8 us -> 0 us
  Pallas kernels: 0 us -> 13.4 us
  waiting for transfers between devices: 55.8 us -> 46.2 us
  local copies, waits for them, and re-layouts: 12.3 us -> 5.76 us
  other arithmetic: 8.39 us -> 2.1 us
  starting transfers between devices: 64 us -> 68 us
    dot_general x3 -> x0, matrix products: 13.8 us -> none  [the longest x1 8.07 us: on_device(): grad = jnp.dot(weights, partner, preferred_element_type=jnp.float32)]
    pallas_call x0 -> x4, Pallas kernels: none -> 13.4 us  [the longest x1 5.88 us: on_device(): pl.pallas_call(functools.partial(grad_kernel, own), out_shape=(jax.ShapeD...]
    ppermute x4 -> x7, waiting for transfers between devices: 34.2 us -> 22.6 us  [the longest x6 16.8 us: passed_on(): lax.ppermute(value, axis, [(i, i + by) for i in range(count) if 0 <= i +...]
    all_to_all x3 -> x1, starting transfers between devices: 17.7 us -> 6.99 us  [spread(): return lax.all_to_all(copies, axis, split_axis=0, concat_axis=0)]
    all_to_all x1 -> x3, starting transfers between devices: 15 us -> 21.5 us  [the longest x1 10.6 us: on_device(): lax.all_to_all(local.reshape(width // share, share, columns), GRP, split_...]
    ppermute x4 -> x7, starting transfers between devices: 16.5 us -> 21.6 us  [the longest x6 14.5 us: passed_on(): lax.ppermute(value, axis, [(i, i + by) for i in range(count) if 0 <= i +...]
    unnamed x15 -> x18, local copies, waits for them, and re-layouts: 5.87 us -> 2.26 us
    ppermute x1, starting transfers between devices: 3.35 us -> 6.48 us  [on_device(): partner = lax.ppermute(half, 'core', SWAP)]
  transfers between devices with their start and end apart: 11 -> 14, of which waited for: 7 -> 9; matrix products, arithmetic and copies ran while one was open for 5% -> 1% of each run, Pallas kernels for 0% -> 0%
where the time goes in v2:
time: 138 us; the launch traced here: 137 us
  starting transfers between devices  68 us (49%)
  waiting for transfers between devices  46.2 us (33%)
  Pallas kernels  13.4 us (10%)
  local copies, waits for them, and re-layouts  5.76 us (4%)
  between operations  2.13 us (2%)
  other arithmetic  2.1 us (2%)
    ppermute x6, waiting for transfers between devices, passed_on(): lax.ppermute(value, axis, [(i, i + by) for i in range(count) if 0 <= i +...  16.8 us
    all_to_all x1, waiting for transfers between devices, on_device(): lax.all_to_all(local.reshape(width // share, share, columns), GRP, split_...  15.6 us
    ppermute x6, starting transfers between devices, passed_on(): lax.ppermute(value, axis, [(i, i + by) for i in range(count) if 0 <= i +...  14.5 us
    all_to_all x1, starting transfers between devices, on_device(): lax.all_to_all(local.reshape(width // share, share, columns), GRP, split_...  10.6 us
    ppermute x1, starting transfers between devices, on_device(): chunk = jnp.concatenate([mine, lax.ppermute(sent, 'core', SWAP)], axis=0)  8.79 us
    ppermute x1, starting transfers between devices, on_device(): other = lax.ppermute(piece, 'zhi', SWAP)  7.07 us
    all_to_all x1, starting transfers between devices, spread(): return lax.all_to_all(copies, axis, split_axis=0, concat_axis=0)  6.99 us
    all_to_all x1, starting transfers between devices, on_device(): near = lax.all_to_all(copies, 'y', split_axis=0, concat_axis=0)  6.82 us
  transfers between devices with their start and end apart: 14, of which 9 were waited for; matrix products, arithmetic and copies ran while one was open for 1% of the time, Pallas kernels for 0%

profile of v2, /device:TPU:1, one launch (start us, length us, event | category | flops | bytes accessed | tf_op | source)
XLA Modules:
  0.0 137.5 jit_solution(8677454983622226817)
XLA Ops:
  0.6 0.0 copy-start.6
  0.6 0.0 copy-start.7
  0.7 1.1 broadcast_select_fusion.1
  1.7 8.8 %collective-permute-start.1 = (bf16[128,768]{1,0:T(8,128)(2,1)S(1)}, bf16[128,768]{1,0:T(8,128)(2,1)S(1)}, u32[]{:S(2)}, u32[]{:S(2)}) collective-permute-start(bf16[128,768]{1,0:T(8,128)(2,1)S(1)} %get-tuple-element.21), channel_id=1, source_target_pairs={{0,64},{64,0},{1,65},{65,1},{2,66},{66,2},{3,67},{67,3},{4,68},{68... | collective-permute-start | bytes 589832 | tf_op jit(solution)/shard_map/ppermute | solution.py:119
  10.5 1.0 collective-permute-done.1
  11.6 1.3 collective-permute-start.2
  12.9 1.3 collective-permute-start.3
  14.2 0.0 copy-done.6
  14.2 0.0 copy-done.7
  14.2 0.0 copy-start.5
  14.3 7.1 %collective-permute-start = (bf16[12,768]{1,0:T(8,128)(2,1)S(1)}, bf16[12,768]{1,0:T(8,128)(2,1)S(1)}, u32[]{:S(2)}, u32[]{:S(2)}) collective-permute-start(bf16[12,768]{1,0:T(8,128)(2,1)S(1)} %broadcast_select_fusion.2.own_ref), channel_id=1, source_target_pairs={{0,4},{4,0},{1,5},{5,1},{2,6},{6,2},{3,7},{7,3},{8,12},{12,8},{9,1... | collective-permute-start | bytes 55304 | tf_op jit(solution)/shard_map/ppermute | solution.py:116
  21.3 5.8 %collective-permute-done.other_ref = bf16[12,768]{1,0:T(8,128)(2,1)S(1)} collective-permute-done((bf16[12,768]{1,0:T(8,128)(2,1)S(1)}, bf16[12,768]{1,0:T(8,128)(2,1)S(1)}, u32[]{:S(2)}, u32[]{:S(2)}) %collective-permute-start) | collective-permute-done | bytes 18464 | tf_op jit(solution)/shard_map/ppermute | solution.py:116
  27.1 0.0 copy-start.8
  27.1 0.0 collective-permute-done.2.up_ref.up1
  27.1 0.0 copy-start
  27.1 0.0 collective-permute-done.3.down_ref.down1
  27.1 0.0 copy-done.5
  27.2 0.6 copy-done.8
  27.7 0.1 copy-done
  27.9 0.0 copy-start.2
  27.9 0.8 copy-done.2
  28.7 1.5 %shard_map.93 = bf16[8,24,768]{2,1,0:T(8,128)(2,1)} custom-call(bf16[12,768]{1,0:T(8,128)(2,1)} %copy-done.5, bf16[12,768]{1,0:T(8,128)(2,1)} %copy-done.8, bf16[256,768]{1,0:T(8,128)(2,1)} %copy-done, bf16[256,768]{1,0:T(8,128)(2,1)} %copy-done.2), custom_call_target="tpu_custom_call" | custom-call | bytes 524288 | tf_op jit(solution)/shard_map/pallas_call | solution.py:125
  30.1 6.8 %all-to-all-start = ((bf16[8,24,768]{2,1,0:T(8,128)(2,1)}), bf16[8,24,768]{2,1,0:T(8,128)(2,1)S(1)}, u32[]{:S(2)}, u32[]{:S(2)}) async-start(bf16[8,24,768]{2,1,0:T(8,128)(2,1)} %shard_map.93), calls=%async_computation | async-start | bytes 589824 | tf_op jit(solution)/shard_map/all_to_all | solution.py:132
  37.0 5.7 %collective-permute-start.4 = (bf16[256,768]{1,0:T(8,128)(2,1)}, bf16[256,768]{1,0:T(8,128)(2,1)}, u32[]{:S(2)}, u32[]{:S(2)}) collective-permute-start(bf16[256,768]{1,0:T(8,128)(2,1)} %copy-done), channel_id=1, source_target_pairs={{0,128},{128,256},{256,384},{1,129},{129,257},{257,385},{2,130},{1... | collective-permute-start | bytes 1179656 | tf_op jit(solution)/shard_map/ppermute | solution.py:22
  42.7 1.3 collective-permute-start.5
  44.0 4.6 %collective-permute-done.4.up_ref.up2 = bf16[256,768]{1,0:T(8,128)(2,1)} collective-permute-done((bf16[256,768]{1,0:T(8,128)(2,1)}, bf16[256,768]{1,0:T(8,128)(2,1)}, u32[]{:S(2)}, u32[]{:S(2)}) %collective-permute-start.4) | collective-permute-done | bytes 393248 | tf_op jit(solution)/shard_map/ppermute | solution.py:22
  48.6 4.6 %collective-permute-done.5.down_ref.down2 = bf16[256,768]{1,0:T(8,128)(2,1)} collective-permute-done((bf16[256,768]{1,0:T(8,128)(2,1)}, bf16[256,768]{1,0:T(8,128)(2,1)}, u32[]{:S(2)}, u32[]{:S(2)}) %collective-permute-start.5) | collective-permute-done | bytes 393248 | tf_op jit(solution)/shard_map/ppermute | solution.py:22
  53.1 0.0 all-to-all-done
  53.1 0.0 copy-start.4
  53.1 0.7 copy-done.4
  53.9 2.1 %shard_map.94 = bf16[4,192,768]{2,1,0:T(8,128)(2,1)} custom-call(bf16[192,768]{1,0:T(8,128)(2,1)} %bitcast.8, bf16[256,768]{1,0:T(8,128)(2,1)} %collective-permute-done.4.up_ref.up2, bf16[256,768]{1,0:T(8,128)(2,1)} %collective-permute-done.5.down_ref.down2), custom_call_target="tpu_custom_call" | custom-call | bytes 2097152 | tf_op jit(solution)/shard_map/pallas_call | solution.py:134
  56.0 0.0 copy-start.1
  56.0 0.0 copy-start.3
  56.0 4.1 %all-to-all-start.1 = ((bf16[4,192,768]{2,1,0:T(8,128)(2,1)}), bf16[4,192,768]{2,1,0:T(8,128)(2,1)S(1)}, u32[]{:S(2)}, u32[]{:S(2)}) async-start(bf16[4,192,768]{2,1,0:T(8,128)(2,1)} %shard_map.94), calls=%async_computation.1 | async-start | bytes 2359296 | tf_op jit(solution)/shard_map/all_to_all | solution.py:141
  60.1 3.6 %collective-permute-start.6 = (bf16[256,768]{1,0:T(8,128)(2,1)}, bf16[256,768]{1,0:T(8,128)(2,1)}, u32[]{:S(2)}, u32[]{:S(2)}) collective-permute-start(bf16[256,768]{1,0:T(8,128)(2,1)} %collective-permute-done.4.up_ref.up2), channel_id=1, source_target_pairs={{0,128},{128,256},{256,384},{1,129},{129,257},{257,385},{2,130},{1... | collective-permute-start | bytes 1179656 | tf_op jit(solution)/shard_map/ppermute | solution.py:22
  63.8 1.3 collective-permute-start.7
  65.1 0.3 fusion.order_ref
  65.4 3.1 %collective-permute-done.6.up3 = bf16[256,768]{1,0:T(8,128)(2,1)} collective-permute-done((bf16[256,768]{1,0:T(8,128)(2,1)}, bf16[256,768]{1,0:T(8,128)(2,1)}, u32[]{:S(2)}, u32[]{:S(2)}) %collective-permute-start.6) | collective-permute-done | bytes 393248 | tf_op jit(solution)/shard_map/ppermute | solution.py:22
  68.4 4.6 %collective-permute-done.7.down3 = bf16[256,768]{1,0:T(8,128)(2,1)} collective-permute-done((bf16[256,768]{1,0:T(8,128)(2,1)}, bf16[256,768]{1,0:T(8,128)(2,1)}, u32[]{:S(2)}, u32[]{:S(2)}) %collective-permute-start.7) | collective-permute-done | bytes 393248 | tf_op jit(solution)/shard_map/ppermute | solution.py:22
  73.0 0.0 all-to-all-done.1
  73.0 0.0 copy-done.1
  73.0 0.0 copy-done.3
  73.0 3.9 %shard_map.95 = (bf16[1024,768]{1,0:T(8,128)(2,1)S(1)}, f32[1024,768]{1,0:T(8,128)S(1)}, f32[1024,1]{1,0:T(8,128)S(1)}, bf16[1024,768]{1,0:T(8,128)(2,1)S(1)}) custom-call(s32[1]{0:T(128)} %bitcast.place, bf16[768,768]{1,0:T(8,128)(2,1)S(1)} %fusion.order_ref, bf16[768,768]{1,0:T(8,128)(2,1)S(1)} %bitcast.7, bf16[256,768]{1,0:T(8,128)(2,1)S(1)} %pad_maximum_fusion.x0, ...), custom_call_target="tpu_custom_call" | custom-call | flops 2113929216 | bytes 8388608 | tf_op jit(solution)/shard_map/pallas_call | solution.py:149
  76.9 6.5 %collective-permute-start.8 = (bf16[1024,768]{1,0:T(8,128)(2,1)S(1)}, bf16[1024,768]{1,0:T(8,128)(2,1)S(1)}, u32[]{:S(2)}, u32[]{:S(2)}) collective-permute-start(bf16[1024,768]{1,0:T(8,128)(2,1)S(1)} %get-tuple-element.10.half_ref), channel_id=1, source_target_pairs={{0,64},{64,0},{1,65},{65,1},{2,66},{66,2},{3,67},{67,3},{4,68},{68... | collective-permute-start | bytes 4718600 | tf_op jit(solution)/shard_map/ppermute | solution.py:165
  84.7 0.1 pad_maximum_fusion.1.scalars
  84.8 1.6 %collective-permute-done.8.partner_ref = bf16[1024,768]{1,0:T(8,128)(2,1)S(1)} collective-permute-done((bf16[1024,768]{1,0:T(8,128)(2,1)S(1)}, bf16[1024,768]{1,0:T(8,128)(2,1)S(1)}, u32[]{:S(2)}, u32[]{:S(2)}) %collective-permute-start.8) | collective-permute-done | bytes 1572896 | tf_op jit(solution)/shard_map/ppermute | solution.py:165
  86.4 5.9 %shard_map.96 = (bf16[768,192]{1,0:T(8,128)(2,1)S(1)}, f32[256,1]{1,0:T(8,128)S(1)}) custom-call(f32[2]{0:T(128)S(1)} %pad_maximum_fusion.1.scalars, s32[1]{0:T(128)} %bitcast.place, bf16[1024,768]{1,0:T(8,128)(2,1)S(1)} %get-tuple-element.10.half_ref, bf16[1024,768]{1,0:T(8,128)(2,1)S(1)} %collective-permute-done.8.partner_ref, ...), custom_call_target="tpu_custom_call" | custom-call | flops 3221225472 | bytes 8388608 | tf_op jit(solution)/shard_map/pallas_call | solution.py:167
  92.3 0.9 reshape.107
  93.2 10.6 %all-to-all-start.2 = ((bf16[64,12,192]{2,1,0:T(8,128)(2,1)}), bf16[64,12,192]{2,1,0:T(8,128)(2,1)S(1)}, u32[]{:S(2)}, u32[]{:S(2)}) async-start(bf16[64,12,192]{2,1,0:T(8,128)(2,1)} %reshape.107), calls=%async_computation.2 | async-start | bytes 1048576 | tf_op jit(solution)/shard_map/all_to_all | solution.py:189
  103.8 0.1 slice_reduce_fusion
  103.9 2.6 %collective-permute-start.9 = (f32[128]{0:T(128)S(1)}, f32[128]{0:T(128)S(1)}, u32[]{:S(2)}, u32[]{:S(2)}) collective-permute-start(f32[128]{0:T(128)S(1)} %get-tuple-element.16), channel_id=1, source_target_pairs={{0,64},{64,0},{1,65},{65,1},{2,66},{66,2},{3,67},{67,3},{4,68},{68... | collective-permute-start | bytes 1544 | tf_op jit(solution)/shard_map/ppermute | solution.py:197
  106.5 15.6 %all-to-all-done.2 = bf16[64,12,192]{2,1,0:T(8,128)(2,1)S(1)} async-done(((bf16[64,12,192]{2,1,0:T(8,128)(2,1)}), bf16[64,12,192]{2,1,0:T(8,128)(2,1)S(1)}, u32[]{:S(2)}, u32[]{:S(2)}) %all-to-all-start.2) | async-done | bytes 294944 | tf_op jit(solution)/shard_map/all_to_all | solution.py:189
  122.0 0.1 convert_reduce_fusion
  122.2 0.7 broadcast_in_dim.2
  122.8 7.0 %all-to-all-start.3 = ((f32[8,12,192]{2,1,0:T(8,128)}), f32[8,12,192]{2,1,0:T(8,128)S(1)}, u32[]{:S(2)}, u32[]{:S(2)}) async-start(f32[8,12,192]{2,1,0:T(8,128)} %broadcast_in_dim.2), calls=%async_computation.3 | async-start | bytes 262144 | tf_op jit(solution)/shard_map/all_to_all | solution.py:28
  129.8 0.0 collective-permute-done.9
  129.8 0.5 broadcast_select_fusion.3
  130.4 5.3 %all-to-all-done.3 = f32[8,12,192]{2,1,0:T(8,128)S(1)} async-done(((f32[8,12,192]{2,1,0:T(8,128)}), f32[8,12,192]{2,1,0:T(8,128)S(1)}, u32[]{:S(2)}, u32[]{:S(2)}) %all-to-all-start.3) | async-done | bytes 73760 | tf_op jit(solution)/shard_map/all_to_all | solution.py:28
  135.7 0.1 copy.13
  135.8 0.3 slice_reduce_fusion.2
  136.0 0.7 squeeze.6
  136.8 0.7 squeeze.7
  (3 shorter events, 0.1 us)
Async XLA Ops:
  0.6 13.6 %copy-start.6 = (bf16[12,768]{1,0:T(8,128)(2,1)S(1)}, bf16[12,768]{1,0:T(8,128)(2,1)}, u32[]{:S(2)}) copy-start(bf16[12,768]{1,0:T(8,128)(2,1)} %param.8) | copy-start | bytes 55300
  0.6 13.6 %copy-start.7 = (bf16[12,768]{1,0:T(8,128)(2,1)S(1)}, bf16[12,768]{1,0:T(8,128)(2,1)}, u32[]{:S(2)}) copy-start(bf16[12,768]{1,0:T(8,128)(2,1)} %param.9) | copy-start | bytes 55300
  1.7 9.8 %collective-permute-start.1 = (bf16[128,768]{1,0:T(8,128)(2,1)S(1)}, bf16[128,768]{1,0:T(8,128)(2,1)S(1)}, u32[]{:S(2)}, u32[]{:S(2)}) collective-permute-start(bf16[128,768]{1,0:T(8,128)(2,1)S(1)} %get-tuple-element.21), channel_id=1, source_target_pairs={{0,64},{64,0},{1,65},{65,1},{2,66},{66,2},{3,67},{67,3},{4,68},{68... | collective-permute-start | bytes 589832 | tf_op jit(solution)/shard_map/ppermute | solution.py:119
  11.6 15.6 %collective-permute-start.2 = (bf16[256,768]{1,0:T(8,128)(2,1)S(1)}, bf16[256,768]{1,0:T(8,128)(2,1)S(1)}, u32[]{:S(2)}, u32[]{:S(2)}) collective-permute-start(bf16[256,768]{1,0:T(8,128)(2,1)S(1)} %pad_maximum_fusion.x0), channel_id=1, source_target_pairs={{0,128},{128,256},{256,384},{1,129},{129,257},{257,385},{2,130},{1... | collective-permute-start | bytes 1179656 | tf_op jit(solution)/shard_map/ppermute | solution.py:22
  12.9 14.2 %collective-permute-start.3 = (bf16[256,768]{1,0:T(8,128)(2,1)S(1)}, bf16[256,768]{1,0:T(8,128)(2,1)S(1)}, u32[]{:S(2)}, u32[]{:S(2)}) collective-permute-start(bf16[256,768]{1,0:T(8,128)(2,1)S(1)} %pad_maximum_fusion.x0), channel_id=1, source_target_pairs={{128,0},{256,128},{384,256},{129,1},{257,129},{385,257},{130,2},{2... | collective-permute-start | bytes 1179656 | tf_op jit(solution)/shard_map/ppermute | solution.py:22
  14.2 12.9 %copy-start.5 = (bf16[12,768]{1,0:T(8,128)(2,1)}, bf16[12,768]{1,0:T(8,128)(2,1)S(1)}, u32[]{:S(2)}) copy-start(bf16[12,768]{1,0:T(8,128)(2,1)S(1)} %broadcast_select_fusion.2.own_ref) | copy-start | bytes 55300
  14.3 12.9 %collective-permute-start = (bf16[12,768]{1,0:T(8,128)(2,1)S(1)}, bf16[12,768]{1,0:T(8,128)(2,1)S(1)}, u32[]{:S(2)}, u32[]{:S(2)}) collective-permute-start(bf16[12,768]{1,0:T(8,128)(2,1)S(1)} %broadcast_select_fusion.2.own_ref), channel_id=1, source_target_pairs={{0,4},{4,0},{1,5},{5,1},{2,6},{6,2},{3,7},{7,3},{8,12},{12,8},{9,1... | collective-permute-start | bytes 55304 | tf_op jit(solution)/shard_map/ppermute | solution.py:116
  27.1 0.6 copy-start.8
  27.1 0.7 copy-start
  27.9 0.8 copy-start.2
  30.1 23.0 %all-to-all-start = ((bf16[8,24,768]{2,1,0:T(8,128)(2,1)}), bf16[8,24,768]{2,1,0:T(8,128)(2,1)S(1)}, u32[]{:S(2)}, u32[]{:S(2)}) async-start(bf16[8,24,768]{2,1,0:T(8,128)(2,1)} %shard_map.93), calls=%async_computation | async-start | bytes 589824 | tf_op jit(solution)/shard_map/all_to_all | solution.py:132
  37.0 11.6 %collective-permute-start.4 = (bf16[256,768]{1,0:T(8,128)(2,1)}, bf16[256,768]{1,0:T(8,128)(2,1)}, u32[]{:S(2)}, u32[]{:S(2)}) collective-permute-start(bf16[256,768]{1,0:T(8,128)(2,1)} %copy-done), channel_id=1, source_target_pairs={{0,128},{128,256},{256,384},{1,129},{129,257},{257,385},{2,130},{1... | collective-permute-start | bytes 1179656 | tf_op jit(solution)/shard_map/ppermute | solution.py:22
  42.7 10.4 %collective-permute-start.5 = (bf16[256,768]{1,0:T(8,128)(2,1)}, bf16[256,768]{1,0:T(8,128)(2,1)}, u32[]{:S(2)}, u32[]{:S(2)}) collective-permute-start(bf16[256,768]{1,0:T(8,128)(2,1)} %copy-done.2), channel_id=1, source_target_pairs={{128,0},{256,128},{384,256},{129,1},{257,129},{385,257},{130,2},{2... | collective-permute-start | bytes 1179656 | tf_op jit(solution)/shard_map/ppermute | solution.py:22
  53.1 0.7 copy-start.4
  56.0 17.0 %copy-start.1 = (bf16[256,768]{1,0:T(8,128)(2,1)S(1)}, bf16[256,768]{1,0:T(8,128)(2,1)}, u32[]{:S(2)}) copy-start(bf16[256,768]{1,0:T(8,128)(2,1)} %copy-done) | copy-start | bytes 1179652
  56.0 17.0 %copy-start.3 = (bf16[256,768]{1,0:T(8,128)(2,1)S(1)}, bf16[256,768]{1,0:T(8,128)(2,1)}, u32[]{:S(2)}) copy-start(bf16[256,768]{1,0:T(8,128)(2,1)} %copy-done.2) | copy-start | bytes 1179652
  56.0 17.0 %all-to-all-start.1 = ((bf16[4,192,768]{2,1,0:T(8,128)(2,1)}), bf16[4,192,768]{2,1,0:T(8,128)(2,1)S(1)}, u32[]{:S(2)}, u32[]{:S(2)}) async-start(bf16[4,192,768]{2,1,0:T(8,128)(2,1)} %shard_map.94), calls=%async_computation.1 | async-start | bytes 2359296 | tf_op jit(solution)/shard_map/all_to_all | solution.py:141
  60.1 8.3 %collective-permute-start.6 = (bf16[256,768]{1,0:T(8,128)(2,1)}, bf16[256,768]{1,0:T(8,128)(2,1)}, u32[]{:S(2)}, u32[]{:S(2)}) collective-permute-start(bf16[256,768]{1,0:T(8,128)(2,1)} %collective-permute-done.4.up_ref.up2), channel_id=1, source_target_pairs={{0,128},{128,256},{256,384},{1,129},{129,257},{257,385},{2,130},{1... | collective-permute-start | bytes 1179656 | tf_op jit(solution)/shard_map/ppermute | solution.py:22
  63.8 9.2 %collective-permute-start.7 = (bf16[256,768]{1,0:T(8,128)(2,1)}, bf16[256,768]{1,0:T(8,128)(2,1)}, u32[]{:S(2)}, u32[]{:S(2)}) collective-permute-start(bf16[256,768]{1,0:T(8,128)(2,1)} %collective-permute-done.5.down_ref.down2), channel_id=1, source_target_pairs={{128,0},{256,128},{384,256},{129,1},{257,129},{385,257},{130,2},{2... | collective-permute-start | bytes 1179656 | tf_op jit(solution)/shard_map/ppermute | solution.py:22
  76.9 9.5 %collective-permute-start.8 = (bf16[1024,768]{1,0:T(8,128)(2,1)S(1)}, bf16[1024,768]{1,0:T(8,128)(2,1)S(1)}, u32[]{:S(2)}, u32[]{:S(2)}) collective-permute-start(bf16[1024,768]{1,0:T(8,128)(2,1)S(1)} %get-tuple-element.10.half_ref), channel_id=1, source_target_pairs={{0,64},{64,0},{1,65},{65,1},{2,66},{66,2},{3,67},{67,3},{4,68},{68... | collective-permute-start | bytes 4718600 | tf_op jit(solution)/shard_map/ppermute | solution.py:165
  93.2 28.8 %all-to-all-start.2 = ((bf16[64,12,192]{2,1,0:T(8,128)(2,1)}), bf16[64,12,192]{2,1,0:T(8,128)(2,1)S(1)}, u32[]{:S(2)}, u32[]{:S(2)}) async-start(bf16[64,12,192]{2,1,0:T(8,128)(2,1)} %reshape.107), calls=%async_computation.2 | async-start | bytes 1048576 | tf_op jit(solution)/shard_map/all_to_all | solution.py:189
  103.9 25.9 %collective-permute-start.9 = (f32[128]{0:T(128)S(1)}, f32[128]{0:T(128)S(1)}, u32[]{:S(2)}, u32[]{:S(2)}) collective-permute-start(f32[128]{0:T(128)S(1)} %get-tuple-element.16), channel_id=1, source_target_pairs={{0,64},{64,0},{1,65},{65,1},{2,66},{66,2},{3,67},{67,3},{4,68},{68... | collective-permute-start | bytes 1544 | tf_op jit(solution)/shard_map/ppermute | solution.py:197
  122.8 12.8 %all-to-all-start.3 = ((f32[8,12,192]{2,1,0:T(8,128)}), f32[8,12,192]{2,1,0:T(8,128)S(1)}, u32[]{:S(2)}, u32[]{:S(2)}) async-start(f32[8,12,192]{2,1,0:T(8,128)} %broadcast_in_dim.2), calls=%async_computation.3 | async-start | bytes 262144 | tf_op jit(solution)/shard_map/all_to_all | solution.py:28

commit v3 on v2

--- a/solution.py
+++ b/solution.py
@@ -12,14 +12,8 @@
 SWAP = [(0, 1), (1, 0)]
 F32, BF16 = jnp.float32, jnp.bfloat16
 VMEM = pl.BlockSpec(memory_space=pltpu.VMEM)
-ANY = pl.BlockSpec(memory_space=pl.ANY)
 SMEM = pl.BlockSpec(memory_space=pltpu.SMEM)
 PARAMS = pltpu.CompilerParams(vmem_limit_bytes=40 * 1024 * 1024)
-
-
-def passed_on(value, axis, by):
-    count = lax.axis_size(axis)
-    return lax.ppermute(value, axis, [(i, i + by) for i in range(count) if 0 <= i + by < count])
 
 
 def spread(value, axis):
@@ -28,32 +22,26 @@
     return lax.all_to_all(copies, axis, split_axis=0, concat_axis=0)
 
 
-def copies_kernel(own_ref, other_ref, up_ref, down_ref, out_ref):
+def copies_kernel(own_ref, other_ref, out_ref):
     share = own_ref.shape[0]
     for k in range(out_ref.shape[0]):
         out_ref[k, :share] = own_ref[...]
         out_ref[k, share:] = other_ref[...]
 
 
-def spread_kernel(near_ref, up_ref, down_ref, out_ref):
+def spread_kernel(near_ref, out_ref):
     for k in range(out_ref.shape[0]):
         out_ref[k] = near_ref[...]
 
 
-def embed_kernel(
-    place, order_ref, gathered_ref, x0, up1, up2, up3, down1, down2, down3,
-    half_ref, unit_ref, radius_ref, rows_ref, mapping,
-):
+def embed_kernel(order_ref, gathered_ref, rows_ref, half_ref, unit_ref, radius_ref, mapping):
     mapping[...] = jnp.dot(
         order_ref[...], gathered_ref[...], preferred_element_type=F32
     ).astype(BF16)
-    blocks = ((x0, None), (up1, down3), (up2, down2), (up3, down1))
-    for k, (low, high) in enumerate(blocks):
-        rows = low.shape[0]
-        at = pl.ds(k * rows, rows)
-        block = low[...] if high is None else jnp.where(place[0] >= k, low[...], high[...])
-        rows_ref[at, :] = block
-        out = jnp.dot(block, mapping[...], preferred_element_type=F32)
+    block = 256
+    for k in range(rows_ref.shape[0] // block):
+        at = pl.ds(k * block, block)
+        out = jnp.dot(rows_ref[at, :], mapping[...], preferred_element_type=F32)
         radius = jnp.sqrt(jnp.sum(out * out, axis=-1, keepdims=True) + 1e-06)
         unit = out / radius
         radius_ref[at, :] = radius
@@ -83,11 +71,14 @@
         unit = unit_ref[at, :]
         pre = (grad - unit * jnp.sum(unit * grad, axis=-1, keepdims=True)) / radius_ref[at, :]
         pre_ref[...] = pre
-        if k == 0:
+
+        @pl.when(place[0] == k)
+        def _():
             wide = rows_ref[at, :].astype(F32)
             norms_ref[...] = jnp.sqrt(jnp.sum(wide * wide, axis=-1, keepdims=True)) * jnp.sqrt(
                 jnp.sum(pre * pre, axis=-1, keepdims=True)
             )
+
         part = lax.dot_general(
             rows_ref[at, :],
             pre_ref[:, pl.ds(start, 256)].astype(BF16),
@@ -117,27 +108,24 @@
     mine = jnp.where(first, picture_inputs, caption_inputs)
     sent = jnp.where(first, caption_inputs, picture_inputs)
     chunk = jnp.concatenate([mine, lax.ppermute(sent, "core", SWAP)], axis=0)
-    up, down = [chunk], [chunk]
-    for _ in range(1, chips):
-        up.append(passed_on(up[-1], "zlo", 1))
-        down.append(passed_on(down[-1], "zlo", -1))
+    set_rows = lax.all_gather(chunk, "zlo", axis=0, tiled=True)
     at_chip = lax.axis_index("zlo").astype(jnp.int32).reshape(1)
     copies = pl.pallas_call(
         copies_kernel,
         out_shape=jax.ShapeDtypeStruct((n_y, n_zhi * share, embed), BF16),
-        in_specs=[VMEM, VMEM, ANY, ANY],
+        in_specs=[VMEM] * 2,
         out_specs=VMEM,
         cost_estimate=pl.CostEstimate(flops=0, bytes_accessed=2**19, transcendentals=0),
-    )(piece, other, up[1], down[1])
+    )(piece, other)
     near = lax.all_to_all(copies, "y", split_axis=0, concat_axis=0)
     near = near.reshape(n_y * n_zhi * share, embed)
     copies = pl.pallas_call(
         spread_kernel,
         out_shape=jax.ShapeDtypeStruct((n_x,) + near.shape, BF16),
-        in_specs=[VMEM, ANY, ANY],
+        in_specs=[VMEM],
         out_specs=VMEM,
         cost_estimate=pl.CostEstimate(flops=0, bytes_accessed=2**21, transcendentals=0),
-    )(near, up[2], down[2])
+    )(near)
     gathered = lax.all_to_all(copies, "x", split_axis=0, concat_axis=0).reshape(width, embed)
     at = jnp.arange(width, dtype=jnp.int32)
     owner, row = at // share, at % share
@@ -146,22 +134,21 @@
     from_row = (((owner % n_x) * n_y + owner // (n_x * n_zhi)) * n_zhi + at_half) * share + row
     order = (from_row[:, None] == at[None, :]).astype(BF16)
     rows = chips * chunk.shape[0]
-    half, unit, radius, set_rows = pl.pallas_call(
+    half, unit, radius = pl.pallas_call(
         embed_kernel,
         out_shape=(
             jax.ShapeDtypeStruct((rows, embed), BF16),
             jax.ShapeDtypeStruct((rows, embed), F32),
             jax.ShapeDtypeStruct((rows, 1), F32),
-            jax.ShapeDtypeStruct((rows, width), BF16),
         ),
-        in_specs=[SMEM] + [VMEM] * 9,
-        out_specs=(VMEM,) * 4,
+        in_specs=[VMEM] * 3,
+        out_specs=(VMEM,) * 3,
         scratch_shapes=[pltpu.VMEM((width, embed), BF16)],
         compiler_params=PARAMS,
         cost_estimate=pl.CostEstimate(
             flops=2 * (rows + width) * width * embed, bytes_accessed=8 * 2**20, transcendentals=0
         ),
-    )(at_chip, order, gathered, *up, *down[1:])
+    )(order, gathered, set_rows)
     partner = lax.ppermute(half, "core", SWAP)
     columns = embed // chips
     local, norms = pl.pallas_call(

time: 138 us -> 145 us (1.051)
  starting transfers between devices: 68 us -> 44.9 us
  blocking collectives: 0 us -> 15.3 us
  between operations: 2.13 us -> 15.5 us
  waiting for transfers between devices: 46.2 us -> 39.8 us
  local copies, waits for them, and re-layouts: 5.76 us -> 10.4 us
  Pallas kernels: 13.4 us -> 15 us
    ppermute x6 -> x0, waiting for transfers between devices: 16.8 us -> none  [passed_on(): lax.ppermute(value, axis, [(i, i + by) for i in range(count) if 0 <= i +...]
    all_to_all x0 -> x1, blocking collectives: none -> 15.3 us  [on_device(): near = lax.all_to_all(copies, 'y', split_axis=0, concat_axis=0)]
    ppermute x6 -> x0, starting transfers between devices: 14.5 us -> none  [passed_on(): lax.ppermute(value, axis, [(i, i + by) for i in range(count) if 0 <= i +...]
    all_to_all x1, waiting for transfers between devices: 0.01 us -> 12.5 us  [on_device(): lax.all_to_all(copies, 'x', split_axis=0, concat_axis=0)]
    all_to_all x1 -> x0, starting transfers between devices: 6.82 us -> none  [on_device(): near = lax.all_to_all(copies, 'y', split_axis=0, concat_axis=0)]
    unnamed x18 -> x16, local copies, waits for them, and re-layouts: 2.26 us -> 6.95 us
    ppermute x1, waiting for transfers between devices: 5.8 us -> 3.21 us  [on_device(): other = lax.ppermute(piece, 'zhi', SWAP)]
    pallas_call x1, Pallas kernels: 5.88 us -> 7.83 us  [on_device(): pl.pallas_call(functools.partial(grad_kernel, own), out_shape=(jax.ShapeD...]
  transfers between devices with their start and end apart: 14 -> 8, of which waited for: 9 -> 6; matrix products, arithmetic and copies ran while one was open for 1% -> 1% of each run, Pallas kernels for 0% -> 2%
where the time goes in v3:
time: 145 us; the launch traced here: 144 us
  starting transfers between devices  44.9 us (31%)
  waiting for transfers between devices  39.8 us (27%)
  between operations  15.5 us (11%)
  blocking collectives  15.3 us (11%)
  Pallas kernels  15 us (10%)
  local copies, waits for them, and re-layouts  10.4 us (7%)
  other arithmetic  2.87 us (2%)
    all_to_all x1, waiting for transfers between devices, on_device(): lax.all_to_all(local.reshape(width // share, share, columns), GRP, split_...  15.9 us
    all_to_all x1, blocking collectives, on_device(): near = lax.all_to_all(copies, 'y', split_axis=0, concat_axis=0)  15.3 us
    all_to_all x1, waiting for transfers between devices, on_device(): lax.all_to_all(copies, 'x', split_axis=0, concat_axis=0)  12.5 us
    all_to_all x1, starting transfers between devices, on_device(): lax.all_to_all(local.reshape(width // share, share, columns), GRP, split_...  10.1 us
    ppermute x1, starting transfers between devices, on_device(): chunk = jnp.concatenate([mine, lax.ppermute(sent, 'core', SWAP)], axis=0)  8.79 us
    pallas_call x1, Pallas kernels, on_device(): pl.pallas_call(functools.partial(grad_kernel, own), out_shape=(jax.ShapeD...  7.83 us
    all_to_all x1, starting transfers between devices, spread(): return lax.all_to_all(copies, axis, split_axis=0, concat_axis=0)  7.58 us
    unnamed x16, local copies, waits for them, and re-layouts  6.95 us
  transfers between devices with their start and end apart: 8, of which 6 were waited for; matrix products, arithmetic and copies ran while one was open for 1% of the time, Pallas kernels for 2%

profile of v3, /device:TPU:1, one launch (start us, length us, event | category | flops | bytes accessed | tf_op | source)
XLA Modules:
  0.0 143.8 jit_solution(12611596128255427726)
XLA Ops:
  7.2 0.0 copy-start.5
  7.2 0.0 copy-start.6
  7.2 0.0 all-gather.2.cloned.1.call-start
  7.2 1.1 broadcast_select_fusion.1
  8.3 8.8 %collective-permute-start.1 = (bf16[128,768]{1,0:T(8,128)(2,1)S(1)}, bf16[128,768]{1,0:T(8,128)(2,1)S(1)}, u32[]{:S(2)}, u32[]{:S(2)}) collective-permute-start(bf16[128,768]{1,0:T(8,128)(2,1)S(1)} %get-tuple-element.19), channel_id=1, source_target_pairs={{0,64},{64,0},{1,65},{65,1},{2,66},{66,2},{3,67},{67,3},{4,68},{68... | collective-permute-start | bytes 589832 | tf_op jit(solution)/shard_map/ppermute | solution.py:110
  17.1 1.0 collective-permute-done.1
  18.1 0.8 pad_maximum_fusion
  18.9 0.0 all-gather.2.cloned.1.call-update
  19.0 0.0 copy-done.5
  19.0 0.0 copy-done.6
  19.0 0.0 copy-start.4
  19.0 5.3 %collective-permute-start = (bf16[12,768]{1,0:T(8,128)(2,1)S(1)}, bf16[12,768]{1,0:T(8,128)(2,1)S(1)}, u32[]{:S(2)}, u32[]{:S(2)}) collective-permute-start(bf16[12,768]{1,0:T(8,128)(2,1)S(1)} %broadcast_select_fusion.2.own_ref), channel_id=1, source_target_pairs={{0,4},{4,0},{1,5},{5,1},{2,6},{6,2},{3,7},{7,3},{8,12},{12,8},{9,1... | collective-permute-start | bytes 55304 | tf_op jit(solution)/shard_map/ppermute | solution.py:107
  24.3 3.2 %collective-permute-done.other_ref = bf16[12,768]{1,0:T(8,128)(2,1)S(1)} collective-permute-done((bf16[12,768]{1,0:T(8,128)(2,1)S(1)}, bf16[12,768]{1,0:T(8,128)(2,1)S(1)}, u32[]{:S(2)}, u32[]{:S(2)}) %collective-permute-start) | collective-permute-done | bytes 18464 | tf_op jit(solution)/shard_map/ppermute | solution.py:107
  27.5 0.0 copy-done.4
  27.5 0.0 copy-start.7
  27.5 0.6 copy-done.7
  28.1 1.5 %shard_map.93 = bf16[8,24,768]{2,1,0:T(8,128)(2,1)} custom-call(bf16[12,768]{1,0:T(8,128)(2,1)} %copy-done.4, bf16[12,768]{1,0:T(8,128)(2,1)} %copy-done.7), custom_call_target="tpu_custom_call" | custom-call | bytes 524288 | tf_op jit(solution)/shard_map/pallas_call | solution.py:113
  29.6 15.3 %all_to_all.20 = bf16[8,24,768]{2,1,0:T(8,128)(2,1)} all-to-all(bf16[8,24,768]{2,1,0:T(8,128)(2,1)} %shard_map.93), channel_id=1, replica_groups=mesh['zlo'=4,'core'=2,'y'=8,'zhi'=2,'x'=4] {'y'}, dimensions={0} | all-to-all | bytes 589824 | tf_op jit(solution)/shard_map/all_to_all | solution.py:120
  44.9 2.1 %shard_map.94 = bf16[4,192,768]{2,1,0:T(8,128)(2,1)} custom-call(bf16[192,768]{1,0:T(8,128)(2,1)} %bitcast.8), custom_call_target="tpu_custom_call" | custom-call | bytes 2097152 | tf_op jit(solution)/shard_map/pallas_call | solution.py:122
  47.0 4.0 %all-to-all-start.1 = ((bf16[4,192,768]{2,1,0:T(8,128)(2,1)}), bf16[4,192,768]{2,1,0:T(8,128)(2,1)S(1)}, u32[]{:S(2)}, u32[]{:S(2)}) async-start(bf16[4,192,768]{2,1,0:T(8,128)(2,1)} %shard_map.94), calls=%async_computation.1 | async-start | bytes 2359296 | tf_op jit(solution)/shard_map/all_to_all | solution.py:129
  51.0 0.3 fusion.order_ref
  51.3 12.5 %all-to-all-done.1 = bf16[4,192,768]{2,1,0:T(8,128)(2,1)S(1)} async-done(((bf16[4,192,768]{2,1,0:T(8,128)(2,1)}), bf16[4,192,768]{2,1,0:T(8,128)(2,1)S(1)}, u32[]{:S(2)}, u32[]{:S(2)}) %all-to-all-start.1) | async-done | bytes 1179680 | tf_op jit(solution)/shard_map/all_to_all | solution.py:129
  63.8 0.0 all-gather.2.cloned.1.call-done.rows_ref
  63.8 0.0 copy-start
  63.8 1.4 copy-done
  65.2 3.6 %shard_map.95 = (bf16[1024,768]{1,0:T(8,128)(2,1)}, f32[1024,768]{1,0:T(8,128)S(1)}, f32[1024,1]{1,0:T(8,128)S(1)}) custom-call(bf16[768,768]{1,0:T(8,128)(2,1)S(1)} %fusion.order_ref, bf16[768,768]{1,0:T(8,128)(2,1)S(1)} %bitcast.7, bf16[1024,768]{1,0:T(8,128)(2,1)S(1)} %copy-done), custom_call_target="tpu_custom_call" | custom-call | flops 2113929216 | bytes 8388608 | tf_op jit(solution)/shard_map/pallas_call | solution.py:137
  68.9 0.0 copy-start.2
  68.9 1.6 %copy-done.2 = f32[1024,768]{1,0:T(8,128)} copy-done((f32[1024,768]{1,0:T(8,128)}, f32[1024,768]{1,0:T(8,128)S(1)}, u32[]{:S(2)}) %copy-start.2) | copy-done | bytes 3145752
  70.5 6.5 %collective-permute-start.2 = (bf16[1024,768]{1,0:T(8,128)(2,1)}, bf16[1024,768]{1,0:T(8,128)(2,1)S(1)}, u32[]{:S(2)}, u32[]{:S(2)}) collective-permute-start(bf16[1024,768]{1,0:T(8,128)(2,1)} %get-tuple-element.9.half_ref), channel_id=1, source_target_pairs={{0,64},{64,0},{1,65},{65,1},{2,66},{66,2},{3,67},{67,3},{4,68},{68... | collective-permute-start | bytes 4718600 | tf_op jit(solution)/shard_map/ppermute | solution.py:152
  78.3 0.1 pad_maximum_fusion.1.scalars
  78.4 1.9 %collective-permute-done.2.partner_ref = bf16[1024,768]{1,0:T(8,128)(2,1)S(1)} collective-permute-done((bf16[1024,768]{1,0:T(8,128)(2,1)}, bf16[1024,768]{1,0:T(8,128)(2,1)S(1)}, u32[]{:S(2)}, u32[]{:S(2)}) %collective-permute-start.2) | collective-permute-done | bytes 1572896 | tf_op jit(solution)/shard_map/ppermute | solution.py:152
  80.3 0.0 copy-start.1
  80.3 1.4 copy-done.1
  81.7 0.0 copy-start.3
  81.7 1.9 %copy-done.3 = f32[1024,768]{1,0:T(8,128)S(1)} copy-done((f32[1024,768]{1,0:T(8,128)S(1)}, f32[1024,768]{1,0:T(8,128)}, u32[]{:S(2)}) %copy-start.3) | copy-done | bytes 3145752
  83.6 7.8 %shard_map.96 = (bf16[768,192]{1,0:T(8,128)(2,1)S(1)}, f32[256,1]{1,0:T(8,128)S(1)}) custom-call(f32[2]{0:T(128)S(1)} %pad_maximum_fusion.1.scalars, s32[1]{0:T(128)} %bitcast.place, bf16[1024,768]{1,0:T(8,128)(2,1)} %get-tuple-element.9.half_ref, bf16[1024,768]{1,0:T(8,128)(2,1)S(1)} %collective-permute-done.2.partner_ref, f32[1024,768]{1,0:T(8,128)S(1)} %copy-done.3, ...), custom_call_target="tpu_custom_call" | custom-call | flops 3221225472 | bytes 8388608 | tf_op jit(solution)/shard_map/pallas_call | solution.py:154
  91.4 0.9 reshape.107
  92.3 10.1 %all-to-all-start.2 = ((bf16[64,12,192]{2,1,0:T(8,128)(2,1)}), bf16[64,12,192]{2,1,0:T(8,128)(2,1)S(1)}, u32[]{:S(2)}, u32[]{:S(2)}) async-start(bf16[64,12,192]{2,1,0:T(8,128)(2,1)} %reshape.107), calls=%async_computation.2 | async-start | bytes 1048576 | tf_op jit(solution)/shard_map/all_to_all | solution.py:176
  102.4 0.1 slice_reduce_fusion
  102.5 2.6 %collective-permute-start.3 = (f32[128]{0:T(128)S(1)}, f32[128]{0:T(128)S(1)}, u32[]{:S(2)}, u32[]{:S(2)}) collective-permute-start(f32[128]{0:T(128)S(1)} %get-tuple-element.14), channel_id=1, source_target_pairs={{0,64},{64,0},{1,65},{65,1},{2,66},{66,2},{3,67},{67,3},{4,68},{68... | collective-permute-start | bytes 1544 | tf_op jit(solution)/shard_map/ppermute | solution.py:184
  105.1 15.9 %all-to-all-done.2 = bf16[64,12,192]{2,1,0:T(8,128)(2,1)S(1)} async-done(((bf16[64,12,192]{2,1,0:T(8,128)(2,1)}), bf16[64,12,192]{2,1,0:T(8,128)(2,1)S(1)}, u32[]{:S(2)}, u32[]{:S(2)}) %all-to-all-start.2) | async-done | bytes 294944 | tf_op jit(solution)/shard_map/all_to_all | solution.py:176
  121.0 0.1 convert_reduce_fusion
  121.1 0.7 broadcast_in_dim.2
  121.7 7.6 %all-to-all-start.3 = ((f32[8,12,192]{2,1,0:T(8,128)}), f32[8,12,192]{2,1,0:T(8,128)S(1)}, u32[]{:S(2)}, u32[]{:S(2)}) async-start(f32[8,12,192]{2,1,0:T(8,128)} %broadcast_in_dim.2), calls=%async_computation.3 | async-start | bytes 262144 | tf_op jit(solution)/shard_map/all_to_all | solution.py:22
  129.3 0.0 collective-permute-done.3
  129.3 0.5 broadcast_select_fusion.3
  129.9 5.3 %all-to-all-done.3 = f32[8,12,192]{2,1,0:T(8,128)S(1)} async-done(((f32[8,12,192]{2,1,0:T(8,128)}), f32[8,12,192]{2,1,0:T(8,128)S(1)}, u32[]{:S(2)}, u32[]{:S(2)}) %all-to-all-start.3) | async-done | bytes 73760 | tf_op jit(solution)/shard_map/all_to_all | solution.py:22
  135.1 0.1 copy.13
  135.2 0.3 slice_reduce_fusion.2
  135.5 0.7 squeeze.6
  136.2 0.7 squeeze.7
  (2 shorter events, 0.0 us)
Async XLA Ops:
  7.2 11.8 %copy-start.5 = (bf16[12,768]{1,0:T(8,128)(2,1)S(1)}, bf16[12,768]{1,0:T(8,128)(2,1)}, u32[]{:S(2)}) copy-start(bf16[12,768]{1,0:T(8,128)(2,1)} %param.8) | copy-start | bytes 55300
  7.2 11.8 %copy-start.6 = (bf16[12,768]{1,0:T(8,128)(2,1)S(1)}, bf16[12,768]{1,0:T(8,128)(2,1)}, u32[]{:S(2)}) copy-start(bf16[12,768]{1,0:T(8,128)(2,1)} %param.9) | copy-start | bytes 55300
  7.2 56.6 %all-gather.2.cloned.1.call-start = ((), (), s32[]{:S(2)}) async-start(), calls=%async_computation.4 | async-start | bytes 1966080 | tf_op jit(solution)/shard_map/all_gather | solution.py:111
  8.3 9.8 %collective-permute-start.1 = (bf16[128,768]{1,0:T(8,128)(2,1)S(1)}, bf16[128,768]{1,0:T(8,128)(2,1)S(1)}, u32[]{:S(2)}, u32[]{:S(2)}) collective-permute-start(bf16[128,768]{1,0:T(8,128)(2,1)S(1)} %get-tuple-element.19), channel_id=1, source_target_pairs={{0,64},{64,0},{1,65},{65,1},{2,66},{66,2},{3,67},{67,3},{4,68},{68... | collective-permute-start | bytes 589832 | tf_op jit(solution)/shard_map/ppermute | solution.py:110
  19.0 8.5 %copy-start.4 = (bf16[12,768]{1,0:T(8,128)(2,1)}, bf16[12,768]{1,0:T(8,128)(2,1)S(1)}, u32[]{:S(2)}) copy-start(bf16[12,768]{1,0:T(8,128)(2,1)S(1)} %broadcast_select_fusion.2.own_ref) | copy-start | bytes 55300
  19.0 8.5 %collective-permute-start = (bf16[12,768]{1,0:T(8,128)(2,1)S(1)}, bf16[12,768]{1,0:T(8,128)(2,1)S(1)}, u32[]{:S(2)}, u32[]{:S(2)}) collective-permute-start(bf16[12,768]{1,0:T(8,128)(2,1)S(1)} %broadcast_select_fusion.2.own_ref), channel_id=1, source_target_pairs={{0,4},{4,0},{1,5},{5,1},{2,6},{6,2},{3,7},{7,3},{8,12},{12,8},{9,1... | collective-permute-start | bytes 55304 | tf_op jit(solution)/shard_map/ppermute | solution.py:107
  27.5 0.6 copy-start.7
  47.0 16.8 %all-to-all-start.1 = ((bf16[4,192,768]{2,1,0:T(8,128)(2,1)}), bf16[4,192,768]{2,1,0:T(8,128)(2,1)S(1)}, u32[]{:S(2)}, u32[]{:S(2)}) async-start(bf16[4,192,768]{2,1,0:T(8,128)(2,1)} %shard_map.94), calls=%async_computation.1 | async-start | bytes 2359296 | tf_op jit(solution)/shard_map/all_to_all | solution.py:129
  63.8 1.4 copy-start
  68.9 1.6 %copy-start.2 = (f32[1024,768]{1,0:T(8,128)}, f32[1024,768]{1,0:T(8,128)S(1)}, u32[]{:S(2)}) copy-start(f32[1024,768]{1,0:T(8,128)S(1)} %get-tuple-element.10.unit_ref) | copy-start | bytes 9437188
  70.5 9.8 %collective-permute-start.2 = (bf16[1024,768]{1,0:T(8,128)(2,1)}, bf16[1024,768]{1,0:T(8,128)(2,1)S(1)}, u32[]{:S(2)}, u32[]{:S(2)}) collective-permute-start(bf16[1024,768]{1,0:T(8,128)(2,1)} %get-tuple-element.9.half_ref), channel_id=1, source_target_pairs={{0,64},{64,0},{1,65},{65,1},{2,66},{66,2},{3,67},{67,3},{4,68},{68... | collective-permute-start | bytes 4718600 | tf_op jit(solution)/shard_map/ppermute | solution.py:152
  80.3 1.4 copy-start.1
  81.7 1.9 %copy-start.3 = (f32[1024,768]{1,0:T(8,128)S(1)}, f32[1024,768]{1,0:T(8,128)}, u32[]{:S(2)}) copy-start(f32[1024,768]{1,0:T(8,128)} %copy-done.2) | copy-start | bytes 9437188
  92.3 28.6 %all-to-all-start.2 = ((bf16[64,12,192]{2,1,0:T(8,128)(2,1)}), bf16[64,12,192]{2,1,0:T(8,128)(2,1)S(1)}, u32[]{:S(2)}, u32[]{:S(2)}) async-start(bf16[64,12,192]{2,1,0:T(8,128)(2,1)} %reshape.107), calls=%async_computation.2 | async-start | bytes 1048576 | tf_op jit(solution)/shard_map/all_to_all | solution.py:176
  102.5 26.8 %collective-permute-start.3 = (f32[128]{0:T(128)S(1)}, f32[128]{0:T(128)S(1)}, u32[]{:S(2)}, u32[]{:S(2)}) collective-permute-start(f32[128]{0:T(128)S(1)} %get-tuple-element.14), channel_id=1, source_target_pairs={{0,64},{64,0},{1,65},{65,1},{2,66},{66,2},{3,67},{67,3},{4,68},{68... | collective-permute-start | bytes 1544 | tf_op jit(solution)/shard_map/ppermute | solution.py:184
  121.7 13.4 %all-to-all-start.3 = ((f32[8,12,192]{2,1,0:T(8,128)}), f32[8,12,192]{2,1,0:T(8,128)S(1)}, u32[]{:S(2)}, u32[]{:S(2)}) async-start(f32[8,12,192]{2,1,0:T(8,128)} %broadcast_in_dim.2), calls=%async_computation.3 | async-start | bytes 262144 | tf_op jit(solution)/shard_map/all_to_all | solution.py:22
Sparse Core Ops, SparseCore 0:
  19.1 43.5 all-gather.1

commit v4 on v3

--- a/solution.py
+++ b/solution.py
@@ -12,8 +12,14 @@
 SWAP = [(0, 1), (1, 0)]
 F32, BF16 = jnp.float32, jnp.bfloat16
 VMEM = pl.BlockSpec(memory_space=pltpu.VMEM)
+STACK = 10**10
 SMEM = pl.BlockSpec(memory_space=pltpu.SMEM)
 PARAMS = pltpu.CompilerParams(vmem_limit_bytes=40 * 1024 * 1024)
+
+
+def turned(value, axis, by):
+    count = lax.axis_size(axis)
+    return lax.ppermute(value, axis, [(i, (i + by) % count) for i in range(count)])
 
 
 def spread(value, axis):
@@ -32,6 +38,12 @@
 def spread_kernel(near_ref, out_ref):
     for k in range(out_ref.shape[0]):
         out_ref[k] = near_ref[...]
+
+
+def stack_kernel(x0, x1, x2, x3, rows_ref):
+    rows = x0.shape[0]
+    for k, x in enumerate((x0, x1, x2, x3)):
+        rows_ref[pl.ds(k * rows, rows), :] = x[...]
 
 
 def embed_kernel(order_ref, gathered_ref, rows_ref, half_ref, unit_ref, radius_ref, mapping):
@@ -71,14 +83,11 @@
         unit = unit_ref[at, :]
         pre = (grad - unit * jnp.sum(unit * grad, axis=-1, keepdims=True)) / radius_ref[at, :]
         pre_ref[...] = pre
-
-        @pl.when(place[0] == k)
-        def _():
+        if k == 0:
             wide = rows_ref[at, :].astype(F32)
             norms_ref[...] = jnp.sqrt(jnp.sum(wide * wide, axis=-1, keepdims=True)) * jnp.sqrt(
                 jnp.sum(pre * pre, axis=-1, keepdims=True)
             )
-
         part = lax.dot_general(
             rows_ref[at, :],
             pre_ref[:, pl.ds(start, 256)].astype(BF16),
@@ -108,7 +117,14 @@
     mine = jnp.where(first, picture_inputs, caption_inputs)
     sent = jnp.where(first, caption_inputs, picture_inputs)
     chunk = jnp.concatenate([mine, lax.ppermute(sent, "core", SWAP)], axis=0)
-    set_rows = lax.all_gather(chunk, "zlo", axis=0, tiled=True)
+    chunks = [chunk] + [turned(chunk, "zlo", k) for k in range(1, chips)]
+    set_rows = pl.pallas_call(
+        stack_kernel,
+        out_shape=jax.ShapeDtypeStruct((chips * 2 * own, width), BF16),
+        in_specs=[VMEM] * 4,
+        out_specs=VMEM,
+        cost_estimate=pl.CostEstimate(flops=STACK, bytes_accessed=2**21, transcendentals=0),
+    )(*chunks)
     at_chip = lax.axis_index("zlo").astype(jnp.int32).reshape(1)
     copies = pl.pallas_call(
         copies_kernel,

time: 145 us -> 143 us (0.986)
  starting transfers between devices: 44.9 us -> 68.9 us
  blocking collectives: 15.3 us -> 0 us
  between operations: 15.5 us -> 2.09 us
  Pallas kernels: 15 us -> 16.6 us
    all_to_all x1 -> x0, blocking collectives: 15.3 us -> none  [on_device(): near = lax.all_to_all(copies, 'y', split_axis=0, concat_axis=0)]
    ppermute x0 -> x3, waiting for transfers between devices: none -> 13.7 us  [turned(): lax.ppermute(value, axis, [(i, (i + by) % count) for i in range(count)])]
    all_to_all x1, waiting for transfers between devices: 12.5 us -> 0.01 us  [on_device(): lax.all_to_all(copies, 'x', split_axis=0, concat_axis=0)]
    ppermute x0 -> x3, starting transfers between devices: none -> 10.9 us  [turned(): lax.ppermute(value, axis, [(i, (i + by) % count) for i in range(count)])]
    all_to_all x1, starting transfers between devices: 7.58 us -> 14.9 us  [spread(): return lax.all_to_all(copies, axis, split_axis=0, concat_axis=0)]
    all_to_all x0 -> x1, starting transfers between devices: none -> 5.17 us  [on_device(): near = lax.all_to_all(copies, 'y', split_axis=0, concat_axis=0)]
    all_to_all x1, starting transfers between devices: 10.1 us -> 14.3 us  [on_device(): lax.all_to_all(local.reshape(width // share, share, columns), GRP, split_...]
    ppermute x1, starting transfers between devices: 6.53 us -> 3.05 us  [on_device(): partner = lax.ppermute(half, 'core', SWAP)]
  transfers between devices with their start and end apart: 8 -> 11, of which waited for: 6 -> 5; matrix products, arithmetic and copies ran while one was open for 1% -> 2% of each run, Pallas kernels for 2% -> 4%
where the time goes in v4:
time: 143 us; the launch traced here: 142 us
  starting transfers between devices  68.9 us (48%)
  waiting for transfers between devices  40 us (28%)
  Pallas kernels  16.6 us (12%)
  local copies, waits for them, and re-layouts  11.1 us (8%)
  other arithmetic  2.85 us (2%)
  between operations  2.09 us (1%)
    all_to_all x1, waiting for transfers between devices, on_device(): lax.all_to_all(local.reshape(width // share, share, columns), GRP, split_...  15.9 us
    all_to_all x1, starting transfers between devices, spread(): return lax.all_to_all(copies, axis, split_axis=0, concat_axis=0)  14.9 us
    all_to_all x1, starting transfers between devices, on_device(): lax.all_to_all(local.reshape(width // share, share, columns), GRP, split_...  14.3 us
    ppermute x3, waiting for transfers between devices, turned(): lax.ppermute(value, axis, [(i, (i + by) % count) for i in range(count)])  13.7 us
    ppermute x3, starting transfers between devices, turned(): lax.ppermute(value, axis, [(i, (i + by) % count) for i in range(count)])  10.9 us
    ppermute x1, starting transfers between devices, on_device(): chunk = jnp.concatenate([mine, lax.ppermute(sent, 'core', SWAP)], axis=0)  8.79 us
    unnamed x16, local copies, waits for them, and re-layouts  7.67 us
    pallas_call x1, Pallas kernels, on_device(): pl.pallas_call(functools.partial(grad_kernel, own), out_shape=(jax.ShapeD...  6.76 us
  transfers between devices with their start and end apart: 11, of which 5 were waited for; matrix products, arithmetic and copies ran while one was open for 2% of the time, Pallas kernels for 4%

profile of v4, /device:TPU:1, one launch (start us, length us, event | category | flops | bytes accessed | tf_op | source)
XLA Modules:
  0.0 141.6 jit_solution(5794348413118990851)
XLA Ops:
  0.6 1.1 broadcast_select_fusion.1
  1.7 8.8 %collective-permute-start.1 = (bf16[128,768]{1,0:T(8,128)(2,1)S(1)}, bf16[128,768]{1,0:T(8,128)(2,1)S(1)}, u32[]{:S(2)}, u32[]{:S(2)}) collective-permute-start(bf16[128,768]{1,0:T(8,128)(2,1)S(1)} %get-tuple-element.19), channel_id=1, source_target_pairs={{0,64},{64,0},{1,65},{65,1},{2,66},{66,2},{3,67},{67,3},{4,68},{68... | collective-permute-start | bytes 589832 | tf_op jit(solution)/shard_map/ppermute | solution.py:119
  10.5 0.8 broadcast_select_fusion.2.own_ref
  11.2 0.0 copy-start.6
  11.2 5.3 %collective-permute-start = (bf16[12,768]{1,0:T(8,128)(2,1)S(1)}, bf16[12,768]{1,0:T(8,128)(2,1)S(1)}, u32[]{:S(2)}, u32[]{:S(2)}) collective-permute-start(bf16[12,768]{1,0:T(8,128)(2,1)S(1)} %broadcast_select_fusion.2.own_ref), channel_id=1, source_target_pairs={{0,4},{4,0},{1,5},{5,1},{2,6},{6,2},{3,7},{7,3},{8,12},{12,8},{9,1... | collective-permute-start | bytes 55304 | tf_op jit(solution)/shard_map/ppermute | solution.py:116
  16.5 3.2 %collective-permute-done.other_ref = bf16[12,768]{1,0:T(8,128)(2,1)S(1)} collective-permute-done((bf16[12,768]{1,0:T(8,128)(2,1)S(1)}, bf16[12,768]{1,0:T(8,128)(2,1)S(1)}, u32[]{:S(2)}, u32[]{:S(2)}) %collective-permute-start) | collective-permute-done | bytes 18464 | tf_op jit(solution)/shard_map/ppermute | solution.py:116
  19.7 0.0 copy-done.6
  19.7 0.0 copy-start.7
  19.7 0.6 copy-done.7
  20.3 1.5 %shard_map.93 = bf16[8,24,768]{2,1,0:T(8,128)(2,1)} custom-call(bf16[12,768]{1,0:T(8,128)(2,1)} %copy-done.6, bf16[12,768]{1,0:T(8,128)(2,1)} %copy-done.7), custom_call_target="tpu_custom_call" | custom-call | bytes 524288 | tf_op jit(solution)/shard_map/pallas_call | solution.py:129
  21.8 5.2 %all-to-all-start = ((bf16[8,24,768]{2,1,0:T(8,128)(2,1)}), bf16[8,24,768]{2,1,0:T(8,128)(2,1)S(1)}, u32[]{:S(2)}, u32[]{:S(2)}) async-start(bf16[8,24,768]{2,1,0:T(8,128)(2,1)} %shard_map.93), calls=%async_computation | async-start | bytes 589824 | tf_op jit(solution)/shard_map/all_to_all | solution.py:136
  27.0 0.0 collective-permute-done.1
  27.0 0.0 copy-start.5
  27.0 3.1 %collective-permute-start.2 = (bf16[256,768]{1,0:T(8,128)(2,1)S(1)}, bf16[256,768]{1,0:T(8,128)(2,1)}, u32[]{:S(2)}, u32[]{:S(2)}) collective-permute-start(bf16[256,768]{1,0:T(8,128)(2,1)S(1)} %pad_maximum_fusion.x0), channel_id=1, source_target_pairs={{0,128},{128,256},{256,384},{384,0},{1,129},{129,257},{257,385},{3... | collective-permute-start | bytes 1179656 | tf_op jit(solution)/shard_map/ppermute | solution.py:22
  30.2 4.0 %collective-permute-start.3 = (bf16[256,768]{1,0:T(8,128)(2,1)S(1)}, bf16[256,768]{1,0:T(8,128)(2,1)}, u32[]{:S(2)}, u32[]{:S(2)}) collective-permute-start(bf16[256,768]{1,0:T(8,128)(2,1)S(1)} %pad_maximum_fusion.x0), channel_id=1, source_target_pairs={{0,256},{128,384},{256,0},{384,128},{1,257},{129,385},{257,1},{385... | collective-permute-start | bytes 1179656 | tf_op jit(solution)/shard_map/ppermute | solution.py:22
  34.2 3.8 %collective-permute-start.4 = (bf16[256,768]{1,0:T(8,128)(2,1)S(1)}, bf16[256,768]{1,0:T(8,128)(2,1)}, u32[]{:S(2)}, u32[]{:S(2)}) collective-permute-start(bf16[256,768]{1,0:T(8,128)(2,1)S(1)} %pad_maximum_fusion.x0), channel_id=1, source_target_pairs={{0,384},{128,0},{256,128},{384,256},{1,385},{129,1},{257,129},{385... | collective-permute-start | bytes 1179656 | tf_op jit(solution)/shard_map/ppermute | solution.py:22
  38.0 0.3 fusion.order_ref
  38.2 0.0 all-to-all-done
  38.3 0.0 copy-start.4
  38.3 0.7 copy-done.4
  39.0 2.1 %shard_map.94 = bf16[4,192,768]{2,1,0:T(8,128)(2,1)} custom-call(bf16[192,768]{1,0:T(8,128)(2,1)} %bitcast.8), custom_call_target="tpu_custom_call" | custom-call | bytes 2097152 | tf_op jit(solution)/shard_map/pallas_call | solution.py:138
  41.1 0.0 copy-done.5
  41.1 4.0 %all-to-all-start.1 = ((bf16[4,192,768]{2,1,0:T(8,128)(2,1)}), bf16[4,192,768]{2,1,0:T(8,128)(2,1)S(1)}, u32[]{:S(2)}, u32[]{:S(2)}) async-start(bf16[4,192,768]{2,1,0:T(8,128)(2,1)} %shard_map.94), calls=%async_computation.1 | async-start | bytes 2359296 | tf_op jit(solution)/shard_map/all_to_all | solution.py:145
  45.1 0.0 collective-permute-done.2.x1
  45.1 13.7 %collective-permute-done.3.x2 = bf16[256,768]{1,0:T(8,128)(2,1)} collective-permute-done((bf16[256,768]{1,0:T(8,128)(2,1)S(1)}, bf16[256,768]{1,0:T(8,128)(2,1)}, u32[]{:S(2)}, u32[]{:S(2)}) %collective-permute-start.3) | collective-permute-done | bytes 393248 | tf_op jit(solution)/shard_map/ppermute | solution.py:22
  58.8 0.0 collective-permute-done.4.x3
  58.8 2.6 %shard_map.95.rows_ref = bf16[1024,768]{1,0:T(8,128)(2,1)} custom-call(bf16[256,768]{1,0:T(8,128)(2,1)} %copy-done.5, bf16[256,768]{1,0:T(8,128)(2,1)} %collective-permute-done.2.x1, bf16[256,768]{1,0:T(8,128)(2,1)} %collective-permute-done.3.x2, bf16[256,768]{1,0:T(8,128)(2,1)} %collective-permute-done.4.x3), custom_call_target="tpu_custom_call" | custom-call | flops 10000000000 | bytes 2097152 | tf_op jit(solution)/shard_map/pallas_call | solution.py:121
  61.4 0.0 all-to-all-done.1
  61.4 0.0 copy-start.2
  61.4 1.4 copy-done.2
  62.8 3.6 %shard_map.96 = (bf16[1024,768]{1,0:T(8,128)(2,1)}, f32[1024,768]{1,0:T(8,128)S(1)}, f32[1024,1]{1,0:T(8,128)S(1)}) custom-call(bf16[768,768]{1,0:T(8,128)(2,1)S(1)} %fusion.order_ref, bf16[768,768]{1,0:T(8,128)(2,1)S(1)} %bitcast.7, bf16[1024,768]{1,0:T(8,128)(2,1)S(1)} %copy-done.2), custom_call_target="tpu_custom_call" | custom-call | flops 2113929216 | bytes 8388608 | tf_op jit(solution)/shard_map/pallas_call | solution.py:153
  66.4 0.0 copy-start
  66.4 1.6 %copy-done = f32[1024,768]{1,0:T(8,128)} copy-done((f32[1024,768]{1,0:T(8,128)}, f32[1024,768]{1,0:T(8,128)S(1)}, u32[]{:S(2)}) %copy-start) | copy-done | bytes 3145752
  68.1 3.1 %collective-permute-start.5 = (bf16[1024,768]{1,0:T(8,128)(2,1)}, bf16[1024,768]{1,0:T(8,128)(2,1)S(1)}, u32[]{:S(2)}, u32[]{:S(2)}) collective-permute-start(bf16[1024,768]{1,0:T(8,128)(2,1)} %get-tuple-element.9.half_ref), channel_id=1, source_target_pairs={{0,64},{64,0},{1,65},{65,1},{2,66},{66,2},{3,67},{67,3},{4,68},{68... | collective-permute-start | bytes 4718600 | tf_op jit(solution)/shard_map/ppermute | solution.py:168
  72.4 0.1 pad_maximum_fusion.1.scalars
  72.5 1.9 %collective-permute-done.5.partner_ref = bf16[1024,768]{1,0:T(8,128)(2,1)S(1)} collective-permute-done((bf16[1024,768]{1,0:T(8,128)(2,1)}, bf16[1024,768]{1,0:T(8,128)(2,1)S(1)}, u32[]{:S(2)}, u32[]{:S(2)}) %collective-permute-start.5) | collective-permute-done | bytes 1572896 | tf_op jit(solution)/shard_map/ppermute | solution.py:168
  74.4 0.0 copy-start.1
  74.4 1.9 %copy-done.1 = f32[1024,768]{1,0:T(8,128)S(1)} copy-done((f32[1024,768]{1,0:T(8,128)S(1)}, f32[1024,768]{1,0:T(8,128)}, u32[]{:S(2)}) %copy-start.1) | copy-done | bytes 3145752
  76.2 0.0 copy-start.3
  76.2 1.4 copy-done.3
  77.6 6.8 %shard_map.97 = (bf16[768,192]{1,0:T(8,128)(2,1)S(1)}, f32[256,1]{1,0:T(8,128)S(1)}) custom-call(f32[2]{0:T(128)S(1)} %pad_maximum_fusion.1.scalars, s32[1]{0:T(128)} %bitcast.place, bf16[1024,768]{1,0:T(8,128)(2,1)} %get-tuple-element.9.half_ref, bf16[1024,768]{1,0:T(8,128)(2,1)S(1)} %collective-permute-done.5.partner_ref, f32[1024,768]{1,0:T(8,128)S(1)} %copy-done.1, ...), custom_call_target="tpu_custom_call" | custom-call | flops 3221225472 | bytes 8388608 | tf_op jit(solution)/shard_map/pallas_call | solution.py:170
  84.4 0.9 reshape.107
  85.3 14.3 %all-to-all-start.2 = ((bf16[64,12,192]{2,1,0:T(8,128)(2,1)}), bf16[64,12,192]{2,1,0:T(8,128)(2,1)S(1)}, u32[]{:S(2)}, u32[]{:S(2)}) async-start(bf16[64,12,192]{2,1,0:T(8,128)(2,1)} %reshape.107), calls=%async_computation.2 | async-start | bytes 1048576 | tf_op jit(solution)/shard_map/all_to_all | solution.py:192
  99.6 0.1 slice_reduce_fusion
  99.8 2.6 %collective-permute-start.6 = (f32[128]{0:T(128)S(1)}, f32[128]{0:T(128)S(1)}, u32[]{:S(2)}, u32[]{:S(2)}) collective-permute-start(f32[128]{0:T(128)S(1)} %get-tuple-element.14), channel_id=1, source_target_pairs={{0,64},{64,0},{1,65},{65,1},{2,66},{66,2},{3,67},{67,3},{4,68},{68... | collective-permute-start | bytes 1544 | tf_op jit(solution)/shard_map/ppermute | solution.py:200
  102.3 15.9 %all-to-all-done.2 = bf16[64,12,192]{2,1,0:T(8,128)(2,1)S(1)} async-done(((bf16[64,12,192]{2,1,0:T(8,128)(2,1)}), bf16[64,12,192]{2,1,0:T(8,128)(2,1)S(1)}, u32[]{:S(2)}, u32[]{:S(2)}) %all-to-all-start.2) | async-done | bytes 294944 | tf_op jit(solution)/shard_map/all_to_all | solution.py:192
  118.3 0.1 convert_reduce_fusion
  118.4 0.7 broadcast_in_dim.2
  119.1 14.9 %all-to-all-start.3 = ((f32[8,12,192]{2,1,0:T(8,128)}), f32[8,12,192]{2,1,0:T(8,128)S(1)}, u32[]{:S(2)}, u32[]{:S(2)}) async-start(f32[8,12,192]{2,1,0:T(8,128)} %broadcast_in_dim.2), calls=%async_computation.3 | async-start | bytes 262144 | tf_op jit(solution)/shard_map/all_to_all | solution.py:28
  134.0 0.0 collective-permute-done.6
  134.0 0.5 broadcast_select_fusion.3
  134.5 5.3 %all-to-all-done.3 = f32[8,12,192]{2,1,0:T(8,128)S(1)} async-done(((f32[8,12,192]{2,1,0:T(8,128)}), f32[8,12,192]{2,1,0:T(8,128)S(1)}, u32[]{:S(2)}, u32[]{:S(2)}) %all-to-all-start.3) | async-done | bytes 73760 | tf_op jit(solution)/shard_map/all_to_all | solution.py:28
  139.8 0.1 copy.13
  139.9 0.3 slice_reduce_fusion.2
  140.1 0.7 squeeze.6
  140.9 0.7 squeeze.7
  (2 shorter events, 0.1 us)
Async XLA Ops:
  1.7 25.3 %collective-permute-start.1 = (bf16[128,768]{1,0:T(8,128)(2,1)S(1)}, bf16[128,768]{1,0:T(8,128)(2,1)S(1)}, u32[]{:S(2)}, u32[]{:S(2)}) collective-permute-start(bf16[128,768]{1,0:T(8,128)(2,1)S(1)} %get-tuple-element.19), channel_id=1, source_target_pairs={{0,64},{64,0},{1,65},{65,1},{2,66},{66,2},{3,67},{67,3},{4,68},{68... | collective-permute-start | bytes 589832 | tf_op jit(solution)/shard_map/ppermute | solution.py:119
  11.2 8.5 %copy-start.6 = (bf16[12,768]{1,0:T(8,128)(2,1)}, bf16[12,768]{1,0:T(8,128)(2,1)S(1)}, u32[]{:S(2)}) copy-start(bf16[12,768]{1,0:T(8,128)(2,1)S(1)} %broadcast_select_fusion.2.own_ref) | copy-start | bytes 55300
  11.2 8.5 %collective-permute-start = (bf16[12,768]{1,0:T(8,128)(2,1)S(1)}, bf16[12,768]{1,0:T(8,128)(2,1)S(1)}, u32[]{:S(2)}, u32[]{:S(2)}) collective-permute-start(bf16[12,768]{1,0:T(8,128)(2,1)S(1)} %broadcast_select_fusion.2.own_ref), channel_id=1, source_target_pairs={{0,4},{4,0},{1,5},{5,1},{2,6},{6,2},{3,7},{7,3},{8,12},{12,8},{9,1... | collective-permute-start | bytes 55304 | tf_op jit(solution)/shard_map/ppermute | solution.py:116
  19.7 0.6 copy-start.7
  21.8 16.4 %all-to-all-start = ((bf16[8,24,768]{2,1,0:T(8,128)(2,1)}), bf16[8,24,768]{2,1,0:T(8,128)(2,1)S(1)}, u32[]{:S(2)}, u32[]{:S(2)}) async-start(bf16[8,24,768]{2,1,0:T(8,128)(2,1)} %shard_map.93), calls=%async_computation | async-start | bytes 589824 | tf_op jit(solution)/shard_map/all_to_all | solution.py:136
  27.0 14.0 %copy-start.5 = (bf16[256,768]{1,0:T(8,128)(2,1)}, bf16[256,768]{1,0:T(8,128)(2,1)S(1)}, u32[]{:S(2)}) copy-start(bf16[256,768]{1,0:T(8,128)(2,1)S(1)} %pad_maximum_fusion.x0) | copy-start | bytes 1179652
  27.0 18.0 %collective-permute-start.2 = (bf16[256,768]{1,0:T(8,128)(2,1)S(1)}, bf16[256,768]{1,0:T(8,128)(2,1)}, u32[]{:S(2)}, u32[]{:S(2)}) collective-permute-start(bf16[256,768]{1,0:T(8,128)(2,1)S(1)} %pad_maximum_fusion.x0), channel_id=1, source_target_pairs={{0,128},{128,256},{256,384},{384,0},{1,129},{129,257},{257,385},{3... | collective-permute-start | bytes 1179656 | tf_op jit(solution)/shard_map/ppermute | solution.py:22
  30.2 28.6 %collective-permute-start.3 = (bf16[256,768]{1,0:T(8,128)(2,1)S(1)}, bf16[256,768]{1,0:T(8,128)(2,1)}, u32[]{:S(2)}, u32[]{:S(2)}) collective-permute-start(bf16[256,768]{1,0:T(8,128)(2,1)S(1)} %pad_maximum_fusion.x0), channel_id=1, source_target_pairs={{0,256},{128,384},{256,0},{384,128},{1,257},{129,385},{257,1},{385... | collective-permute-start | bytes 1179656 | tf_op jit(solution)/shard_map/ppermute | solution.py:22
  34.2 24.6 %collective-permute-start.4 = (bf16[256,768]{1,0:T(8,128)(2,1)S(1)}, bf16[256,768]{1,0:T(8,128)(2,1)}, u32[]{:S(2)}, u32[]{:S(2)}) collective-permute-start(bf16[256,768]{1,0:T(8,128)(2,1)S(1)} %pad_maximum_fusion.x0), channel_id=1, source_target_pairs={{0,384},{128,0},{256,128},{384,256},{1,385},{129,1},{257,129},{385... | collective-permute-start | bytes 1179656 | tf_op jit(solution)/shard_map/ppermute | solution.py:22
  38.3 0.7 copy-start.4
  41.1 20.3 %all-to-all-start.1 = ((bf16[4,192,768]{2,1,0:T(8,128)(2,1)}), bf16[4,192,768]{2,1,0:T(8,128)(2,1)S(1)}, u32[]{:S(2)}, u32[]{:S(2)}) async-start(bf16[4,192,768]{2,1,0:T(8,128)(2,1)} %shard_map.94), calls=%async_computation.1 | async-start | bytes 2359296 | tf_op jit(solution)/shard_map/all_to_all | solution.py:145
  61.4 1.4 copy-start.2
  66.4 1.6 %copy-start = (f32[1024,768]{1,0:T(8,128)}, f32[1024,768]{1,0:T(8,128)S(1)}, u32[]{:S(2)}) copy-start(f32[1024,768]{1,0:T(8,128)S(1)} %get-tuple-element.10.unit_ref) | copy-start | bytes 9437188
  68.1 6.3 %collective-permute-start.5 = (bf16[1024,768]{1,0:T(8,128)(2,1)}, bf16[1024,768]{1,0:T(8,128)(2,1)S(1)}, u32[]{:S(2)}, u32[]{:S(2)}) collective-permute-start(bf16[1024,768]{1,0:T(8,128)(2,1)} %get-tuple-element.9.half_ref), channel_id=1, source_target_pairs={{0,64},{64,0},{1,65},{65,1},{2,66},{66,2},{3,67},{67,3},{4,68},{68... | collective-permute-start | bytes 4718600 | tf_op jit(solution)/shard_map/ppermute | solution.py:168
  74.4 1.9 %copy-start.1 = (f32[1024,768]{1,0:T(8,128)S(1)}, f32[1024,768]{1,0:T(8,128)}, u32[]{:S(2)}) copy-start(f32[1024,768]{1,0:T(8,128)} %copy-done) | copy-start | bytes 9437188
  76.2 1.4 copy-start.3
  85.3 33.0 %all-to-all-start.2 = ((bf16[64,12,192]{2,1,0:T(8,128)(2,1)}), bf16[64,12,192]{2,1,0:T(8,128)(2,1)S(1)}, u32[]{:S(2)}, u32[]{:S(2)}) async-start(bf16[64,12,192]{2,1,0:T(8,128)(2,1)} %reshape.107), calls=%async_computation.2 | async-start | bytes 1048576 | tf_op jit(solution)/shard_map/all_to_all | solution.py:192
  99.8 34.2 %collective-permute-start.6 = (f32[128]{0:T(128)S(1)}, f32[128]{0:T(128)S(1)}, u32[]{:S(2)}, u32[]{:S(2)}) collective-permute-start(f32[128]{0:T(128)S(1)} %get-tuple-element.14), channel_id=1, source_target_pairs={{0,64},{64,0},{1,65},{65,1},{2,66},{66,2},{3,67},{67,3},{4,68},{68... | collective-permute-start | bytes 1544 | tf_op jit(solution)/shard_map/ppermute | solution.py:200
  119.1 20.7 %all-to-all-start.3 = ((f32[8,12,192]{2,1,0:T(8,128)}), f32[8,12,192]{2,1,0:T(8,128)S(1)}, u32[]{:S(2)}, u32[]{:S(2)}) async-start(f32[8,12,192]{2,1,0:T(8,128)} %broadcast_in_dim.2), calls=%async_computation.3 | async-start | bytes 262144 | tf_op jit(solution)/shard_map/all_to_all | solution.py:28

commit v5 on v4

--- a/solution.py
+++ b/solution.py
@@ -14,7 +14,7 @@
 VMEM = pl.BlockSpec(memory_space=pltpu.VMEM)
 STACK = 10**10
 SMEM = pl.BlockSpec(memory_space=pltpu.SMEM)
-PARAMS = pltpu.CompilerParams(vmem_limit_bytes=40 * 1024 * 1024)
+PARAMS = pltpu.CompilerParams(vmem_limit_bytes=24 * 1024 * 1024)
 
 
 def turned(value, axis, by):
@@ -26,18 +26,6 @@
     count = lax.axis_size(axis)
     copies = jnp.broadcast_to(value[None], (count,) + value.shape)
     return lax.all_to_all(copies, axis, split_axis=0, concat_axis=0)
-
-
-def copies_kernel(own_ref, other_ref, out_ref):
-    share = own_ref.shape[0]
-    for k in range(out_ref.shape[0]):
-        out_ref[k, :share] = own_ref[...]
-        out_ref[k, share:] = other_ref[...]
-
-
-def spread_kernel(near_ref, out_ref):
-    for k in range(out_ref.shape[0]):
-        out_ref[k] = near_ref[...]
 
 
 def stack_kernel(x0, x1, x2, x3, rows_ref):
@@ -66,7 +54,7 @@
     local_ref, norms_ref, pre_ref,
 ):
     multiplier, offset = scalars[0], scalars[1]
-    columns = local_ref.shape[1]
+    owners, share, columns = local_ref.shape
     start = pl.multiple_of((3 * place[0]) // 2 * 128, 128)
     total = None
     rows = 2 * own
@@ -96,7 +84,21 @@
         )
         total = part if total is None else total + part
     odd = place[0] % 2 == 1
-    local_ref[...] = jnp.where(odd, total[:, 256 - columns :], total[:, :columns]).astype(BF16)
+    total = jnp.where(odd, total[:, 256 - columns :], total[:, :columns])
+    for k in range(owners):
+        local_ref[k] = total[k * share : (k + 1) * share].astype(BF16)
+
+
+def sum_kernel(pieces_ref, out_ref):
+    total = jnp.sum(pieces_ref[...].astype(F32), axis=0)
+    for k in range(out_ref.shape[0]):
+        out_ref[k] = total
+
+
+def join_kernel(parts_ref, img_ref, txt_ref):
+    for core, ref in enumerate((img_ref, txt_ref)):
+        parts = [parts_ref[k] for k in range(core, parts_ref.shape[0], 2)]
+        ref[...] = jnp.concatenate(parts, axis=1)
 
 
 def on_device(
@@ -113,7 +115,6 @@
     chips = lax.axis_size("zlo")
     n_y, n_zhi, n_x = (lax.axis_size(a) for a in GRP)
     piece = jnp.where(first, picture_mapping, caption_mapping)
-    other = lax.ppermute(piece, "zhi", SWAP)
     mine = jnp.where(first, picture_inputs, caption_inputs)
     sent = jnp.where(first, caption_inputs, picture_inputs)
     chunk = jnp.concatenate([mine, lax.ppermute(sent, "core", SWAP)], axis=0)
@@ -126,28 +127,11 @@
         cost_estimate=pl.CostEstimate(flops=STACK, bytes_accessed=2**21, transcendentals=0),
     )(*chunks)
     at_chip = lax.axis_index("zlo").astype(jnp.int32).reshape(1)
-    copies = pl.pallas_call(
-        copies_kernel,
-        out_shape=jax.ShapeDtypeStruct((n_y, n_zhi * share, embed), BF16),
-        in_specs=[VMEM] * 2,
-        out_specs=VMEM,
-        cost_estimate=pl.CostEstimate(flops=0, bytes_accessed=2**19, transcendentals=0),
-    )(piece, other)
-    near = lax.all_to_all(copies, "y", split_axis=0, concat_axis=0)
-    near = near.reshape(n_y * n_zhi * share, embed)
-    copies = pl.pallas_call(
-        spread_kernel,
-        out_shape=jax.ShapeDtypeStruct((n_x,) + near.shape, BF16),
-        in_specs=[VMEM],
-        out_specs=VMEM,
-        cost_estimate=pl.CostEstimate(flops=0, bytes_accessed=2**21, transcendentals=0),
-    )(near)
-    gathered = lax.all_to_all(copies, "x", split_axis=0, concat_axis=0).reshape(width, embed)
+    near = spread(piece, ("y", "zhi")).reshape(n_y * n_zhi * share, embed)
+    gathered = spread(near, "x").reshape(width, embed)
     at = jnp.arange(width, dtype=jnp.int32)
     owner, row = at // share, at % share
-    at_half = (owner // n_x) % n_zhi
-    at_half = jnp.where(lax.axis_index("zhi") == 0, at_half, 1 - at_half)
-    from_row = (((owner % n_x) * n_y + owner // (n_x * n_zhi)) * n_zhi + at_half) * share + row
+    from_row = ((owner % n_x) * (n_y * n_zhi) + owner // n_x) * share + row
     order = (from_row[:, None] == at[None, :]).astype(BF16)
     rows = chips * chunk.shape[0]
     half, unit, radius = pl.pallas_call(
@@ -170,7 +154,7 @@
     local, norms = pl.pallas_call(
         functools.partial(grad_kernel, own),
         out_shape=(
-            jax.ShapeDtypeStruct((width, columns), BF16),
+            jax.ShapeDtypeStruct((width // share, share, columns), BF16),
             jax.ShapeDtypeStruct((2 * own, 1), F32),
         ),
         in_specs=[SMEM] * 2 + [VMEM] * 5,
@@ -189,18 +173,26 @@
         radius,
         set_rows,
     )
-    pieces = lax.all_to_all(
-        local.reshape(width // share, share, columns), GRP, split_axis=0, concat_axis=0, tiled=True
-    )
-    total = jnp.sum(pieces.astype(F32), axis=0)
-    whole = spread(total, ("zlo", "core")).reshape(chips, 2, share, columns)
-    whole = whole.transpose(1, 2, 0, 3).reshape(2, share, embed)
+    pieces = lax.all_to_all(local, GRP, split_axis=0, concat_axis=0, tiled=True)
+    totals = pl.pallas_call(
+        sum_kernel,
+        out_shape=jax.ShapeDtypeStruct((2 * chips, share, columns), F32),
+        in_specs=[VMEM],
+        out_specs=VMEM,
+    )(pieces)
+    parts = lax.all_to_all(totals, ("zlo", "core"), split_axis=0, concat_axis=0)
+    img_proj_grad, txt_proj_grad = pl.pallas_call(
+        join_kernel,
+        out_shape=(jax.ShapeDtypeStruct((share, embed), F32),) * 2,
+        in_specs=[VMEM],
+        out_specs=(VMEM,) * 2,
+    )(parts)
     norms = norms.reshape(2 * own)
     own_norms = norms[:own]
     their_norms = lax.ppermute(norms[own:], "core", SWAP)
     img_norms = jnp.where(first, own_norms, their_norms)
     txt_norms = jnp.where(first, their_norms, own_norms)
-    return (whole[0], whole[1], img_norms, txt_norms)
+    return (img_proj_grad, txt_proj_grad, img_norms, txt_norms)
 
 
 def build(fine):

time: 143 us -> 146 us (1.021)
  waiting for transfers between devices: 40 us -> 48 us
  starting transfers between devices: 68.9 us -> 65.2 us
    all_to_all x3 -> x2, waiting for transfers between devices: 16 us -> 21.2 us  [the longest x1 15.9 us: on_device(): pieces = lax.all_to_all(local, GRP, split_axis=0, concat_axis=0, tiled=True)]
    ppermute x1 -> x0, starting transfers between devices: 5.25 us -> none  [on_device(): other = lax.ppermute(piece, 'zhi', SWAP)]
    ppermute x3, waiting for transfers between devices: 13.7 us -> 17.6 us  [turned(): lax.ppermute(value, axis, [(i, (i + by) % count) for i in range(count)])]
    all_to_all x3 -> x2, starting transfers between devices: 23.5 us -> 27.2 us  [the longest x1 13.8 us: on_device(): parts = lax.all_to_all(totals, ('zlo', 'core'), split_axis=0, concat_axis=0)]
    ppermute x1 -> x0, waiting for transfers between devices: 3.21 us -> none  [on_device(): other = lax.ppermute(piece, 'zhi', SWAP)]
    all_to_all x1 -> x2, waiting for transfers between devices: 5.29 us -> 7.3 us  [spread(): return lax.all_to_all(copies, axis, split_axis=0, concat_axis=0)]
    all_to_all x1 -> x2, starting transfers between devices: 14.9 us -> 14 us  [spread(): return lax.all_to_all(copies, axis, split_axis=0, concat_axis=0)]
    unnamed x16 -> x14, local copies, waits for them, and re-layouts: 7.67 us -> 7.81 us
  transfers between devices with their start and end apart: 11 -> 10, of which waited for: 5 -> 6; matrix products, arithmetic and copies ran while one was open for 2% -> 3% of each run, Pallas kernels for 4% -> 3%
where the time goes in v5:
time: 146 us; the launch traced here: 145 us
  starting transfers between devices  65.2 us (45%)
  waiting for transfers between devices  48 us (33%)
  Pallas kernels  17.3 us (12%)
  local copies, waits for them, and re-layouts  9.87 us (7%)
  other arithmetic  2.71 us (2%)
  between operations  2.06 us (1%)
    ppermute x3, waiting for transfers between devices, turned(): lax.ppermute(value, axis, [(i, (i + by) % count) for i in range(count)])  17.6 us
    all_to_all x1, waiting for transfers between devices, on_device(): pieces = lax.all_to_all(local, GRP, split_axis=0, concat_axis=0, tiled=True)  15.9 us
    all_to_all x2, starting transfers between devices, spread(): return lax.all_to_all(copies, axis, split_axis=0, concat_axis=0)  14 us
    all_to_all x1, starting transfers between devices, on_device(): parts = lax.all_to_all(totals, ('zlo', 'core'), split_axis=0, concat_axis=0)  13.8 us
    all_to_all x1, starting transfers between devices, on_device(): pieces = lax.all_to_all(local, GRP, split_axis=0, concat_axis=0, tiled=True)  13.4 us
    ppermute x3, starting transfers between devices, turned(): lax.ppermute(value, axis, [(i, (i + by) % count) for i in range(count)])  10.2 us
    ppermute x1, starting transfers between devices, on_device(): chunk = jnp.concatenate([mine, lax.ppermute(sent, 'core', SWAP)], axis=0)  8.79 us
    unnamed x14, local copies, waits for them, and re-layouts  7.81 us
  transfers between devices with their start and end apart: 10, of which 6 were waited for; matrix products, arithmetic and copies ran while one was open for 3% of the time, Pallas kernels for 3%

profile of v5, /device:TPU:1, one launch (start us, length us, event | category | flops | bytes accessed | tf_op | source)
XLA Modules:
  0.0 145.2 jit_solution(14333474035258479936)
XLA Ops:
  0.6 1.1 broadcast_select_fusion.1
  1.7 8.8 %collective-permute-start = (bf16[128,768]{1,0:T(8,128)(2,1)S(1)}, bf16[128,768]{1,0:T(8,128)(2,1)S(1)}, u32[]{:S(2)}, u32[]{:S(2)}) collective-permute-start(bf16[128,768]{1,0:T(8,128)(2,1)S(1)} %get-tuple-element.21), channel_id=1, source_target_pairs={{0,64},{64,0},{1,65},{65,1},{2,66},{66,2},{3,67},{67,3},{4,68},{68... | collective-permute-start | bytes 589832 | tf_op jit(solution)/shard_map/ppermute | solution.py:120
  10.5 0.8 broadcast_select_fusion.2
  11.2 0.8 broadcast_in_dim.6
  12.0 10.0 %all-to-all-start = ((bf16[16,12,768]{2,1,0:T(8,128)(2,1)}), bf16[16,12,768]{2,1,0:T(8,128)(2,1)S(1)}, u32[]{:S(2)}, u32[]{:S(2)}) async-start(bf16[16,12,768]{2,1,0:T(8,128)(2,1)} %broadcast_in_dim.6), calls=%async_computation | async-start | bytes 786432 | tf_op jit(solution)/shard_map/all_to_all | solution.py:28
  22.0 0.0 collective-permute-done
  22.1 0.0 copy-start.6
  22.1 3.1 %collective-permute-start.1 = (bf16[256,768]{1,0:T(8,128)(2,1)S(1)}, bf16[256,768]{1,0:T(8,128)(2,1)}, u32[]{:S(2)}, u32[]{:S(2)}) collective-permute-start(bf16[256,768]{1,0:T(8,128)(2,1)S(1)} %pad_maximum_fusion.x0), channel_id=1, source_target_pairs={{0,128},{128,256},{256,384},{384,0},{1,129},{129,257},{257,385},{3... | collective-permute-start | bytes 1179656 | tf_op jit(solution)/shard_map/ppermute | solution.py:22
  25.2 4.0 %collective-permute-start.2 = (bf16[256,768]{1,0:T(8,128)(2,1)S(1)}, bf16[256,768]{1,0:T(8,128)(2,1)}, u32[]{:S(2)}, u32[]{:S(2)}) collective-permute-start(bf16[256,768]{1,0:T(8,128)(2,1)S(1)} %pad_maximum_fusion.x0), channel_id=1, source_target_pairs={{0,256},{128,384},{256,0},{384,128},{1,257},{129,385},{257,1},{385... | collective-permute-start | bytes 1179656 | tf_op jit(solution)/shard_map/ppermute | solution.py:22
  29.2 3.1 %collective-permute-start.3 = (bf16[256,768]{1,0:T(8,128)(2,1)S(1)}, bf16[256,768]{1,0:T(8,128)(2,1)}, u32[]{:S(2)}, u32[]{:S(2)}) collective-permute-start(bf16[256,768]{1,0:T(8,128)(2,1)S(1)} %pad_maximum_fusion.x0), channel_id=1, source_target_pairs={{0,384},{128,0},{256,128},{384,256},{1,385},{129,1},{257,129},{385... | collective-permute-start | bytes 1179656 | tf_op jit(solution)/shard_map/ppermute | solution.py:22
  32.3 0.3 fusion.order_ref
  32.6 7.3 %all-to-all-done = bf16[16,12,768]{2,1,0:T(8,128)(2,1)S(1)} async-done(((bf16[16,12,768]{2,1,0:T(8,128)(2,1)}), bf16[16,12,768]{2,1,0:T(8,128)(2,1)S(1)}, u32[]{:S(2)}, u32[]{:S(2)}) %all-to-all-start) | async-done | bytes 294944 | tf_op jit(solution)/shard_map/all_to_all | solution.py:28
  39.9 0.1 broadcast_in_dim.7
  40.0 1.1 broadcast_in_dim.8
  41.1 0.0 copy-done.6
  41.1 4.0 %all-to-all-start.1 = ((bf16[4,192,768]{2,1,0:T(8,128)(2,1)}), bf16[4,192,768]{2,1,0:T(8,128)(2,1)S(1)}, u32[]{:S(2)}, u32[]{:S(2)}) async-start(bf16[4,192,768]{2,1,0:T(8,128)(2,1)} %broadcast_in_dim.8), calls=%async_computation.1 | async-start | bytes 2359296 | tf_op jit(solution)/shard_map/all_to_all | solution.py:28
  45.1 0.2 collective-permute-done.1.x1
  45.3 17.4 %collective-permute-done.2.x2 = bf16[256,768]{1,0:T(8,128)(2,1)} collective-permute-done((bf16[256,768]{1,0:T(8,128)(2,1)S(1)}, bf16[256,768]{1,0:T(8,128)(2,1)}, u32[]{:S(2)}, u32[]{:S(2)}) %collective-permute-start.2) | collective-permute-done | bytes 393248 | tf_op jit(solution)/shard_map/ppermute | solution.py:22
  62.7 0.0 collective-permute-done.3.x3
  62.7 2.6 %shard_map.93.rows_ref = bf16[1024,768]{1,0:T(8,128)(2,1)} custom-call(bf16[256,768]{1,0:T(8,128)(2,1)} %copy-done.6, bf16[256,768]{1,0:T(8,128)(2,1)} %collective-permute-done.1.x1, bf16[256,768]{1,0:T(8,128)(2,1)} %collective-permute-done.2.x2, bf16[256,768]{1,0:T(8,128)(2,1)} %collective-permute-done.3.x3), custom_call_target="tpu_custom_call" | custom-call | flops 10000000000 | bytes 2097152 | tf_op jit(solution)/shard_map/pallas_call | solution.py:122
  65.3 0.0 all-to-all-done.1
  65.3 0.0 copy-start.2
  65.3 1.4 copy-done.2
  66.7 3.7 %shard_map.94 = (bf16[1024,768]{1,0:T(8,128)(2,1)}, f32[1024,768]{1,0:T(8,128)S(1)}, f32[1024,1]{1,0:T(8,128)S(1)}) custom-call(bf16[768,768]{1,0:T(8,128)(2,1)S(1)} %fusion.order_ref, bf16[768,768]{1,0:T(8,128)(2,1)S(1)} %bitcast.2, bf16[1024,768]{1,0:T(8,128)(2,1)S(1)} %copy-done.2), custom_call_target="tpu_custom_call" | custom-call | flops 2113929216 | bytes 8388608 | tf_op jit(solution)/shard_map/pallas_call | solution.py:137
  70.4 0.0 copy-start
  70.4 1.6 %copy-done = f32[1024,768]{1,0:T(8,128)} copy-done((f32[1024,768]{1,0:T(8,128)}, f32[1024,768]{1,0:T(8,128)S(1)}, u32[]{:S(2)}) %copy-start) | copy-done | bytes 3145752
  72.0 2.5 %collective-permute-start.4 = (bf16[1024,768]{1,0:T(8,128)(2,1)}, bf16[1024,768]{1,0:T(8,128)(2,1)S(1)}, u32[]{:S(2)}, u32[]{:S(2)}) collective-permute-start(bf16[1024,768]{1,0:T(8,128)(2,1)} %get-tuple-element.11.half_ref), channel_id=1, source_target_pairs={{0,64},{64,0},{1,65},{65,1},{2,66},{66,2},{3,67},{67,3},{4,68},{68... | collective-permute-start | bytes 4718600 | tf_op jit(solution)/shard_map/ppermute | solution.py:152
  75.8 0.1 pad_maximum_fusion.1.scalars
  75.9 1.9 %collective-permute-done.4.partner_ref = bf16[1024,768]{1,0:T(8,128)(2,1)S(1)} collective-permute-done((bf16[1024,768]{1,0:T(8,128)(2,1)}, bf16[1024,768]{1,0:T(8,128)(2,1)S(1)}, u32[]{:S(2)}, u32[]{:S(2)}) %collective-permute-start.4) | collective-permute-done | bytes 1572896 | tf_op jit(solution)/shard_map/ppermute | solution.py:152
  77.8 0.0 copy-start.1
  77.8 1.9 %copy-done.1 = f32[1024,768]{1,0:T(8,128)S(1)} copy-done((f32[1024,768]{1,0:T(8,128)S(1)}, f32[1024,768]{1,0:T(8,128)}, u32[]{:S(2)}) %copy-start.1) | copy-done | bytes 3145752
  79.6 0.0 copy-start.3
  79.6 1.4 copy-done.3
  81.1 7.6 %shard_map.95 = (bf16[64,12,192]{2,1,0:T(8,128)(2,1)}, f32[256,1]{1,0:T(8,128)S(1)}) custom-call(f32[2]{0:T(128)S(1)} %pad_maximum_fusion.1.scalars, s32[1]{0:T(128)} %bitcast.place, bf16[1024,768]{1,0:T(8,128)(2,1)} %get-tuple-element.11.half_ref, bf16[1024,768]{1,0:T(8,128)(2,1)S(1)} %collective-permute-done.4.partner_ref, f32[1024,768]{1,0:T(8,128)S(1)} %copy-done.1, ...), custom_call_target="tpu_custom_call" | custom-call | flops 3221225472 | bytes 8388608 | tf_op jit(solution)/shard_map/pallas_call | solution.py:154
  88.6 13.4 %all-to-all-start.2 = ((bf16[64,12,192]{2,1,0:T(8,128)(2,1)}), bf16[64,12,192]{2,1,0:T(8,128)(2,1)S(1)}, u32[]{:S(2)}, u32[]{:S(2)}) async-start(bf16[64,12,192]{2,1,0:T(8,128)(2,1)} %get-tuple-element.14), calls=%async_computation.2 | async-start | bytes 1048576 | tf_op jit(solution)/shard_map/all_to_all | solution.py:176
  102.0 0.1 slice_reduce_fusion
  102.1 2.6 %collective-permute-start.5 = (f32[128]{0:T(128)S(1)}, f32[128]{0:T(128)S(1)}, u32[]{:S(2)}, u32[]{:S(2)}) collective-permute-start(f32[128]{0:T(128)S(1)} %get-tuple-element.18), channel_id=1, source_target_pairs={{0,64},{64,0},{1,65},{65,1},{2,66},{66,2},{3,67},{67,3},{4,68},{68... | collective-permute-start | bytes 1544 | tf_op jit(solution)/shard_map/ppermute | solution.py:192
  104.7 15.9 %all-to-all-done.2.pieces_ref = bf16[64,12,192]{2,1,0:T(8,128)(2,1)S(1)} async-done(((bf16[64,12,192]{2,1,0:T(8,128)(2,1)}), bf16[64,12,192]{2,1,0:T(8,128)(2,1)S(1)}, u32[]{:S(2)}, u32[]{:S(2)}) %all-to-all-start.2) | async-done | bytes 294944 | tf_op jit(solution)/shard_map/all_to_all | solution.py:176
  120.7 0.0 copy-start.4
  120.7 0.8 copy-done.4
  121.5 1.8 %shard_map.96 = f32[8,12,192]{2,1,0:T(8,128)} custom-call(bf16[64,12,192]{2,1,0:T(8,128)(2,1)} %copy-done.4), custom_call_target="tpu_custom_call" | custom-call | tf_op jit(solution)/shard_map/pallas_call | solution.py:177
  123.3 13.8 %all-to-all-start.3 = ((f32[8,12,192]{2,1,0:T(8,128)}), f32[8,12,192]{2,1,0:T(8,128)S(1)}, u32[]{:S(2)}, u32[]{:S(2)}) async-start(f32[8,12,192]{2,1,0:T(8,128)} %shard_map.96), calls=%async_computation.3 | async-start | bytes 262144 | tf_op jit(solution)/shard_map/all_to_all | solution.py:183
  137.1 0.0 collective-permute-done.5
  137.1 0.5 broadcast_select_fusion.3
  137.6 5.3 %all-to-all-done.3.parts_ref = f32[8,12,192]{2,1,0:T(8,128)S(1)} async-done(((f32[8,12,192]{2,1,0:T(8,128)}), f32[8,12,192]{2,1,0:T(8,128)S(1)}, u32[]{:S(2)}, u32[]{:S(2)}) %all-to-all-start.3) | async-done | bytes 73760 | tf_op jit(solution)/shard_map/all_to_all | solution.py:183
  142.9 0.0 copy-start.5
  142.9 0.6 copy-done.5
  143.6 1.6 %shard_map.97 = (f32[12,768]{1,0:T(8,128)}, f32[12,768]{1,0:T(8,128)}) custom-call(f32[8,12,192]{2,1,0:T(8,128)} %copy-done.5), custom_call_target="tpu_custom_call" | custom-call | tf_op jit(solution)/shard_map/pallas_call | solution.py:184
  (2 shorter events, 0.0 us)
Async XLA Ops:
  1.7 20.3 %collective-permute-start = (bf16[128,768]{1,0:T(8,128)(2,1)S(1)}, bf16[128,768]{1,0:T(8,128)(2,1)S(1)}, u32[]{:S(2)}, u32[]{:S(2)}) collective-permute-start(bf16[128,768]{1,0:T(8,128)(2,1)S(1)} %get-tuple-element.21), channel_id=1, source_target_pairs={{0,64},{64,0},{1,65},{65,1},{2,66},{66,2},{3,67},{67,3},{4,68},{68... | collective-permute-start | bytes 589832 | tf_op jit(solution)/shard_map/ppermute | solution.py:120
  12.0 27.9 %all-to-all-start = ((bf16[16,12,768]{2,1,0:T(8,128)(2,1)}), bf16[16,12,768]{2,1,0:T(8,128)(2,1)S(1)}, u32[]{:S(2)}, u32[]{:S(2)}) async-start(bf16[16,12,768]{2,1,0:T(8,128)(2,1)} %broadcast_in_dim.6), calls=%async_computation | async-start | bytes 786432 | tf_op jit(solution)/shard_map/all_to_all | solution.py:28
  22.1 19.0 %copy-start.6 = (bf16[256,768]{1,0:T(8,128)(2,1)}, bf16[256,768]{1,0:T(8,128)(2,1)S(1)}, u32[]{:S(2)}) copy-start(bf16[256,768]{1,0:T(8,128)(2,1)S(1)} %pad_maximum_fusion.x0) | copy-start | bytes 1179652
  22.1 23.2 %collective-permute-start.1 = (bf16[256,768]{1,0:T(8,128)(2,1)S(1)}, bf16[256,768]{1,0:T(8,128)(2,1)}, u32[]{:S(2)}, u32[]{:S(2)}) collective-permute-start(bf16[256,768]{1,0:T(8,128)(2,1)S(1)} %pad_maximum_fusion.x0), channel_id=1, source_target_pairs={{0,128},{128,256},{256,384},{384,0},{1,129},{129,257},{257,385},{3... | collective-permute-start | bytes 1179656 | tf_op jit(solution)/shard_map/ppermute | solution.py:22
  25.2 37.5 %collective-permute-start.2 = (bf16[256,768]{1,0:T(8,128)(2,1)S(1)}, bf16[256,768]{1,0:T(8,128)(2,1)}, u32[]{:S(2)}, u32[]{:S(2)}) collective-permute-start(bf16[256,768]{1,0:T(8,128)(2,1)S(1)} %pad_maximum_fusion.x0), channel_id=1, source_target_pairs={{0,256},{128,384},{256,0},{384,128},{1,257},{129,385},{257,1},{385... | collective-permute-start | bytes 1179656 | tf_op jit(solution)/shard_map/ppermute | solution.py:22
  29.2 33.5 %collective-permute-start.3 = (bf16[256,768]{1,0:T(8,128)(2,1)S(1)}, bf16[256,768]{1,0:T(8,128)(2,1)}, u32[]{:S(2)}, u32[]{:S(2)}) collective-permute-start(bf16[256,768]{1,0:T(8,128)(2,1)S(1)} %pad_maximum_fusion.x0), channel_id=1, source_target_pairs={{0,384},{128,0},{256,128},{384,256},{1,385},{129,1},{257,129},{385... | collective-permute-start | bytes 1179656 | tf_op jit(solution)/shard_map/ppermute | solution.py:22
  41.1 24.2 %all-to-all-start.1 = ((bf16[4,192,768]{2,1,0:T(8,128)(2,1)}), bf16[4,192,768]{2,1,0:T(8,128)(2,1)S(1)}, u32[]{:S(2)}, u32[]{:S(2)}) async-start(bf16[4,192,768]{2,1,0:T(8,128)(2,1)} %broadcast_in_dim.8), calls=%async_computation.1 | async-start | bytes 2359296 | tf_op jit(solution)/shard_map/all_to_all | solution.py:28
  65.3 1.4 copy-start.2
  70.4 1.6 %copy-start = (f32[1024,768]{1,0:T(8,128)}, f32[1024,768]{1,0:T(8,128)S(1)}, u32[]{:S(2)}) copy-start(f32[1024,768]{1,0:T(8,128)S(1)} %get-tuple-element.12.unit_ref) | copy-start | bytes 9437188
  72.0 5.7 %collective-permute-start.4 = (bf16[1024,768]{1,0:T(8,128)(2,1)}, bf16[1024,768]{1,0:T(8,128)(2,1)S(1)}, u32[]{:S(2)}, u32[]{:S(2)}) collective-permute-start(bf16[1024,768]{1,0:T(8,128)(2,1)} %get-tuple-element.11.half_ref), channel_id=1, source_target_pairs={{0,64},{64,0},{1,65},{65,1},{2,66},{66,2},{3,67},{67,3},{4,68},{68... | collective-permute-start | bytes 4718600 | tf_op jit(solution)/shard_map/ppermute | solution.py:152
  77.8 1.9 %copy-start.1 = (f32[1024,768]{1,0:T(8,128)S(1)}, f32[1024,768]{1,0:T(8,128)}, u32[]{:S(2)}) copy-start(f32[1024,768]{1,0:T(8,128)} %copy-done) | copy-start | bytes 9437188
  79.6 1.4 copy-start.3
  88.6 32.0 %all-to-all-start.2 = ((bf16[64,12,192]{2,1,0:T(8,128)(2,1)}), bf16[64,12,192]{2,1,0:T(8,128)(2,1)S(1)}, u32[]{:S(2)}, u32[]{:S(2)}) async-start(bf16[64,12,192]{2,1,0:T(8,128)(2,1)} %get-tuple-element.14), calls=%async_computation.2 | async-start | bytes 1048576 | tf_op jit(solution)/shard_map/all_to_all | solution.py:176
  102.1 35.0 %collective-permute-start.5 = (f32[128]{0:T(128)S(1)}, f32[128]{0:T(128)S(1)}, u32[]{:S(2)}, u32[]{:S(2)}) collective-permute-start(f32[128]{0:T(128)S(1)} %get-tuple-element.18), channel_id=1, source_target_pairs={{0,64},{64,0},{1,65},{65,1},{2,66},{66,2},{3,67},{67,3},{4,68},{68... | collective-permute-start | bytes 1544 | tf_op jit(solution)/shard_map/ppermute | solution.py:192
  120.7 0.8 copy-start.4
  123.3 19.6 %all-to-all-start.3 = ((f32[8,12,192]{2,1,0:T(8,128)}), f32[8,12,192]{2,1,0:T(8,128)S(1)}, u32[]{:S(2)}, u32[]{:S(2)}) async-start(f32[8,12,192]{2,1,0:T(8,128)} %shard_map.96), calls=%async_computation.3 | async-start | bytes 262144 | tf_op jit(solution)/shard_map/all_to_all | solution.py:183
  142.9 0.6 copy-start.5

commit v6 on v2

--- a/solution.py
+++ b/solution.py
@@ -9,6 +9,7 @@
 
 EVERY = ("zlo", "core", "y", "zhi", "x")
 GRP = ("y", "zhi", "x")
+ARRIVED = 3 * 10**9
 SWAP = [(0, 1), (1, 0)]
 F32, BF16 = jnp.float32, jnp.bfloat16
 VMEM = pl.BlockSpec(memory_space=pltpu.VMEM)
@@ -28,20 +29,19 @@
     return lax.all_to_all(copies, axis, split_axis=0, concat_axis=0)
 
 
-def copies_kernel(own_ref, other_ref, up_ref, down_ref, out_ref):
+def copies_kernel(own_ref, other_ref, out_ref):
     share = own_ref.shape[0]
     for k in range(out_ref.shape[0]):
         out_ref[k, :share] = own_ref[...]
         out_ref[k, share:] = other_ref[...]
 
 
-def spread_kernel(near_ref, up_ref, down_ref, out_ref):
-    for k in range(out_ref.shape[0]):
-        out_ref[k] = near_ref[...]
+def arrived_kernel(up_ref, down_ref, out_ref):
+    out_ref[...] = jnp.zeros_like(out_ref)
 
 
 def embed_kernel(
-    place, order_ref, gathered_ref, x0, up1, up2, up3, down1, down2, down3,
+    place, arrived_ref, order_ref, gathered_ref, x0, up1, up2, up3, down1, down2, down3,
     half_ref, unit_ref, radius_ref, rows_ref, mapping,
 ):
     mapping[...] = jnp.dot(
@@ -121,24 +121,24 @@
     for _ in range(1, chips):
         up.append(passed_on(up[-1], "zlo", 1))
         down.append(passed_on(down[-1], "zlo", -1))
+    arrived = pl.pallas_call(
+        arrived_kernel,
+        out_shape=jax.ShapeDtypeStruct((8, 128), F32),
+        in_specs=[ANY] * 2,
+        out_specs=VMEM,
+        cost_estimate=pl.CostEstimate(flops=ARRIVED, bytes_accessed=2**12, transcendentals=0),
+    )(up[-1], down[-1])
     at_chip = lax.axis_index("zlo").astype(jnp.int32).reshape(1)
     copies = pl.pallas_call(
         copies_kernel,
         out_shape=jax.ShapeDtypeStruct((n_y, n_zhi * share, embed), BF16),
-        in_specs=[VMEM, VMEM, ANY, ANY],
+        in_specs=[VMEM] * 2,
         out_specs=VMEM,
         cost_estimate=pl.CostEstimate(flops=0, bytes_accessed=2**19, transcendentals=0),
-    )(piece, other, up[1], down[1])
+    )(piece, other)
     near = lax.all_to_all(copies, "y", split_axis=0, concat_axis=0)
     near = near.reshape(n_y * n_zhi * share, embed)
-    copies = pl.pallas_call(
-        spread_kernel,
-        out_shape=jax.ShapeDtypeStruct((n_x,) + near.shape, BF16),
-        in_specs=[VMEM, ANY, ANY],
-        out_specs=VMEM,
-        cost_estimate=pl.CostEstimate(flops=0, bytes_accessed=2**21, transcendentals=0),
-    )(near, up[2], down[2])
-    gathered = lax.all_to_all(copies, "x", split_axis=0, concat_axis=0).reshape(width, embed)
+    gathered = spread(near, "x").reshape(width, embed)
     at = jnp.arange(width, dtype=jnp.int32)
     owner, row = at // share, at % share
     at_half = (owner // n_x) % n_zhi
@@ -154,14 +154,14 @@
             jax.ShapeDtypeStruct((rows, 1), F32),
             jax.ShapeDtypeStruct((rows, width), BF16),
         ),
-        in_specs=[SMEM] + [VMEM] * 9,
+        in_specs=[SMEM, ANY] + [VMEM] * 9,
         out_specs=(VMEM,) * 4,
         scratch_shapes=[pltpu.VMEM((width, embed), BF16)],
         compiler_params=PARAMS,
         cost_estimate=pl.CostEstimate(
             flops=2 * (rows + width) * width * embed, bytes_accessed=8 * 2**20, transcendentals=0
         ),
-    )(at_chip, order, gathered, *up, *down[1:])
+    )(at_chip, arrived, order, gathered, *up, *down[1:])
     partner = lax.ppermute(half, "core", SWAP)
     columns = embed // chips
     local, norms = pl.pallas_call(

time: 138 us -> 129 us (0.935)
  waiting for transfers between devices: 46.2 us -> 40.3 us
  starting transfers between devices: 68 us -> 65.9 us
  Pallas kernels: 13.4 us -> 11.8 us
    ppermute x6, waiting for transfers between devices: 16.8 us -> 7.43 us  [passed_on(): lax.ppermute(value, axis, [(i, i + by) for i in range(count) if 0 <= i +...]
    all_to_all x1, starting transfers between devices: 10.6 us -> 6.38 us  [on_device(): lax.all_to_all(local.reshape(width // share, share, columns), GRP, split_...]
    all_to_all x1 -> x0, starting transfers between devices: 4.14 us -> none  [on_device(): lax.all_to_all(copies, 'x', split_axis=0, concat_axis=0)]
    all_to_all x1 -> x2, starting transfers between devices: 6.99 us -> 10.9 us  [spread(): return lax.all_to_all(copies, axis, split_axis=0, concat_axis=0)]
    all_to_all x1, waiting for transfers between devices: 0.01 us -> 3.17 us  [on_device(): near = lax.all_to_all(copies, 'y', split_axis=0, concat_axis=0)]
    ppermute x6, starting transfers between devices: 14.5 us -> 16.1 us  [passed_on(): lax.ppermute(value, axis, [(i, i + by) for i in range(count) if 0 <= i +...]
    pallas_call x1, Pallas kernels: 2.09 us -> 0.59 us  [on_device(): pl.pallas_call(arrived_kernel, out_shape=jax.ShapeDtypeStruct((8, 128), F...]
    all_to_all x1 -> x2, waiting for transfers between devices: 5.32 us -> 5.29 us  [spread(): return lax.all_to_all(copies, axis, split_axis=0, concat_axis=0)]
  transfers between devices with their start and end apart: 14 -> 14, of which waited for: 9 -> 8; matrix products, arithmetic and copies ran while one was open for 1% -> 2% of each run, Pallas kernels for 0% -> 2%
where the time goes in v6:
time: 129 us; the launch traced here: 128 us
  starting transfers between devices  65.9 us (51%)
  waiting for transfers between devices  40.3 us (31%)
  Pallas kernels  11.8 us (9%)
  local copies, waits for them, and re-layouts  5.89 us (5%)
  between operations  2.11 us (2%)
  other arithmetic  2.1 us (2%)
    ppermute x6, starting transfers between devices, passed_on(): lax.ppermute(value, axis, [(i, i + by) for i in range(count) if 0 <= i +...  16.1 us
    all_to_all x1, waiting for transfers between devices, on_device(): lax.all_to_all(local.reshape(width // share, share, columns), GRP, split_...  15.9 us
    all_to_all x2, starting transfers between devices, spread(): return lax.all_to_all(copies, axis, split_axis=0, concat_axis=0)  10.9 us
    ppermute x1, starting transfers between devices, on_device(): chunk = jnp.concatenate([mine, lax.ppermute(sent, 'core', SWAP)], axis=0)  8.79 us
    ppermute x6, waiting for transfers between devices, passed_on(): lax.ppermute(value, axis, [(i, i + by) for i in range(count) if 0 <= i +...  7.43 us
    ppermute x1, starting transfers between devices, on_device(): partner = lax.ppermute(half, 'core', SWAP)  7.32 us
    ppermute x1, starting transfers between devices, on_device(): other = lax.ppermute(piece, 'zhi', SWAP)  7.07 us
    all_to_all x1, starting transfers between devices, on_device(): near = lax.all_to_all(copies, 'y', split_axis=0, concat_axis=0)  6.82 us
  transfers between devices with their start and end apart: 14, of which 8 were waited for; matrix products, arithmetic and copies ran while one was open for 2% of the time, Pallas kernels for 2%

profile of v6, /device:TPU:1, one launch (start us, length us, event | category | flops | bytes accessed | tf_op | source)
XLA Modules:
  0.0 128.1 jit_solution(15609509717150095231)
XLA Ops:
  0.6 0.0 copy-start.2
  0.6 0.0 copy-start.3
  0.7 1.1 broadcast_select_fusion.1
  1.7 8.8 %collective-permute-start = (bf16[128,768]{1,0:T(8,128)(2,1)S(1)}, bf16[128,768]{1,0:T(8,128)(2,1)S(1)}, u32[]{:S(2)}, u32[]{:S(2)}) collective-permute-start(bf16[128,768]{1,0:T(8,128)(2,1)S(1)} %get-tuple-element.21), channel_id=1, source_target_pairs={{0,64},{64,0},{1,65},{65,1},{2,66},{66,2},{3,67},{67,3},{4,68},{68... | collective-permute-start | bytes 589832 | tf_op jit(solution)/shard_map/ppermute | solution.py:119
  10.5 1.0 collective-permute-done
  11.6 1.3 %collective-permute-start.1 = (bf16[256,768]{1,0:T(8,128)(2,1)S(1)}, bf16[256,768]{1,0:T(8,128)(2,1)S(1)}, u32[]{:S(2)}, u32[]{:S(2)}) collective-permute-start(bf16[256,768]{1,0:T(8,128)(2,1)S(1)} %pad_maximum_fusion.x0), channel_id=1, source_target_pairs={{0,128},{128,256},{256,384},{1,129},{129,257},{257,385},{2,130},{1... | collective-permute-start | bytes 1179656 | tf_op jit(solution)/shard_map/ppermute | solution.py:23
  12.9 1.3 %collective-permute-start.4 = (bf16[256,768]{1,0:T(8,128)(2,1)S(1)}, bf16[256,768]{1,0:T(8,128)(2,1)S(1)}, u32[]{:S(2)}, u32[]{:S(2)}) collective-permute-start(bf16[256,768]{1,0:T(8,128)(2,1)S(1)} %pad_maximum_fusion.x0), channel_id=1, source_target_pairs={{128,0},{256,128},{384,256},{129,1},{257,129},{385,257},{130,2},{2... | collective-permute-start | bytes 1179656 | tf_op jit(solution)/shard_map/ppermute | solution.py:23
  14.2 0.0 copy-done.2
  14.2 0.0 copy-done.3
  14.2 0.0 copy-start.1
  14.3 7.1 %collective-permute-start.7 = (bf16[12,768]{1,0:T(8,128)(2,1)S(1)}, bf16[12,768]{1,0:T(8,128)(2,1)S(1)}, u32[]{:S(2)}, u32[]{:S(2)}) collective-permute-start(bf16[12,768]{1,0:T(8,128)(2,1)S(1)} %broadcast_select_fusion.2.own_ref), channel_id=1, source_target_pairs={{0,4},{4,0},{1,5},{5,1},{2,6},{6,2},{3,7},{7,3},{8,12},{12,8},{9,1... | collective-permute-start | bytes 55304 | tf_op jit(solution)/shard_map/ppermute | solution.py:116
  21.3 5.8 %collective-permute-done.7.other_ref = bf16[12,768]{1,0:T(8,128)(2,1)S(1)} collective-permute-done((bf16[12,768]{1,0:T(8,128)(2,1)S(1)}, bf16[12,768]{1,0:T(8,128)(2,1)S(1)}, u32[]{:S(2)}, u32[]{:S(2)}) %collective-permute-start.7) | collective-permute-done | bytes 18464 | tf_op jit(solution)/shard_map/ppermute | solution.py:116
  27.1 0.0 copy-done.1
  27.1 0.0 copy-start.4
  27.1 0.6 copy-done.4
  27.7 1.5 %shard_map.94 = bf16[8,24,768]{2,1,0:T(8,128)(2,1)} custom-call(bf16[12,768]{1,0:T(8,128)(2,1)} %copy-done.1, bf16[12,768]{1,0:T(8,128)(2,1)} %copy-done.4), custom_call_target="tpu_custom_call" | custom-call | bytes 524288 | tf_op jit(solution)/shard_map/pallas_call | solution.py:132
  29.2 6.8 %all-to-all-start = ((bf16[8,24,768]{2,1,0:T(8,128)(2,1)}), bf16[8,24,768]{2,1,0:T(8,128)(2,1)S(1)}, u32[]{:S(2)}, u32[]{:S(2)}) async-start(bf16[8,24,768]{2,1,0:T(8,128)(2,1)} %shard_map.94), calls=%async_computation | async-start | bytes 589824 | tf_op jit(solution)/shard_map/all_to_all | solution.py:139
  36.1 0.0 collective-permute-done.1.up1
  36.1 5.8 %collective-permute-start.2 = (bf16[256,768]{1,0:T(8,128)(2,1)S(1)}, bf16[256,768]{1,0:T(8,128)(2,1)}, u32[]{:S(2)}, u32[]{:S(2)}) collective-permute-start(bf16[256,768]{1,0:T(8,128)(2,1)S(1)} %collective-permute-done.1.up1), channel_id=1, source_target_pairs={{0,128},{128,256},{256,384},{1,129},{129,257},{257,385},{2,130},{1... | collective-permute-start | bytes 1179656 | tf_op jit(solution)/shard_map/ppermute | solution.py:23
  41.8 0.0 collective-permute-done.4.down1
  41.8 1.3 %collective-permute-start.5 = (bf16[256,768]{1,0:T(8,128)(2,1)S(1)}, bf16[256,768]{1,0:T(8,128)(2,1)}, u32[]{:S(2)}, u32[]{:S(2)}) collective-permute-start(bf16[256,768]{1,0:T(8,128)(2,1)S(1)} %collective-permute-done.4.down1), channel_id=1, source_target_pairs={{128,0},{256,128},{384,256},{129,1},{257,129},{385,257},{130,2},{2... | collective-permute-start | bytes 1179656 | tf_op jit(solution)/shard_map/ppermute | solution.py:23
  43.1 3.2 %all-to-all-done = bf16[8,24,768]{2,1,0:T(8,128)(2,1)S(1)} async-done(((bf16[8,24,768]{2,1,0:T(8,128)(2,1)}), bf16[8,24,768]{2,1,0:T(8,128)(2,1)S(1)}, u32[]{:S(2)}, u32[]{:S(2)}) %all-to-all-start) | async-done | bytes 294944 | tf_op jit(solution)/shard_map/all_to_all | solution.py:139
  46.3 1.1 broadcast_in_dim.7
  47.4 4.0 %all-to-all-start.1 = ((bf16[4,192,768]{2,1,0:T(8,128)(2,1)}), bf16[4,192,768]{2,1,0:T(8,128)(2,1)S(1)}, u32[]{:S(2)}, u32[]{:S(2)}) async-start(bf16[4,192,768]{2,1,0:T(8,128)(2,1)} %broadcast_in_dim.7), calls=%async_computation.1 | async-start | bytes 2359296 | tf_op jit(solution)/shard_map/all_to_all | solution.py:29
  51.4 0.0 collective-permute-done.2.up2
  51.4 5.1 %collective-permute-start.3 = (bf16[256,768]{1,0:T(8,128)(2,1)}, bf16[256,768]{1,0:T(8,128)(2,1)}, u32[]{:S(2)}, u32[]{:S(2)}) collective-permute-start(bf16[256,768]{1,0:T(8,128)(2,1)} %collective-permute-done.2.up2), channel_id=1, source_target_pairs={{0,128},{128,256},{256,384},{1,129},{129,257},{257,385},{2,130},{1... | collective-permute-start | bytes 1179656 | tf_op jit(solution)/shard_map/ppermute | solution.py:23
  56.6 0.0 collective-permute-done.5.down2
  56.6 1.3 %collective-permute-start.6 = (bf16[256,768]{1,0:T(8,128)(2,1)}, bf16[256,768]{1,0:T(8,128)(2,1)}, u32[]{:S(2)}, u32[]{:S(2)}) collective-permute-start(bf16[256,768]{1,0:T(8,128)(2,1)} %collective-permute-done.5.down2), channel_id=1, source_target_pairs={{128,0},{256,128},{384,256},{129,1},{257,129},{385,257},{130,2},{2... | collective-permute-start | bytes 1179656 | tf_op jit(solution)/shard_map/ppermute | solution.py:23
  57.9 0.3 fusion.order_ref
  58.1 2.7 %collective-permute-done.3.up_ref.up3 = bf16[256,768]{1,0:T(8,128)(2,1)} collective-permute-done((bf16[256,768]{1,0:T(8,128)(2,1)}, bf16[256,768]{1,0:T(8,128)(2,1)}, u32[]{:S(2)}, u32[]{:S(2)}) %collective-permute-start.3) | collective-permute-done | bytes 393248 | tf_op jit(solution)/shard_map/ppermute | solution.py:23
  60.8 4.8 %collective-permute-done.6.down_ref.down3 = bf16[256,768]{1,0:T(8,128)(2,1)} collective-permute-done((bf16[256,768]{1,0:T(8,128)(2,1)}, bf16[256,768]{1,0:T(8,128)(2,1)}, u32[]{:S(2)}, u32[]{:S(2)}) %collective-permute-start.6) | collective-permute-done | bytes 393248 | tf_op jit(solution)/shard_map/ppermute | solution.py:23
  65.6 0.6 shard_map.93.arrived_ref
  66.2 0.0 all-to-all-done.1
  66.2 0.0 copy-start
  66.2 0.7 copy-done
  66.9 3.9 %shard_map.95 = (bf16[1024,768]{1,0:T(8,128)(2,1)S(1)}, f32[1024,768]{1,0:T(8,128)S(1)}, f32[1024,1]{1,0:T(8,128)S(1)}, bf16[1024,768]{1,0:T(8,128)(2,1)S(1)}) custom-call(s32[1]{0:T(128)} %bitcast.place, f32[8,128]{1,0:T(8,128)S(1)} %copy-done, bf16[768,768]{1,0:T(8,128)(2,1)S(1)} %fusion.order_ref, bf16[768,768]{1,0:T(8,128)(2,1)S(1)} %bitcast.7, ...), custom_call_target="tpu_custom_call" | custom-call | flops 2113929216 | bytes 8388608 | tf_op jit(solution)/shard_map/pallas_call | solution.py:149
  70.8 7.3 %collective-permute-start.8 = (bf16[1024,768]{1,0:T(8,128)(2,1)S(1)}, bf16[1024,768]{1,0:T(8,128)(2,1)S(1)}, u32[]{:S(2)}, u32[]{:S(2)}) collective-permute-start(bf16[1024,768]{1,0:T(8,128)(2,1)S(1)} %get-tuple-element.10.half_ref), channel_id=1, source_target_pairs={{0,64},{64,0},{1,65},{65,1},{2,66},{66,2},{3,67},{67,3},{4,68},{68... | collective-permute-start | bytes 4718600 | tf_op jit(solution)/shard_map/ppermute | solution.py:165
  79.4 0.1 pad_maximum_fusion.1.scalars
  79.5 1.6 %collective-permute-done.8.partner_ref = bf16[1024,768]{1,0:T(8,128)(2,1)S(1)} collective-permute-done((bf16[1024,768]{1,0:T(8,128)(2,1)S(1)}, bf16[1024,768]{1,0:T(8,128)(2,1)S(1)}, u32[]{:S(2)}, u32[]{:S(2)}) %collective-permute-start.8) | collective-permute-done | bytes 1572896 | tf_op jit(solution)/shard_map/ppermute | solution.py:165
  81.1 5.9 %shard_map.96 = (bf16[768,192]{1,0:T(8,128)(2,1)S(1)}, f32[256,1]{1,0:T(8,128)S(1)}) custom-call(f32[2]{0:T(128)S(1)} %pad_maximum_fusion.1.scalars, s32[1]{0:T(128)} %bitcast.place, bf16[1024,768]{1,0:T(8,128)(2,1)S(1)} %get-tuple-element.10.half_ref, bf16[1024,768]{1,0:T(8,128)(2,1)S(1)} %collective-permute-done.8.partner_ref, ...), custom_call_target="tpu_custom_call" | custom-call | flops 3221225472 | bytes 8388608 | tf_op jit(solution)/shard_map/pallas_call | solution.py:167
  87.0 0.9 reshape.104
  87.9 6.4 %all-to-all-start.2 = ((bf16[64,12,192]{2,1,0:T(8,128)(2,1)}), bf16[64,12,192]{2,1,0:T(8,128)(2,1)S(1)}, u32[]{:S(2)}, u32[]{:S(2)}) async-start(bf16[64,12,192]{2,1,0:T(8,128)(2,1)} %reshape.104), calls=%async_computation.2 | async-start | bytes 1048576 | tf_op jit(solution)/shard_map/all_to_all | solution.py:189
  94.3 0.1 slice_reduce_fusion
  94.4 2.6 %collective-permute-start.9 = (f32[128]{0:T(128)S(1)}, f32[128]{0:T(128)S(1)}, u32[]{:S(2)}, u32[]{:S(2)}) collective-permute-start(f32[128]{0:T(128)S(1)} %get-tuple-element.16), channel_id=1, source_target_pairs={{0,64},{64,0},{1,65},{65,1},{2,66},{66,2},{3,67},{67,3},{4,68},{68... | collective-permute-start | bytes 1544 | tf_op jit(solution)/shard_map/ppermute | solution.py:197
  97.0 15.9 %all-to-all-done.2 = bf16[64,12,192]{2,1,0:T(8,128)(2,1)S(1)} async-done(((bf16[64,12,192]{2,1,0:T(8,128)(2,1)}), bf16[64,12,192]{2,1,0:T(8,128)(2,1)S(1)}, u32[]{:S(2)}, u32[]{:S(2)}) %all-to-all-start.2) | async-done | bytes 294944 | tf_op jit(solution)/shard_map/all_to_all | solution.py:189
  112.8 0.1 convert_reduce_fusion
  113.0 0.7 broadcast_in_dim.8
  113.6 6.9 %all-to-all-start.3 = ((f32[8,12,192]{2,1,0:T(8,128)}), f32[8,12,192]{2,1,0:T(8,128)S(1)}, u32[]{:S(2)}, u32[]{:S(2)}) async-start(f32[8,12,192]{2,1,0:T(8,128)} %broadcast_in_dim.8), calls=%async_computation.3 | async-start | bytes 262144 | tf_op jit(solution)/shard_map/all_to_all | solution.py:29
  120.5 0.0 collective-permute-done.9
  120.5 0.5 broadcast_select_fusion.3
  121.0 5.3 %all-to-all-done.3 = f32[8,12,192]{2,1,0:T(8,128)S(1)} async-done(((f32[8,12,192]{2,1,0:T(8,128)}), f32[8,12,192]{2,1,0:T(8,128)S(1)}, u32[]{:S(2)}, u32[]{:S(2)}) %all-to-all-start.3) | async-done | bytes 73760 | tf_op jit(solution)/shard_map/all_to_all | solution.py:29
  126.3 0.1 copy.13
  126.4 0.3 slice_reduce_fusion.2
  126.7 0.7 squeeze.6
  127.4 0.7 squeeze.7
  (3 shorter events, 0.1 us)
Async XLA Ops:
  0.6 13.6 %copy-start.2 = (bf16[12,768]{1,0:T(8,128)(2,1)S(1)}, bf16[12,768]{1,0:T(8,128)(2,1)}, u32[]{:S(2)}) copy-start(bf16[12,768]{1,0:T(8,128)(2,1)} %param.8) | copy-start | bytes 55300
  0.6 13.6 %copy-start.3 = (bf16[12,768]{1,0:T(8,128)(2,1)S(1)}, bf16[12,768]{1,0:T(8,128)(2,1)}, u32[]{:S(2)}) copy-start(bf16[12,768]{1,0:T(8,128)(2,1)} %param.9) | copy-start | bytes 55300
  1.7 9.8 %collective-permute-start = (bf16[128,768]{1,0:T(8,128)(2,1)S(1)}, bf16[128,768]{1,0:T(8,128)(2,1)S(1)}, u32[]{:S(2)}, u32[]{:S(2)}) collective-permute-start(bf16[128,768]{1,0:T(8,128)(2,1)S(1)} %get-tuple-element.21), channel_id=1, source_target_pairs={{0,64},{64,0},{1,65},{65,1},{2,66},{66,2},{3,67},{67,3},{4,68},{68... | collective-permute-start | bytes 589832 | tf_op jit(solution)/shard_map/ppermute | solution.py:119
  11.6 24.5 %collective-permute-start.1 = (bf16[256,768]{1,0:T(8,128)(2,1)S(1)}, bf16[256,768]{1,0:T(8,128)(2,1)S(1)}, u32[]{:S(2)}, u32[]{:S(2)}) collective-permute-start(bf16[256,768]{1,0:T(8,128)(2,1)S(1)} %pad_maximum_fusion.x0), channel_id=1, source_target_pairs={{0,128},{128,256},{256,384},{1,129},{129,257},{257,385},{2,130},{1... | collective-permute-start | bytes 1179656 | tf_op jit(solution)/shard_map/ppermute | solution.py:23
  12.9 28.9 %collective-permute-start.4 = (bf16[256,768]{1,0:T(8,128)(2,1)S(1)}, bf16[256,768]{1,0:T(8,128)(2,1)S(1)}, u32[]{:S(2)}, u32[]{:S(2)}) collective-permute-start(bf16[256,768]{1,0:T(8,128)(2,1)S(1)} %pad_maximum_fusion.x0), channel_id=1, source_target_pairs={{128,0},{256,128},{384,256},{129,1},{257,129},{385,257},{130,2},{2... | collective-permute-start | bytes 1179656 | tf_op jit(solution)/shard_map/ppermute | solution.py:23
  14.2 12.9 %copy-start.1 = (bf16[12,768]{1,0:T(8,128)(2,1)}, bf16[12,768]{1,0:T(8,128)(2,1)S(1)}, u32[]{:S(2)}) copy-start(bf16[12,768]{1,0:T(8,128)(2,1)S(1)} %broadcast_select_fusion.2.own_ref) | copy-start | bytes 55300
  14.3 12.9 %collective-permute-start.7 = (bf16[12,768]{1,0:T(8,128)(2,1)S(1)}, bf16[12,768]{1,0:T(8,128)(2,1)S(1)}, u32[]{:S(2)}, u32[]{:S(2)}) collective-permute-start(bf16[12,768]{1,0:T(8,128)(2,1)S(1)} %broadcast_select_fusion.2.own_ref), channel_id=1, source_target_pairs={{0,4},{4,0},{1,5},{5,1},{2,6},{6,2},{3,7},{7,3},{8,12},{12,8},{9,1... | collective-permute-start | bytes 55304 | tf_op jit(solution)/shard_map/ppermute | solution.py:116
  27.1 0.6 copy-start.4
  29.2 17.0 %all-to-all-start = ((bf16[8,24,768]{2,1,0:T(8,128)(2,1)}), bf16[8,24,768]{2,1,0:T(8,128)(2,1)S(1)}, u32[]{:S(2)}, u32[]{:S(2)}) async-start(bf16[8,24,768]{2,1,0:T(8,128)(2,1)} %shard_map.94), calls=%async_computation | async-start | bytes 589824 | tf_op jit(solution)/shard_map/all_to_all | solution.py:139
  36.1 15.4 %collective-permute-start.2 = (bf16[256,768]{1,0:T(8,128)(2,1)S(1)}, bf16[256,768]{1,0:T(8,128)(2,1)}, u32[]{:S(2)}, u32[]{:S(2)}) collective-permute-start(bf16[256,768]{1,0:T(8,128)(2,1)S(1)} %collective-permute-done.1.up1), channel_id=1, source_target_pairs={{0,128},{128,256},{256,384},{1,129},{129,257},{257,385},{2,130},{1... | collective-permute-start | bytes 1179656 | tf_op jit(solution)/shard_map/ppermute | solution.py:23
  41.8 14.7 %collective-permute-start.5 = (bf16[256,768]{1,0:T(8,128)(2,1)S(1)}, bf16[256,768]{1,0:T(8,128)(2,1)}, u32[]{:S(2)}, u32[]{:S(2)}) collective-permute-start(bf16[256,768]{1,0:T(8,128)(2,1)S(1)} %collective-permute-done.4.down1), channel_id=1, source_target_pairs={{128,0},{256,128},{384,256},{129,1},{257,129},{385,257},{130,2},{2... | collective-permute-start | bytes 1179656 | tf_op jit(solution)/shard_map/ppermute | solution.py:23
  47.4 18.8 %all-to-all-start.1 = ((bf16[4,192,768]{2,1,0:T(8,128)(2,1)}), bf16[4,192,768]{2,1,0:T(8,128)(2,1)S(1)}, u32[]{:S(2)}, u32[]{:S(2)}) async-start(bf16[4,192,768]{2,1,0:T(8,128)(2,1)} %broadcast_in_dim.7), calls=%async_computation.1 | async-start | bytes 2359296 | tf_op jit(solution)/shard_map/all_to_all | solution.py:29
  51.4 9.4 %collective-permute-start.3 = (bf16[256,768]{1,0:T(8,128)(2,1)}, bf16[256,768]{1,0:T(8,128)(2,1)}, u32[]{:S(2)}, u32[]{:S(2)}) collective-permute-start(bf16[256,768]{1,0:T(8,128)(2,1)} %collective-permute-done.2.up2), channel_id=1, source_target_pairs={{0,128},{128,256},{256,384},{1,129},{129,257},{257,385},{2,130},{1... | collective-permute-start | bytes 1179656 | tf_op jit(solution)/shard_map/ppermute | solution.py:23
  56.6 9.0 %collective-permute-start.6 = (bf16[256,768]{1,0:T(8,128)(2,1)}, bf16[256,768]{1,0:T(8,128)(2,1)}, u32[]{:S(2)}, u32[]{:S(2)}) collective-permute-start(bf16[256,768]{1,0:T(8,128)(2,1)} %collective-permute-done.5.down2), channel_id=1, source_target_pairs={{128,0},{256,128},{384,256},{129,1},{257,129},{385,257},{130,2},{2... | collective-permute-start | bytes 1179656 | tf_op jit(solution)/shard_map/ppermute | solution.py:23
  66.2 0.7 copy-start
  70.8 10.3 %collective-permute-start.8 = (bf16[1024,768]{1,0:T(8,128)(2,1)S(1)}, bf16[1024,768]{1,0:T(8,128)(2,1)S(1)}, u32[]{:S(2)}, u32[]{:S(2)}) collective-permute-start(bf16[1024,768]{1,0:T(8,128)(2,1)S(1)} %get-tuple-element.10.half_ref), channel_id=1, source_target_pairs={{0,64},{64,0},{1,65},{65,1},{2,66},{66,2},{3,67},{67,3},{4,68},{68... | collective-permute-start | bytes 4718600 | tf_op jit(solution)/shard_map/ppermute | solution.py:165
  87.9 24.9 %all-to-all-start.2 = ((bf16[64,12,192]{2,1,0:T(8,128)(2,1)}), bf16[64,12,192]{2,1,0:T(8,128)(2,1)S(1)}, u32[]{:S(2)}, u32[]{:S(2)}) async-start(bf16[64,12,192]{2,1,0:T(8,128)(2,1)} %reshape.104), calls=%async_computation.2 | async-start | bytes 1048576 | tf_op jit(solution)/shard_map/all_to_all | solution.py:189
  94.4 26.1 %collective-permute-start.9 = (f32[128]{0:T(128)S(1)}, f32[128]{0:T(128)S(1)}, u32[]{:S(2)}, u32[]{:S(2)}) collective-permute-start(f32[128]{0:T(128)S(1)} %get-tuple-element.16), channel_id=1, source_target_pairs={{0,64},{64,0},{1,65},{65,1},{2,66},{66,2},{3,67},{67,3},{4,68},{68... | collective-permute-start | bytes 1544 | tf_op jit(solution)/shard_map/ppermute | solution.py:197
  113.6 12.7 %all-to-all-start.3 = ((f32[8,12,192]{2,1,0:T(8,128)}), f32[8,12,192]{2,1,0:T(8,128)S(1)}, u32[]{:S(2)}, u32[]{:S(2)}) async-start(f32[8,12,192]{2,1,0:T(8,128)} %broadcast_in_dim.8), calls=%async_computation.3 | async-start | bytes 262144 | tf_op jit(solution)/shard_map/all_to_all | solution.py:29

commit v7 on v6

--- a/solution.py
+++ b/solution.py
@@ -9,7 +9,7 @@
 
 EVERY = ("zlo", "core", "y", "zhi", "x")
 GRP = ("y", "zhi", "x")
-ARRIVED = 3 * 10**9
+ARRIVED = 8 * 10**9
 SWAP = [(0, 1), (1, 0)]
 F32, BF16 = jnp.float32, jnp.bfloat16
 VMEM = pl.BlockSpec(memory_space=pltpu.VMEM)
@@ -36,7 +36,7 @@
         out_ref[k, share:] = other_ref[...]
 
 
-def arrived_kernel(up_ref, down_ref, out_ref):
+def arrived_kernel(up2_ref, up3_ref, down2_ref, down3_ref, out_ref):
     out_ref[...] = jnp.zeros_like(out_ref)
 
 
@@ -117,17 +117,16 @@
     mine = jnp.where(first, picture_inputs, caption_inputs)
     sent = jnp.where(first, caption_inputs, picture_inputs)
     chunk = jnp.concatenate([mine, lax.ppermute(sent, "core", SWAP)], axis=0)
-    up, down = [chunk], [chunk]
-    for _ in range(1, chips):
-        up.append(passed_on(up[-1], "zlo", 1))
-        down.append(passed_on(down[-1], "zlo", -1))
+    up1, down1 = passed_on(chunk, "zlo", 1), passed_on(chunk, "zlo", -1)
+    up = [chunk, up1] + [passed_on(up1, "zlo", k) for k in range(1, chips - 1)]
+    down = [chunk, down1] + [passed_on(down1, "zlo", -k) for k in range(1, chips - 1)]
     arrived = pl.pallas_call(
         arrived_kernel,
         out_shape=jax.ShapeDtypeStruct((8, 128), F32),
-        in_specs=[ANY] * 2,
+        in_specs=[ANY] * 4,
         out_specs=VMEM,
         cost_estimate=pl.CostEstimate(flops=ARRIVED, bytes_accessed=2**12, transcendentals=0),
-    )(up[-1], down[-1])
+    )(*up[2:], *down[2:])
     at_chip = lax.axis_index("zlo").astype(jnp.int32).reshape(1)
     copies = pl.pallas_call(
         copies_kernel,

time: 129 us -> 131 us (1.016)
    ppermute x6, waiting for transfers between devices: 7.43 us -> 19.1 us  [passed_on(): lax.ppermute(value, axis, [(i, i + by) for i in range(count) if 0 <= i +...]
    ppermute x1, waiting for transfers between devices: 5.8 us -> 0.01 us  [on_device(): other = lax.ppermute(piece, 'zhi', SWAP)]
    all_to_all x1, starting transfers between devices: 6.38 us -> 11 us  [on_device(): lax.all_to_all(local.reshape(width // share, share, columns), GRP, split_...]
    all_to_all x1, waiting for transfers between devices: 3.17 us -> 0.01 us  [on_device(): near = lax.all_to_all(copies, 'y', split_axis=0, concat_axis=0)]
    ppermute x1, starting transfers between devices: 7.32 us -> 4.25 us  [on_device(): partner = lax.ppermute(half, 'core', SWAP)]
    ppermute x1, starting transfers between devices: 7.07 us -> 5.25 us  [on_device(): other = lax.ppermute(piece, 'zhi', SWAP)]
  transfers between devices with their start and end apart: 14 -> 14, of which waited for: 8 -> 5; matrix products, arithmetic and copies ran while one was open for 2% -> 3% of each run, Pallas kernels for 2% -> 2%
where the time goes in v7:
time: 131 us; the launch traced here: 130 us
  starting transfers between devices  65.4 us (50%)
  waiting for transfers between devices  41.6 us (32%)
  Pallas kernels  11.9 us (9%)
  local copies, waits for them, and re-layouts  5.88 us (4%)
  other arithmetic  2.85 us (2%)
  between operations  2.12 us (2%)
    ppermute x6, waiting for transfers between devices, passed_on(): lax.ppermute(value, axis, [(i, i + by) for i in range(count) if 0 <= i +...  19.1 us
    ppermute x6, starting transfers between devices, passed_on(): lax.ppermute(value, axis, [(i, i + by) for i in range(count) if 0 <= i +...  15.7 us
    all_to_all x1, waiting for transfers between devices, on_device(): lax.all_to_all(local.reshape(width // share, share, columns), GRP, split_...  15.5 us
    all_to_all x2, starting transfers between devices, spread(): return lax.all_to_all(copies, axis, split_axis=0, concat_axis=0)  11 us
    all_to_all x1, starting transfers between devices, on_device(): lax.all_to_all(local.reshape(width // share, share, columns), GRP, split_...  11 us
    ppermute x1, starting transfers between devices, on_device(): chunk = jnp.concatenate([mine, lax.ppermute(sent, 'core', SWAP)], axis=0)  8.79 us
    all_to_all x1, starting transfers between devices, on_device(): near = lax.all_to_all(copies, 'y', split_axis=0, concat_axis=0)  6.82 us
    pallas_call x1, Pallas kernels, on_device(): pl.pallas_call(functools.partial(grad_kernel, own), out_shape=(jax.ShapeD...  5.88 us
  transfers between devices with their start and end apart: 14, of which 5 were waited for; matrix products, arithmetic and copies ran while one was open for 3% of the time, Pallas kernels for 2%

profile of v7, /device:TPU:1, one launch (start us, length us, event | category | flops | bytes accessed | tf_op | source)
XLA Modules:
  0.0 129.8 jit_solution(6128161800170363943)
XLA Ops:
  0.6 1.1 broadcast_select_fusion.1
  1.7 8.8 %collective-permute-start = (bf16[128,768]{1,0:T(8,128)(2,1)S(1)}, bf16[128,768]{1,0:T(8,128)(2,1)S(1)}, u32[]{:S(2)}, u32[]{:S(2)}) collective-permute-start(bf16[128,768]{1,0:T(8,128)(2,1)S(1)} %get-tuple-element.21), channel_id=1, source_target_pairs={{0,64},{64,0},{1,65},{65,1},{2,66},{66,2},{3,67},{67,3},{4,68},{68... | collective-permute-start | bytes 589832 | tf_op jit(solution)/shard_map/ppermute | solution.py:119
  10.5 0.8 broadcast_select_fusion.2.own_ref
  11.2 0.0 copy-start.1
  11.2 5.3 %collective-permute-start.7 = (bf16[12,768]{1,0:T(8,128)(2,1)S(1)}, bf16[12,768]{1,0:T(8,128)(2,1)S(1)}, u32[]{:S(2)}, u32[]{:S(2)}) collective-permute-start(bf16[12,768]{1,0:T(8,128)(2,1)S(1)} %broadcast_select_fusion.2.own_ref), channel_id=1, source_target_pairs={{0,4},{4,0},{1,5},{5,1},{2,6},{6,2},{3,7},{7,3},{8,12},{12,8},{9,1... | collective-permute-start | bytes 55304 | tf_op jit(solution)/shard_map/ppermute | solution.py:116
  16.5 0.0 collective-permute-done
  16.6 3.1 %collective-permute-start.1 = (bf16[256,768]{1,0:T(8,128)(2,1)S(1)}, bf16[256,768]{1,0:T(8,128)(2,1)S(1)}, u32[]{:S(2)}, u32[]{:S(2)}) collective-permute-start(bf16[256,768]{1,0:T(8,128)(2,1)S(1)} %pad_maximum_fusion.x0), channel_id=1, source_target_pairs={{0,128},{128,256},{256,384},{1,129},{129,257},{257,385},{2,130},{1... | collective-permute-start | bytes 1179656 | tf_op jit(solution)/shard_map/ppermute | solution.py:23
  19.7 1.3 collective-permute-start.4
  21.0 0.0 collective-permute-done.7.other_ref
  21.0 0.0 copy-done.1
  21.0 0.0 copy-start.2
  21.0 0.6 copy-done.2
  21.6 1.5 %shard_map.94 = bf16[8,24,768]{2,1,0:T(8,128)(2,1)} custom-call(bf16[12,768]{1,0:T(8,128)(2,1)} %copy-done.1, bf16[12,768]{1,0:T(8,128)(2,1)} %copy-done.2), custom_call_target="tpu_custom_call" | custom-call | bytes 524288 | tf_op jit(solution)/shard_map/pallas_call | solution.py:131
  23.1 6.8 %all-to-all-start = ((bf16[8,24,768]{2,1,0:T(8,128)(2,1)}), bf16[8,24,768]{2,1,0:T(8,128)(2,1)S(1)}, u32[]{:S(2)}, u32[]{:S(2)}) async-start(bf16[8,24,768]{2,1,0:T(8,128)(2,1)} %shard_map.94), calls=%async_computation | async-start | bytes 589824 | tf_op jit(solution)/shard_map/all_to_all | solution.py:138
  29.9 0.0 collective-permute-done.1.up1
  29.9 4.8 %collective-permute-start.2 = (bf16[256,768]{1,0:T(8,128)(2,1)S(1)}, bf16[256,768]{1,0:T(8,128)(2,1)}, u32[]{:S(2)}, u32[]{:S(2)}) collective-permute-start(bf16[256,768]{1,0:T(8,128)(2,1)S(1)} %collective-permute-done.1.up1), channel_id=1, source_target_pairs={{0,128},{128,256},{256,384},{1,129},{129,257},{257,385},{2,130},{1... | collective-permute-start | bytes 1179656 | tf_op jit(solution)/shard_map/ppermute | solution.py:23
  34.7 4.0 %collective-permute-start.3 = (bf16[256,768]{1,0:T(8,128)(2,1)S(1)}, bf16[256,768]{1,0:T(8,128)(2,1)}, u32[]{:S(2)}, u32[]{:S(2)}) collective-permute-start(bf16[256,768]{1,0:T(8,128)(2,1)S(1)} %collective-permute-done.1.up1), channel_id=1, source_target_pairs={{0,256},{128,384},{1,257},{129,385},{2,258},{130,386},{3,259},{131... | collective-permute-start | bytes 1179656 | tf_op jit(solution)/shard_map/ppermute | solution.py:23
  38.7 0.0 collective-permute-done.4.down1
  38.7 1.3 collective-permute-start.5
  40.0 1.3 collective-permute-start.6
  41.3 0.0 all-to-all-done
  41.3 1.1 broadcast_in_dim.7
  42.4 4.0 %all-to-all-start.1 = ((bf16[4,192,768]{2,1,0:T(8,128)(2,1)}), bf16[4,192,768]{2,1,0:T(8,128)(2,1)S(1)}, u32[]{:S(2)}, u32[]{:S(2)}) async-start(bf16[4,192,768]{2,1,0:T(8,128)(2,1)} %broadcast_in_dim.7), calls=%async_computation.1 | async-start | bytes 2359296 | tf_op jit(solution)/shard_map/all_to_all | solution.py:29
  46.5 0.3 fusion.order_ref
  46.7 0.0 collective-permute-done.2.up2_ref.up2
  46.7 2.9 %collective-permute-done.3.up3_ref.up3 = bf16[256,768]{1,0:T(8,128)(2,1)} collective-permute-done((bf16[256,768]{1,0:T(8,128)(2,1)S(1)}, bf16[256,768]{1,0:T(8,128)(2,1)}, u32[]{:S(2)}, u32[]{:S(2)}) %collective-permute-start.3) | collective-permute-done | bytes 393248 | tf_op jit(solution)/shard_map/ppermute | solution.py:23
  49.7 0.0 collective-permute-done.5.down2_ref.down2
  49.7 16.2 %collective-permute-done.6.down3_ref.down3 = bf16[256,768]{1,0:T(8,128)(2,1)} collective-permute-done((bf16[256,768]{1,0:T(8,128)(2,1)S(1)}, bf16[256,768]{1,0:T(8,128)(2,1)}, u32[]{:S(2)}, u32[]{:S(2)}) %collective-permute-start.6) | collective-permute-done | bytes 393248 | tf_op jit(solution)/shard_map/ppermute | solution.py:23
  65.8 0.6 shard_map.93.arrived_ref
  66.4 0.0 all-to-all-done.1
  66.4 0.0 copy-start
  66.4 0.7 copy-done
  67.1 3.9 %shard_map.95 = (bf16[1024,768]{1,0:T(8,128)(2,1)S(1)}, f32[1024,768]{1,0:T(8,128)S(1)}, f32[1024,1]{1,0:T(8,128)S(1)}, bf16[1024,768]{1,0:T(8,128)(2,1)S(1)}) custom-call(s32[1]{0:T(128)} %bitcast.place, f32[8,128]{1,0:T(8,128)S(1)} %copy-done, bf16[768,768]{1,0:T(8,128)(2,1)S(1)} %fusion.order_ref, bf16[768,768]{1,0:T(8,128)(2,1)S(1)} %bitcast.7, ...), custom_call_target="tpu_custom_call" | custom-call | flops 2113929216 | bytes 8388608 | tf_op jit(solution)/shard_map/pallas_call | solution.py:148
  71.0 4.2 %collective-permute-start.8 = (bf16[1024,768]{1,0:T(8,128)(2,1)S(1)}, bf16[1024,768]{1,0:T(8,128)(2,1)S(1)}, u32[]{:S(2)}, u32[]{:S(2)}) collective-permute-start(bf16[1024,768]{1,0:T(8,128)(2,1)S(1)} %get-tuple-element.10.half_ref), channel_id=1, source_target_pairs={{0,64},{64,0},{1,65},{65,1},{2,66},{66,2},{3,67},{67,3},{4,68},{68... | collective-permute-start | bytes 4718600 | tf_op jit(solution)/shard_map/ppermute | solution.py:164
  76.6 0.1 pad_maximum_fusion.1.scalars
  76.6 1.6 %collective-permute-done.8.partner_ref = bf16[1024,768]{1,0:T(8,128)(2,1)S(1)} collective-permute-done((bf16[1024,768]{1,0:T(8,128)(2,1)S(1)}, bf16[1024,768]{1,0:T(8,128)(2,1)S(1)}, u32[]{:S(2)}, u32[]{:S(2)}) %collective-permute-start.8) | collective-permute-done | bytes 1572896 | tf_op jit(solution)/shard_map/ppermute | solution.py:164
  78.3 5.9 %shard_map.96 = (bf16[768,192]{1,0:T(8,128)(2,1)S(1)}, f32[256,1]{1,0:T(8,128)S(1)}) custom-call(f32[2]{0:T(128)S(1)} %pad_maximum_fusion.1.scalars, s32[1]{0:T(128)} %bitcast.place, bf16[1024,768]{1,0:T(8,128)(2,1)S(1)} %get-tuple-element.10.half_ref, bf16[1024,768]{1,0:T(8,128)(2,1)S(1)} %collective-permute-done.8.partner_ref, ...), custom_call_target="tpu_custom_call" | custom-call | flops 3221225472 | bytes 8388608 | tf_op jit(solution)/shard_map/pallas_call | solution.py:166
  84.2 0.9 reshape.104
  85.1 11.0 %all-to-all-start.2 = ((bf16[64,12,192]{2,1,0:T(8,128)(2,1)}), bf16[64,12,192]{2,1,0:T(8,128)(2,1)S(1)}, u32[]{:S(2)}, u32[]{:S(2)}) async-start(bf16[64,12,192]{2,1,0:T(8,128)(2,1)} %reshape.104), calls=%async_computation.2 | async-start | bytes 1048576 | tf_op jit(solution)/shard_map/all_to_all | solution.py:188
  96.1 0.1 slice_reduce_fusion
  96.2 2.6 %collective-permute-start.9 = (f32[128]{0:T(128)S(1)}, f32[128]{0:T(128)S(1)}, u32[]{:S(2)}, u32[]{:S(2)}) collective-permute-start(f32[128]{0:T(128)S(1)} %get-tuple-element.16), channel_id=1, source_target_pairs={{0,64},{64,0},{1,65},{65,1},{2,66},{66,2},{3,67},{67,3},{4,68},{68... | collective-permute-start | bytes 1544 | tf_op jit(solution)/shard_map/ppermute | solution.py:196
  98.8 15.5 %all-to-all-done.2 = bf16[64,12,192]{2,1,0:T(8,128)(2,1)S(1)} async-done(((bf16[64,12,192]{2,1,0:T(8,128)(2,1)}), bf16[64,12,192]{2,1,0:T(8,128)(2,1)S(1)}, u32[]{:S(2)}, u32[]{:S(2)}) %all-to-all-start.2) | async-done | bytes 294944 | tf_op jit(solution)/shard_map/all_to_all | solution.py:188
  114.3 0.1 convert_reduce_fusion
  114.5 0.7 broadcast_in_dim.8
  115.1 7.0 %all-to-all-start.3 = ((f32[8,12,192]{2,1,0:T(8,128)}), f32[8,12,192]{2,1,0:T(8,128)S(1)}, u32[]{:S(2)}, u32[]{:S(2)}) async-start(f32[8,12,192]{2,1,0:T(8,128)} %broadcast_in_dim.8), calls=%async_computation.3 | async-start | bytes 262144 | tf_op jit(solution)/shard_map/all_to_all | solution.py:29
  122.1 0.0 collective-permute-done.9
  122.1 0.5 broadcast_select_fusion.3
  122.7 5.3 %all-to-all-done.3 = f32[8,12,192]{2,1,0:T(8,128)S(1)} async-done(((f32[8,12,192]{2,1,0:T(8,128)}), f32[8,12,192]{2,1,0:T(8,128)S(1)}, u32[]{:S(2)}, u32[]{:S(2)}) %all-to-all-start.3) | async-done | bytes 73760 | tf_op jit(solution)/shard_map/all_to_all | solution.py:29
  128.0 0.1 copy.13
  128.1 0.3 slice_reduce_fusion.2
  128.3 0.7 squeeze.6
  129.1 0.7 squeeze.7
  (2 shorter events, 0.1 us)
Async XLA Ops:
  1.7 14.8 %collective-permute-start = (bf16[128,768]{1,0:T(8,128)(2,1)S(1)}, bf16[128,768]{1,0:T(8,128)(2,1)S(1)}, u32[]{:S(2)}, u32[]{:S(2)}) collective-permute-start(bf16[128,768]{1,0:T(8,128)(2,1)S(1)} %get-tuple-element.21), channel_id=1, source_target_pairs={{0,64},{64,0},{1,65},{65,1},{2,66},{66,2},{3,67},{67,3},{4,68},{68... | collective-permute-start | bytes 589832 | tf_op jit(solution)/shard_map/ppermute | solution.py:119
  11.2 9.7 %copy-start.1 = (bf16[12,768]{1,0:T(8,128)(2,1)}, bf16[12,768]{1,0:T(8,128)(2,1)S(1)}, u32[]{:S(2)}) copy-start(bf16[12,768]{1,0:T(8,128)(2,1)S(1)} %broadcast_select_fusion.2.own_ref) | copy-start | bytes 55300
  11.2 9.7 %collective-permute-start.7 = (bf16[12,768]{1,0:T(8,128)(2,1)S(1)}, bf16[12,768]{1,0:T(8,128)(2,1)S(1)}, u32[]{:S(2)}, u32[]{:S(2)}) collective-permute-start(bf16[12,768]{1,0:T(8,128)(2,1)S(1)} %broadcast_select_fusion.2.own_ref), channel_id=1, source_target_pairs={{0,4},{4,0},{1,5},{5,1},{2,6},{6,2},{3,7},{7,3},{8,12},{12,8},{9,1... | collective-permute-start | bytes 55304 | tf_op jit(solution)/shard_map/ppermute | solution.py:116
  16.6 13.4 %collective-permute-start.1 = (bf16[256,768]{1,0:T(8,128)(2,1)S(1)}, bf16[256,768]{1,0:T(8,128)(2,1)S(1)}, u32[]{:S(2)}, u32[]{:S(2)}) collective-permute-start(bf16[256,768]{1,0:T(8,128)(2,1)S(1)} %pad_maximum_fusion.x0), channel_id=1, source_target_pairs={{0,128},{128,256},{256,384},{1,129},{129,257},{257,385},{2,130},{1... | collective-permute-start | bytes 1179656 | tf_op jit(solution)/shard_map/ppermute | solution.py:23
  19.7 19.0 %collective-permute-start.4 = (bf16[256,768]{1,0:T(8,128)(2,1)S(1)}, bf16[256,768]{1,0:T(8,128)(2,1)S(1)}, u32[]{:S(2)}, u32[]{:S(2)}) collective-permute-start(bf16[256,768]{1,0:T(8,128)(2,1)S(1)} %pad_maximum_fusion.x0), channel_id=1, source_target_pairs={{128,0},{256,128},{384,256},{129,1},{257,129},{385,257},{130,2},{2... | collective-permute-start | bytes 1179656 | tf_op jit(solution)/shard_map/ppermute | solution.py:23
  21.0 0.6 copy-start.2
  23.1 18.2 %all-to-all-start = ((bf16[8,24,768]{2,1,0:T(8,128)(2,1)}), bf16[8,24,768]{2,1,0:T(8,128)(2,1)S(1)}, u32[]{:S(2)}, u32[]{:S(2)}) async-start(bf16[8,24,768]{2,1,0:T(8,128)(2,1)} %shard_map.94), calls=%async_computation | async-start | bytes 589824 | tf_op jit(solution)/shard_map/all_to_all | solution.py:138
  29.9 16.8 %collective-permute-start.2 = (bf16[256,768]{1,0:T(8,128)(2,1)S(1)}, bf16[256,768]{1,0:T(8,128)(2,1)}, u32[]{:S(2)}, u32[]{:S(2)}) collective-permute-start(bf16[256,768]{1,0:T(8,128)(2,1)S(1)} %collective-permute-done.1.up1), channel_id=1, source_target_pairs={{0,128},{128,256},{256,384},{1,129},{129,257},{257,385},{2,130},{1... | collective-permute-start | bytes 1179656 | tf_op jit(solution)/shard_map/ppermute | solution.py:23
  34.7 15.0 %collective-permute-start.3 = (bf16[256,768]{1,0:T(8,128)(2,1)S(1)}, bf16[256,768]{1,0:T(8,128)(2,1)}, u32[]{:S(2)}, u32[]{:S(2)}) collective-permute-start(bf16[256,768]{1,0:T(8,128)(2,1)S(1)} %collective-permute-done.1.up1), channel_id=1, source_target_pairs={{0,256},{128,384},{1,257},{129,385},{2,258},{130,386},{3,259},{131... | collective-permute-start | bytes 1179656 | tf_op jit(solution)/shard_map/ppermute | solution.py:23
  38.7 11.0 %collective-permute-start.5 = (bf16[256,768]{1,0:T(8,128)(2,1)S(1)}, bf16[256,768]{1,0:T(8,128)(2,1)}, u32[]{:S(2)}, u32[]{:S(2)}) collective-permute-start(bf16[256,768]{1,0:T(8,128)(2,1)S(1)} %collective-permute-done.4.down1), channel_id=1, source_target_pairs={{128,0},{256,128},{384,256},{129,1},{257,129},{385,257},{130,2},{2... | collective-permute-start | bytes 1179656 | tf_op jit(solution)/shard_map/ppermute | solution.py:23
  40.0 25.8 %collective-permute-start.6 = (bf16[256,768]{1,0:T(8,128)(2,1)S(1)}, bf16[256,768]{1,0:T(8,128)(2,1)}, u32[]{:S(2)}, u32[]{:S(2)}) collective-permute-start(bf16[256,768]{1,0:T(8,128)(2,1)S(1)} %collective-permute-done.4.down1), channel_id=1, source_target_pairs={{256,0},{384,128},{257,1},{385,129},{258,2},{386,130},{259,3},{387... | collective-permute-start | bytes 1179656 | tf_op jit(solution)/shard_map/ppermute | solution.py:23
  42.4 24.0 %all-to-all-start.1 = ((bf16[4,192,768]{2,1,0:T(8,128)(2,1)}), bf16[4,192,768]{2,1,0:T(8,128)(2,1)S(1)}, u32[]{:S(2)}, u32[]{:S(2)}) async-start(bf16[4,192,768]{2,1,0:T(8,128)(2,1)} %broadcast_in_dim.7), calls=%async_computation.1 | async-start | bytes 2359296 | tf_op jit(solution)/shard_map/all_to_all | solution.py:29
  66.4 0.7 copy-start
  71.0 7.3 %collective-permute-start.8 = (bf16[1024,768]{1,0:T(8,128)(2,1)S(1)}, bf16[1024,768]{1,0:T(8,128)(2,1)S(1)}, u32[]{:S(2)}, u32[]{:S(2)}) collective-permute-start(bf16[1024,768]{1,0:T(8,128)(2,1)S(1)} %get-tuple-element.10.half_ref), channel_id=1, source_target_pairs={{0,64},{64,0},{1,65},{65,1},{2,66},{66,2},{3,67},{67,3},{4,68},{68... | collective-permute-start | bytes 4718600 | tf_op jit(solution)/shard_map/ppermute | solution.py:164
  85.1 29.2 %all-to-all-start.2 = ((bf16[64,12,192]{2,1,0:T(8,128)(2,1)}), bf16[64,12,192]{2,1,0:T(8,128)(2,1)S(1)}, u32[]{:S(2)}, u32[]{:S(2)}) async-start(bf16[64,12,192]{2,1,0:T(8,128)(2,1)} %reshape.104), calls=%async_computation.2 | async-start | bytes 1048576 | tf_op jit(solution)/shard_map/all_to_all | solution.py:188
  96.2 25.9 %collective-permute-start.9 = (f32[128]{0:T(128)S(1)}, f32[128]{0:T(128)S(1)}, u32[]{:S(2)}, u32[]{:S(2)}) collective-permute-start(f32[128]{0:T(128)S(1)} %get-tuple-element.16), channel_id=1, source_target_pairs={{0,64},{64,0},{1,65},{65,1},{2,66},{66,2},{3,67},{67,3},{4,68},{68... | collective-permute-start | bytes 1544 | tf_op jit(solution)/shard_map/ppermute | solution.py:196
  115.1 12.9 %all-to-all-start.3 = ((f32[8,12,192]{2,1,0:T(8,128)}), f32[8,12,192]{2,1,0:T(8,128)S(1)}, u32[]{:S(2)}, u32[]{:S(2)}) async-start(f32[8,12,192]{2,1,0:T(8,128)} %broadcast_in_dim.8), calls=%async_computation.3 | async-start | bytes 262144 | tf_op jit(solution)/shard_map/all_to_all | solution.py:29

commit v8 on v7

--- a/solution.py
+++ b/solution.py
@@ -9,7 +9,7 @@
 
 EVERY = ("zlo", "core", "y", "zhi", "x")
 GRP = ("y", "zhi", "x")
-ARRIVED = 8 * 10**9
+ARRIVED = 10 * 10**9
 SWAP = [(0, 1), (1, 0)]
 F32, BF16 = jnp.float32, jnp.bfloat16
 VMEM = pl.BlockSpec(memory_space=pltpu.VMEM)
@@ -27,13 +27,6 @@
     count = lax.axis_size(axis)
     copies = jnp.broadcast_to(value[None], (count,) + value.shape)
     return lax.all_to_all(copies, axis, split_axis=0, concat_axis=0)
-
-
-def copies_kernel(own_ref, other_ref, out_ref):
-    share = own_ref.shape[0]
-    for k in range(out_ref.shape[0]):
-        out_ref[k, :share] = own_ref[...]
-        out_ref[k, share:] = other_ref[...]
 
 
 def arrived_kernel(up2_ref, up3_ref, down2_ref, down3_ref, out_ref):
@@ -113,7 +106,6 @@
     chips = lax.axis_size("zlo")
     n_y, n_zhi, n_x = (lax.axis_size(a) for a in GRP)
     piece = jnp.where(first, picture_mapping, caption_mapping)
-    other = lax.ppermute(piece, "zhi", SWAP)
     mine = jnp.where(first, picture_inputs, caption_inputs)
     sent = jnp.where(first, caption_inputs, picture_inputs)
     chunk = jnp.concatenate([mine, lax.ppermute(sent, "core", SWAP)], axis=0)
@@ -128,21 +120,11 @@
         cost_estimate=pl.CostEstimate(flops=ARRIVED, bytes_accessed=2**12, transcendentals=0),
     )(*up[2:], *down[2:])
     at_chip = lax.axis_index("zlo").astype(jnp.int32).reshape(1)
-    copies = pl.pallas_call(
-        copies_kernel,
-        out_shape=jax.ShapeDtypeStruct((n_y, n_zhi * share, embed), BF16),
-        in_specs=[VMEM] * 2,
-        out_specs=VMEM,
-        cost_estimate=pl.CostEstimate(flops=0, bytes_accessed=2**19, transcendentals=0),
-    )(piece, other)
-    near = lax.all_to_all(copies, "y", split_axis=0, concat_axis=0)
-    near = near.reshape(n_y * n_zhi * share, embed)
+    near = spread(piece, ("y", "zhi")).reshape(n_y * n_zhi * share, embed)
     gathered = spread(near, "x").reshape(width, embed)
     at = jnp.arange(width, dtype=jnp.int32)
     owner, row = at // share, at % share
-    at_half = (owner // n_x) % n_zhi
-    at_half = jnp.where(lax.axis_index("zhi") == 0, at_half, 1 - at_half)
-    from_row = (((owner % n_x) * n_y + owner // (n_x * n_zhi)) * n_zhi + at_half) * share + row
+    from_row = ((owner % n_x) * (n_y * n_zhi) + owner // n_x) * share + row
     order = (from_row[:, None] == at[None, :]).astype(BF16)
     rows = chips * chunk.shape[0]
     half, unit, radius, set_rows = pl.pallas_call(

time: 131 us -> 133 us (1.015)
  waiting for transfers between devices: 41.6 us -> 49.5 us
  starting transfers between devices: 65.4 us -> 62.3 us
  Pallas kernels: 11.9 us -> 10.4 us
    all_to_all x2 -> x3, starting transfers between devices: 11 us -> 22.8 us  [spread(): return lax.all_to_all(copies, axis, split_axis=0, concat_axis=0)]
    all_to_all x1 -> x0, starting transfers between devices: 6.82 us -> none  [on_device(): near = lax.all_to_all(copies, 'y', split_axis=0, concat_axis=0)]
    all_to_all x2 -> x3, waiting for transfers between devices: 5.32 us -> 11.6 us  [spread(): return lax.all_to_all(copies, axis, split_axis=0, concat_axis=0)]
    ppermute x1 -> x0, starting transfers between devices: 5.25 us -> none  [on_device(): other = lax.ppermute(piece, 'zhi', SWAP)]
    ppermute x6, starting transfers between devices: 15.7 us -> 13.9 us  [passed_on(): lax.ppermute(value, axis, [(i, i + by) for i in range(count) if 0 <= i +...]
    pallas_call x1 -> x0, Pallas kernels: 1.5 us -> none  [on_device(): pl.pallas_call(copies_kernel, out_shape=jax.ShapeDtypeStruct((n_y, n_zhi...]
    ppermute x1, starting transfers between devices: 4.25 us -> 2.8 us  [on_device(): partner = lax.ppermute(half, 'core', SWAP)]
  transfers between devices with their start and end apart: 14 -> 13, of which waited for: 5 -> 7; matrix products, arithmetic and copies ran while one was open for 3% -> 3% of each run, Pallas kernels for 2% -> 0%
where the time goes in v8:
time: 133 us; the launch traced here: 132 us
  starting transfers between devices  62.3 us (47%)
  waiting for transfers between devices  49.5 us (37%)
  Pallas kernels  10.4 us (8%)
  local copies, waits for them, and re-layouts  6.07 us (5%)
  between operations  2.11 us (2%)
  other arithmetic  2.09 us (2%)
    all_to_all x3, starting transfers between devices, spread(): return lax.all_to_all(copies, axis, split_axis=0, concat_axis=0)  22.8 us
    ppermute x6, waiting for transfers between devices, passed_on(): lax.ppermute(value, axis, [(i, i + by) for i in range(count) if 0 <= i +...  19.6 us
    all_to_all x1, waiting for transfers between devices, on_device(): lax.all_to_all(local.reshape(width // share, share, columns), GRP, split_...  15.6 us
    ppermute x6, starting transfers between devices, passed_on(): lax.ppermute(value, axis, [(i, i + by) for i in range(count) if 0 <= i +...  13.9 us
    all_to_all x3, waiting for transfers between devices, spread(): return lax.all_to_all(copies, axis, split_axis=0, concat_axis=0)  11.6 us
    all_to_all x1, starting transfers between devices, on_device(): lax.all_to_all(local.reshape(width // share, share, columns), GRP, split_...  11.4 us
    ppermute x1, starting transfers between devices, on_device(): chunk = jnp.concatenate([mine, lax.ppermute(sent, 'core', SWAP)], axis=0)  8.79 us
    pallas_call x1, Pallas kernels, on_device(): pl.pallas_call(functools.partial(grad_kernel, own), out_shape=(jax.ShapeD...  5.88 us
  transfers between devices with their start and end apart: 13, of which 7 were waited for; matrix products, arithmetic and copies ran while one was open for 3% of the time, Pallas kernels for 0%

profile of v8, /device:TPU:1, one launch (start us, length us, event | category | flops | bytes accessed | tf_op | source)
XLA Modules:
  0.0 132.4 jit_solution(13951900703768455954)
XLA Ops:
  0.6 0.0 copy-start.1
  0.6 0.0 copy-start.2
  0.7 1.1 broadcast_select_fusion.1
  1.7 8.8 %collective-permute-start = (bf16[128,768]{1,0:T(8,128)(2,1)S(1)}, bf16[128,768]{1,0:T(8,128)(2,1)S(1)}, u32[]{:S(2)}, u32[]{:S(2)}) collective-permute-start(bf16[128,768]{1,0:T(8,128)(2,1)S(1)} %get-tuple-element.21), channel_id=1, source_target_pairs={{0,64},{64,0},{1,65},{65,1},{2,66},{66,2},{3,67},{67,3},{4,68},{68... | collective-permute-start | bytes 589832 | tf_op jit(solution)/shard_map/ppermute | solution.py:111
  10.5 1.0 collective-permute-done
  11.6 1.3 collective-permute-start.1
  12.9 1.3 collective-permute-start.4
  14.2 0.0 copy-done.1
  14.2 0.0 copy-done.2
  14.2 0.8 broadcast_in_dim.8
  15.0 11.8 %all-to-all-start = ((bf16[16,12,768]{2,1,0:T(8,128)(2,1)}), bf16[16,12,768]{2,1,0:T(8,128)(2,1)S(1)}, u32[]{:S(2)}, u32[]{:S(2)}) async-start(bf16[16,12,768]{2,1,0:T(8,128)(2,1)} %broadcast_in_dim.8), calls=%async_computation | async-start | bytes 786432 | tf_op jit(solution)/shard_map/all_to_all | solution.py:29
  26.8 0.0 collective-permute-done.1.up1
  26.8 4.8 %collective-permute-start.2 = (bf16[256,768]{1,0:T(8,128)(2,1)S(1)}, bf16[256,768]{1,0:T(8,128)(2,1)}, u32[]{:S(2)}, u32[]{:S(2)}) collective-permute-start(bf16[256,768]{1,0:T(8,128)(2,1)S(1)} %collective-permute-done.1.up1), channel_id=1, source_target_pairs={{0,128},{128,256},{256,384},{1,129},{129,257},{257,385},{2,130},{1... | collective-permute-start | bytes 1179656 | tf_op jit(solution)/shard_map/ppermute | solution.py:23
  31.6 4.0 %collective-permute-start.3 = (bf16[256,768]{1,0:T(8,128)(2,1)S(1)}, bf16[256,768]{1,0:T(8,128)(2,1)}, u32[]{:S(2)}, u32[]{:S(2)}) collective-permute-start(bf16[256,768]{1,0:T(8,128)(2,1)S(1)} %collective-permute-done.1.up1), channel_id=1, source_target_pairs={{0,256},{128,384},{1,257},{129,385},{2,258},{130,386},{3,259},{131... | collective-permute-start | bytes 1179656 | tf_op jit(solution)/shard_map/ppermute | solution.py:23
  35.6 0.0 collective-permute-done.4.down1
  35.6 1.3 collective-permute-start.5
  36.9 1.3 collective-permute-start.6
  38.2 0.3 fusion.order_ref
  38.5 6.3 %all-to-all-done = bf16[16,12,768]{2,1,0:T(8,128)(2,1)S(1)} async-done(((bf16[16,12,768]{2,1,0:T(8,128)(2,1)}), bf16[16,12,768]{2,1,0:T(8,128)(2,1)S(1)}, u32[]{:S(2)}, u32[]{:S(2)}) %all-to-all-start) | async-done | bytes 294944 | tf_op jit(solution)/shard_map/all_to_all | solution.py:29
  44.8 0.1 broadcast_in_dim.9
  44.9 1.1 broadcast_in_dim.10
  46.0 4.0 %all-to-all-start.1 = ((bf16[4,192,768]{2,1,0:T(8,128)(2,1)}), bf16[4,192,768]{2,1,0:T(8,128)(2,1)S(1)}, u32[]{:S(2)}, u32[]{:S(2)}) async-start(bf16[4,192,768]{2,1,0:T(8,128)(2,1)} %broadcast_in_dim.10), calls=%async_computation.1 | async-start | bytes 2359296 | tf_op jit(solution)/shard_map/all_to_all | solution.py:29
  50.0 0.0 collective-permute-done.2.up2_ref.up2
  50.0 4.8 %collective-permute-done.3.up3_ref.up3 = bf16[256,768]{1,0:T(8,128)(2,1)} collective-permute-done((bf16[256,768]{1,0:T(8,128)(2,1)S(1)}, bf16[256,768]{1,0:T(8,128)(2,1)}, u32[]{:S(2)}, u32[]{:S(2)}) %collective-permute-start.3) | collective-permute-done | bytes 393248 | tf_op jit(solution)/shard_map/ppermute | solution.py:23
  54.8 0.0 collective-permute-done.5.down2_ref.down2
  54.8 14.8 %collective-permute-done.6.down3_ref.down3 = bf16[256,768]{1,0:T(8,128)(2,1)} collective-permute-done((bf16[256,768]{1,0:T(8,128)(2,1)S(1)}, bf16[256,768]{1,0:T(8,128)(2,1)}, u32[]{:S(2)}, u32[]{:S(2)}) %collective-permute-start.6) | collective-permute-done | bytes 393248 | tf_op jit(solution)/shard_map/ppermute | solution.py:23
  69.6 0.6 shard_map.93.arrived_ref
  70.2 0.0 all-to-all-done.1
  70.2 0.0 copy-start
  70.2 0.7 copy-done
  70.9 3.9 %shard_map.94 = (bf16[1024,768]{1,0:T(8,128)(2,1)S(1)}, f32[1024,768]{1,0:T(8,128)S(1)}, f32[1024,1]{1,0:T(8,128)S(1)}, bf16[1024,768]{1,0:T(8,128)(2,1)S(1)}) custom-call(s32[1]{0:T(128)} %bitcast.place, f32[8,128]{1,0:T(8,128)S(1)} %copy-done, bf16[768,768]{1,0:T(8,128)(2,1)S(1)} %fusion.order_ref, bf16[768,768]{1,0:T(8,128)(2,1)S(1)} %bitcast.6, ...), custom_call_target="tpu_custom_call" | custom-call | flops 2113929216 | bytes 8388608 | tf_op jit(solution)/shard_map/pallas_call | solution.py:130
  74.8 2.8 %collective-permute-start.7 = (bf16[1024,768]{1,0:T(8,128)(2,1)S(1)}, bf16[1024,768]{1,0:T(8,128)(2,1)S(1)}, u32[]{:S(2)}, u32[]{:S(2)}) collective-permute-start(bf16[1024,768]{1,0:T(8,128)(2,1)S(1)} %get-tuple-element.10.half_ref), channel_id=1, source_target_pairs={{0,64},{64,0},{1,65},{65,1},{2,66},{66,2},{3,67},{67,3},{4,68},{68... | collective-permute-start | bytes 4718600 | tf_op jit(solution)/shard_map/ppermute | solution.py:146
  78.9 0.1 pad_maximum_fusion.1.scalars
  79.0 1.6 %collective-permute-done.7.partner_ref = bf16[1024,768]{1,0:T(8,128)(2,1)S(1)} collective-permute-done((bf16[1024,768]{1,0:T(8,128)(2,1)S(1)}, bf16[1024,768]{1,0:T(8,128)(2,1)S(1)}, u32[]{:S(2)}, u32[]{:S(2)}) %collective-permute-start.7) | collective-permute-done | bytes 1572896 | tf_op jit(solution)/shard_map/ppermute | solution.py:146
  80.6 5.9 %shard_map.95 = (bf16[768,192]{1,0:T(8,128)(2,1)S(1)}, f32[256,1]{1,0:T(8,128)S(1)}) custom-call(f32[2]{0:T(128)S(1)} %pad_maximum_fusion.1.scalars, s32[1]{0:T(128)} %bitcast.place, bf16[1024,768]{1,0:T(8,128)(2,1)S(1)} %get-tuple-element.10.half_ref, bf16[1024,768]{1,0:T(8,128)(2,1)S(1)} %collective-permute-done.7.partner_ref, ...), custom_call_target="tpu_custom_call" | custom-call | flops 3221225472 | bytes 8388608 | tf_op jit(solution)/shard_map/pallas_call | solution.py:148
  86.5 0.9 reshape.80
  87.4 11.4 %all-to-all-start.2 = ((bf16[64,12,192]{2,1,0:T(8,128)(2,1)}), bf16[64,12,192]{2,1,0:T(8,128)(2,1)S(1)}, u32[]{:S(2)}, u32[]{:S(2)}) async-start(bf16[64,12,192]{2,1,0:T(8,128)(2,1)} %reshape.80), calls=%async_computation.2 | async-start | bytes 1048576 | tf_op jit(solution)/shard_map/all_to_all | solution.py:170
  98.8 0.1 slice_reduce_fusion
  98.9 2.6 %collective-permute-start.8 = (f32[128]{0:T(128)S(1)}, f32[128]{0:T(128)S(1)}, u32[]{:S(2)}, u32[]{:S(2)}) collective-permute-start(f32[128]{0:T(128)S(1)} %get-tuple-element.16), channel_id=1, source_target_pairs={{0,64},{64,0},{1,65},{65,1},{2,66},{66,2},{3,67},{67,3},{4,68},{68... | collective-permute-start | bytes 1544 | tf_op jit(solution)/shard_map/ppermute | solution.py:178
  101.5 15.6 %all-to-all-done.2 = bf16[64,12,192]{2,1,0:T(8,128)(2,1)S(1)} async-done(((bf16[64,12,192]{2,1,0:T(8,128)(2,1)}), bf16[64,12,192]{2,1,0:T(8,128)(2,1)S(1)}, u32[]{:S(2)}, u32[]{:S(2)}) %all-to-all-start.2) | async-done | bytes 294944 | tf_op jit(solution)/shard_map/all_to_all | solution.py:170
  117.0 0.1 convert_reduce_fusion
  117.1 0.6 broadcast_in_dim.11
  117.8 7.0 %all-to-all-start.3 = ((f32[8,12,192]{2,1,0:T(8,128)}), f32[8,12,192]{2,1,0:T(8,128)S(1)}, u32[]{:S(2)}, u32[]{:S(2)}) async-start(f32[8,12,192]{2,1,0:T(8,128)} %broadcast_in_dim.11), calls=%async_computation.3 | async-start | bytes 262144 | tf_op jit(solution)/shard_map/all_to_all | solution.py:29
  124.8 0.0 collective-permute-done.8
  124.8 0.5 broadcast_select_fusion.3
  125.3 5.3 %all-to-all-done.3 = f32[8,12,192]{2,1,0:T(8,128)S(1)} async-done(((f32[8,12,192]{2,1,0:T(8,128)}), f32[8,12,192]{2,1,0:T(8,128)S(1)}, u32[]{:S(2)}, u32[]{:S(2)}) %all-to-all-start.3) | async-done | bytes 73760 | tf_op jit(solution)/shard_map/all_to_all | solution.py:29
  130.6 0.1 copy.13
  130.7 0.3 slice_reduce_fusion.2
  131.0 0.7 squeeze.6
  131.7 0.7 squeeze.7
  (3 shorter events, 0.1 us)
Async XLA Ops:
  0.6 13.6 %copy-start.1 = (bf16[12,768]{1,0:T(8,128)(2,1)S(1)}, bf16[12,768]{1,0:T(8,128)(2,1)}, u32[]{:S(2)}) copy-start(bf16[12,768]{1,0:T(8,128)(2,1)} %param.8) | copy-start | bytes 55300
  0.6 13.6 %copy-start.2 = (bf16[12,768]{1,0:T(8,128)(2,1)S(1)}, bf16[12,768]{1,0:T(8,128)(2,1)}, u32[]{:S(2)}) copy-start(bf16[12,768]{1,0:T(8,128)(2,1)} %param.9) | copy-start | bytes 55300
  1.7 9.8 %collective-permute-start = (bf16[128,768]{1,0:T(8,128)(2,1)S(1)}, bf16[128,768]{1,0:T(8,128)(2,1)S(1)}, u32[]{:S(2)}, u32[]{:S(2)}) collective-permute-start(bf16[128,768]{1,0:T(8,128)(2,1)S(1)} %get-tuple-element.21), channel_id=1, source_target_pairs={{0,64},{64,0},{1,65},{65,1},{2,66},{66,2},{3,67},{67,3},{4,68},{68... | collective-permute-start | bytes 589832 | tf_op jit(solution)/shard_map/ppermute | solution.py:111
  11.6 15.2 %collective-permute-start.1 = (bf16[256,768]{1,0:T(8,128)(2,1)S(1)}, bf16[256,768]{1,0:T(8,128)(2,1)S(1)}, u32[]{:S(2)}, u32[]{:S(2)}) collective-permute-start(bf16[256,768]{1,0:T(8,128)(2,1)S(1)} %pad_maximum_fusion.x0), channel_id=1, source_target_pairs={{0,128},{128,256},{256,384},{1,129},{129,257},{257,385},{2,130},{1... | collective-permute-start | bytes 1179656 | tf_op jit(solution)/shard_map/ppermute | solution.py:23
  12.9 22.7 %collective-permute-start.4 = (bf16[256,768]{1,0:T(8,128)(2,1)S(1)}, bf16[256,768]{1,0:T(8,128)(2,1)S(1)}, u32[]{:S(2)}, u32[]{:S(2)}) collective-permute-start(bf16[256,768]{1,0:T(8,128)(2,1)S(1)} %pad_maximum_fusion.x0), channel_id=1, source_target_pairs={{128,0},{256,128},{384,256},{129,1},{257,129},{385,257},{130,2},{2... | collective-permute-start | bytes 1179656 | tf_op jit(solution)/shard_map/ppermute | solution.py:23
  15.0 29.8 %all-to-all-start = ((bf16[16,12,768]{2,1,0:T(8,128)(2,1)}), bf16[16,12,768]{2,1,0:T(8,128)(2,1)S(1)}, u32[]{:S(2)}, u32[]{:S(2)}) async-start(bf16[16,12,768]{2,1,0:T(8,128)(2,1)} %broadcast_in_dim.8), calls=%async_computation | async-start | bytes 786432 | tf_op jit(solution)/shard_map/all_to_all | solution.py:29
  26.8 23.1 %collective-permute-start.2 = (bf16[256,768]{1,0:T(8,128)(2,1)S(1)}, bf16[256,768]{1,0:T(8,128)(2,1)}, u32[]{:S(2)}, u32[]{:S(2)}) collective-permute-start(bf16[256,768]{1,0:T(8,128)(2,1)S(1)} %collective-permute-done.1.up1), channel_id=1, source_target_pairs={{0,128},{128,256},{256,384},{1,129},{129,257},{257,385},{2,130},{1... | collective-permute-start | bytes 1179656 | tf_op jit(solution)/shard_map/ppermute | solution.py:23
  31.6 23.2 %collective-permute-start.3 = (bf16[256,768]{1,0:T(8,128)(2,1)S(1)}, bf16[256,768]{1,0:T(8,128)(2,1)}, u32[]{:S(2)}, u32[]{:S(2)}) collective-permute-start(bf16[256,768]{1,0:T(8,128)(2,1)S(1)} %collective-permute-done.1.up1), channel_id=1, source_target_pairs={{0,256},{128,384},{1,257},{129,385},{2,258},{130,386},{3,259},{131... | collective-permute-start | bytes 1179656 | tf_op jit(solution)/shard_map/ppermute | solution.py:23
  35.6 19.2 %collective-permute-start.5 = (bf16[256,768]{1,0:T(8,128)(2,1)S(1)}, bf16[256,768]{1,0:T(8,128)(2,1)}, u32[]{:S(2)}, u32[]{:S(2)}) collective-permute-start(bf16[256,768]{1,0:T(8,128)(2,1)S(1)} %collective-permute-done.4.down1), channel_id=1, source_target_pairs={{128,0},{256,128},{384,256},{129,1},{257,129},{385,257},{130,2},{2... | collective-permute-start | bytes 1179656 | tf_op jit(solution)/shard_map/ppermute | solution.py:23
  36.9 32.7 %collective-permute-start.6 = (bf16[256,768]{1,0:T(8,128)(2,1)S(1)}, bf16[256,768]{1,0:T(8,128)(2,1)}, u32[]{:S(2)}, u32[]{:S(2)}) collective-permute-start(bf16[256,768]{1,0:T(8,128)(2,1)S(1)} %collective-permute-done.4.down1), channel_id=1, source_target_pairs={{256,0},{384,128},{257,1},{385,129},{258,2},{386,130},{259,3},{387... | collective-permute-start | bytes 1179656 | tf_op jit(solution)/shard_map/ppermute | solution.py:23
  46.0 24.2 %all-to-all-start.1 = ((bf16[4,192,768]{2,1,0:T(8,128)(2,1)}), bf16[4,192,768]{2,1,0:T(8,128)(2,1)S(1)}, u32[]{:S(2)}, u32[]{:S(2)}) async-start(bf16[4,192,768]{2,1,0:T(8,128)(2,1)} %broadcast_in_dim.10), calls=%async_computation.1 | async-start | bytes 2359296 | tf_op jit(solution)/shard_map/all_to_all | solution.py:29
  70.2 0.7 copy-start
  74.8 5.8 %collective-permute-start.7 = (bf16[1024,768]{1,0:T(8,128)(2,1)S(1)}, bf16[1024,768]{1,0:T(8,128)(2,1)S(1)}, u32[]{:S(2)}, u32[]{:S(2)}) collective-permute-start(bf16[1024,768]{1,0:T(8,128)(2,1)S(1)} %get-tuple-element.10.half_ref), channel_id=1, source_target_pairs={{0,64},{64,0},{1,65},{65,1},{2,66},{66,2},{3,67},{67,3},{4,68},{68... | collective-permute-start | bytes 4718600 | tf_op jit(solution)/shard_map/ppermute | solution.py:146
  87.4 29.6 %all-to-all-start.2 = ((bf16[64,12,192]{2,1,0:T(8,128)(2,1)}), bf16[64,12,192]{2,1,0:T(8,128)(2,1)S(1)}, u32[]{:S(2)}, u32[]{:S(2)}) async-start(bf16[64,12,192]{2,1,0:T(8,128)(2,1)} %reshape.80), calls=%async_computation.2 | async-start | bytes 1048576 | tf_op jit(solution)/shard_map/all_to_all | solution.py:170
  98.9 25.9 %collective-permute-start.8 = (f32[128]{0:T(128)S(1)}, f32[128]{0:T(128)S(1)}, u32[]{:S(2)}, u32[]{:S(2)}) collective-permute-start(f32[128]{0:T(128)S(1)} %get-tuple-element.16), channel_id=1, source_target_pairs={{0,64},{64,0},{1,65},{65,1},{2,66},{66,2},{3,67},{67,3},{4,68},{68... | collective-permute-start | bytes 1544 | tf_op jit(solution)/shard_map/ppermute | solution.py:178
  117.8 12.8 %all-to-all-start.3 = ((f32[8,12,192]{2,1,0:T(8,128)}), f32[8,12,192]{2,1,0:T(8,128)S(1)}, u32[]{:S(2)}, u32[]{:S(2)}) async-start(f32[8,12,192]{2,1,0:T(8,128)} %broadcast_in_dim.11), calls=%async_computation.3 | async-start | bytes 262144 | tf_op jit(solution)/shard_map/all_to_all | solution.py:29

commit v9 on v7

--- a/solution.py
+++ b/solution.py
@@ -62,11 +62,11 @@
 
 
 def grad_kernel(
-    own, scalars, place, half_ref, partner_ref, unit_ref, radius_ref, rows_ref,
+    own, grid, scalars, place, half_ref, partner_ref, unit_ref, radius_ref, rows_ref,
     local_ref, norms_ref, pre_ref,
 ):
     multiplier, offset = scalars[0], scalars[1]
-    columns = local_ref.shape[1]
+    peers, held, columns = local_ref.shape
     start = pl.multiple_of((3 * place[0]) // 2 * 128, 128)
     total = None
     rows = 2 * own
@@ -96,7 +96,13 @@
         )
         total = part if total is None else total + part
     odd = place[0] % 2 == 1
-    local_ref[...] = jnp.where(odd, total[:, 256 - columns :], total[:, :columns]).astype(BF16)
+    total = jnp.where(odd, total[:, 256 - columns :], total[:, :columns])
+    n_y, n_zhi, n_x = grid
+    share = held // n_zhi
+    for k in range(peers * n_zhi):
+        y, zhi, x = k // (n_zhi * n_x), k // n_x % n_zhi, k % n_x
+        piece = total[k * share : (k + 1) * share].astype(BF16)
+        local_ref[y * n_x + x, zhi * share : (zhi + 1) * share] = piece
 
 
 def on_device(
@@ -164,9 +170,9 @@
     partner = lax.ppermute(half, "core", SWAP)
     columns = embed // chips
     local, norms = pl.pallas_call(
-        functools.partial(grad_kernel, own),
+        functools.partial(grad_kernel, own, (n_y, n_zhi, n_x)),
         out_shape=(
-            jax.ShapeDtypeStruct((width, columns), BF16),
+            jax.ShapeDtypeStruct((n_y * n_x, n_zhi * share, columns), BF16),
             jax.ShapeDtypeStruct((2 * own, 1), F32),
         ),
         in_specs=[SMEM] * 2 + [VMEM] * 5,
@@ -185,11 +191,17 @@
         radius,
         set_rows,
     )
-    pieces = lax.all_to_all(
-        local.reshape(width // share, share, columns), GRP, split_axis=0, concat_axis=0, tiled=True
+    pieces = lax.all_to_all(local, ("y", "x"), split_axis=0, concat_axis=0, tiled=True)
+    totals = jnp.sum(pieces.astype(F32), axis=0).reshape(n_zhi, 1, share, columns)
+    totals = jnp.broadcast_to(totals, (n_zhi, 2 * chips, share, columns))
+    parts = lax.all_to_all(
+        totals.reshape(2 * n_zhi * chips, share, columns),
+        ("zhi", "zlo", "core"),
+        split_axis=0,
+        concat_axis=0,
+        tiled=True,
     )
-    total = jnp.sum(pieces.astype(F32), axis=0)
-    whole = spread(total, ("zlo", "core")).reshape(chips, 2, share, columns)
+    whole = jnp.sum(parts.reshape(n_zhi, chips, 2, share, columns), axis=0)
     whole = whole.transpose(1, 2, 0, 3).reshape(2, share, embed)
     norms = norms.reshape(2 * own)
     own_norms = norms[:own]

time: 131 us -> 128 us (0.977)
  blocking collectives: 0 us -> 23.2 us
  starting transfers between devices: 65.4 us -> 52.7 us
  waiting for transfers between devices: 41.6 us -> 29.9 us
    all_to_all x0 -> x1, blocking collectives: none -> 23.2 us  [on_device(): lax.all_to_all(local, ('y', 'x'), split_axis=0, concat_axis=0, tiled=True)]
    all_to_all x1, waiting for transfers between devices: 15.5 us -> 8.22 us  [on_device(): lax.all_to_all(totals.reshape(2 * n_zhi * chips, share, columns), ('zhi',...]
    all_to_all x2 -> x1, starting transfers between devices: 11 us -> 4.01 us  [spread(): return lax.all_to_all(copies, axis, split_axis=0, concat_axis=0)]
    all_to_all x1, starting transfers between devices: 11 us -> 5.67 us  [on_device(): lax.all_to_all(totals.reshape(2 * n_zhi * chips, share, columns), ('zhi',...]
    all_to_all x2 -> x1, waiting for transfers between devices: 5.32 us -> 0.01 us  [spread(): return lax.all_to_all(copies, axis, split_axis=0, concat_axis=0)]
  transfers between devices with their start and end apart: 14 -> 13, of which waited for: 5 -> 5; matrix products, arithmetic and copies ran while one was open for 3% -> 2% of each run, Pallas kernels for 2% -> 2%
where the time goes in v9:
time: 128 us; the launch traced here: 127 us
  starting transfers between devices  52.7 us (41%)
  waiting for transfers between devices  29.9 us (23%)
  blocking collectives  23.2 us (18%)
  Pallas kernels  11.9 us (9%)
  local copies, waits for them, and re-layouts  4.73 us (4%)
  other arithmetic  2.82 us (2%)
  between operations  2.13 us (2%)
    all_to_all x1, blocking collectives, on_device(): lax.all_to_all(local, ('y', 'x'), split_axis=0, concat_axis=0, tiled=True)  23.2 us
    ppermute x6, waiting for transfers between devices, passed_on(): lax.ppermute(value, axis, [(i, i + by) for i in range(count) if 0 <= i +...  19.1 us
    ppermute x6, starting transfers between devices, passed_on(): lax.ppermute(value, axis, [(i, i + by) for i in range(count) if 0 <= i +...  15.7 us
    ppermute x1, starting transfers between devices, on_device(): chunk = jnp.concatenate([mine, lax.ppermute(sent, 'core', SWAP)], axis=0)  8.79 us
    all_to_all x1, waiting for transfers between devices, on_device(): lax.all_to_all(totals.reshape(2 * n_zhi * chips, share, columns), ('zhi',...  8.22 us
    all_to_all x1, starting transfers between devices, on_device(): near = lax.all_to_all(copies, 'y', split_axis=0, concat_axis=0)  6.82 us
    pallas_call x1, Pallas kernels, on_device(): pl.pallas_call(functools.partial(grad_kernel, own, (n_y, n_zhi, n_x)), ou...  5.91 us
    all_to_all x1, starting transfers between devices, on_device(): lax.all_to_all(totals.reshape(2 * n_zhi * chips, share, columns), ('zhi',...  5.67 us
  transfers between devices with their start and end apart: 13, of which 5 were waited for; matrix products, arithmetic and copies ran while one was open for 2% of the time, Pallas kernels for 2%

profile of v9, /device:TPU:1, one launch (start us, length us, event | category | flops | bytes accessed | tf_op | source)
XLA Modules:
  0.0 127.2 jit_solution(9609223003364783297)
XLA Ops:
  0.6 1.1 broadcast_select_fusion.1
  1.7 8.8 %collective-permute-start = (bf16[128,768]{1,0:T(8,128)(2,1)S(1)}, bf16[128,768]{1,0:T(8,128)(2,1)S(1)}, u32[]{:S(2)}, u32[]{:S(2)}) collective-permute-start(bf16[128,768]{1,0:T(8,128)(2,1)S(1)} %get-tuple-element.19), channel_id=1, source_target_pairs={{0,64},{64,0},{1,65},{65,1},{2,66},{66,2},{3,67},{67,3},{4,68},{68... | collective-permute-start | bytes 589832 | tf_op jit(solution)/shard_map/ppermute | solution.py:125
  10.5 0.8 broadcast_select_fusion.2.own_ref
  11.2 0.0 copy-start.1
  11.2 5.3 %collective-permute-start.7 = (bf16[12,768]{1,0:T(8,128)(2,1)S(1)}, bf16[12,768]{1,0:T(8,128)(2,1)S(1)}, u32[]{:S(2)}, u32[]{:S(2)}) collective-permute-start(bf16[12,768]{1,0:T(8,128)(2,1)S(1)} %broadcast_select_fusion.2.own_ref), channel_id=1, source_target_pairs={{0,4},{4,0},{1,5},{5,1},{2,6},{6,2},{3,7},{7,3},{8,12},{12,8},{9,1... | collective-permute-start | bytes 55304 | tf_op jit(solution)/shard_map/ppermute | solution.py:122
  16.5 0.0 collective-permute-done
  16.6 3.1 %collective-permute-start.1 = (bf16[256,768]{1,0:T(8,128)(2,1)S(1)}, bf16[256,768]{1,0:T(8,128)(2,1)S(1)}, u32[]{:S(2)}, u32[]{:S(2)}) collective-permute-start(bf16[256,768]{1,0:T(8,128)(2,1)S(1)} %pad_maximum_fusion.x0), channel_id=1, source_target_pairs={{0,128},{128,256},{256,384},{1,129},{129,257},{257,385},{2,130},{1... | collective-permute-start | bytes 1179656 | tf_op jit(solution)/shard_map/ppermute | solution.py:23
  19.7 1.3 %collective-permute-start.4 = (bf16[256,768]{1,0:T(8,128)(2,1)S(1)}, bf16[256,768]{1,0:T(8,128)(2,1)S(1)}, u32[]{:S(2)}, u32[]{:S(2)}) collective-permute-start(bf16[256,768]{1,0:T(8,128)(2,1)S(1)} %pad_maximum_fusion.x0), channel_id=1, source_target_pairs={{128,0},{256,128},{384,256},{129,1},{257,129},{385,257},{130,2},{2... | collective-permute-start | bytes 1179656 | tf_op jit(solution)/shard_map/ppermute | solution.py:23
  21.0 0.0 collective-permute-done.7.other_ref
  21.0 0.0 copy-done.1
  21.0 0.0 copy-start.2
  21.0 0.6 copy-done.2
  21.6 1.5 %shard_map.94 = bf16[8,24,768]{2,1,0:T(8,128)(2,1)} custom-call(bf16[12,768]{1,0:T(8,128)(2,1)} %copy-done.1, bf16[12,768]{1,0:T(8,128)(2,1)} %copy-done.2), custom_call_target="tpu_custom_call" | custom-call | bytes 524288 | tf_op jit(solution)/shard_map/pallas_call | solution.py:137
  23.1 6.8 %all-to-all-start = ((bf16[8,24,768]{2,1,0:T(8,128)(2,1)}), bf16[8,24,768]{2,1,0:T(8,128)(2,1)S(1)}, u32[]{:S(2)}, u32[]{:S(2)}) async-start(bf16[8,24,768]{2,1,0:T(8,128)(2,1)} %shard_map.94), calls=%async_computation | async-start | bytes 589824 | tf_op jit(solution)/shard_map/all_to_all | solution.py:144
  29.9 0.0 collective-permute-done.1.up1
  29.9 4.8 %collective-permute-start.2 = (bf16[256,768]{1,0:T(8,128)(2,1)S(1)}, bf16[256,768]{1,0:T(8,128)(2,1)}, u32[]{:S(2)}, u32[]{:S(2)}) collective-permute-start(bf16[256,768]{1,0:T(8,128)(2,1)S(1)} %collective-permute-done.1.up1), channel_id=1, source_target_pairs={{0,128},{128,256},{256,384},{1,129},{129,257},{257,385},{2,130},{1... | collective-permute-start | bytes 1179656 | tf_op jit(solution)/shard_map/ppermute | solution.py:23
  34.7 4.0 %collective-permute-start.3 = (bf16[256,768]{1,0:T(8,128)(2,1)S(1)}, bf16[256,768]{1,0:T(8,128)(2,1)}, u32[]{:S(2)}, u32[]{:S(2)}) collective-permute-start(bf16[256,768]{1,0:T(8,128)(2,1)S(1)} %collective-permute-done.1.up1), channel_id=1, source_target_pairs={{0,256},{128,384},{1,257},{129,385},{2,258},{130,386},{3,259},{131... | collective-permute-start | bytes 1179656 | tf_op jit(solution)/shard_map/ppermute | solution.py:23
  38.7 0.0 collective-permute-done.4.down1
  38.7 1.3 %collective-permute-start.5 = (bf16[256,768]{1,0:T(8,128)(2,1)S(1)}, bf16[256,768]{1,0:T(8,128)(2,1)}, u32[]{:S(2)}, u32[]{:S(2)}) collective-permute-start(bf16[256,768]{1,0:T(8,128)(2,1)S(1)} %collective-permute-done.4.down1), channel_id=1, source_target_pairs={{128,0},{256,128},{384,256},{129,1},{257,129},{385,257},{130,2},{2... | collective-permute-start | bytes 1179656 | tf_op jit(solution)/shard_map/ppermute | solution.py:23
  40.0 1.3 %collective-permute-start.6 = (bf16[256,768]{1,0:T(8,128)(2,1)S(1)}, bf16[256,768]{1,0:T(8,128)(2,1)}, u32[]{:S(2)}, u32[]{:S(2)}) collective-permute-start(bf16[256,768]{1,0:T(8,128)(2,1)S(1)} %collective-permute-done.4.down1), channel_id=1, source_target_pairs={{256,0},{384,128},{257,1},{385,129},{258,2},{386,130},{259,3},{387... | collective-permute-start | bytes 1179656 | tf_op jit(solution)/shard_map/ppermute | solution.py:23
  41.3 0.0 all-to-all-done
  41.3 1.1 broadcast_in_dim.17
  42.4 4.0 %all-to-all-start.1 = ((bf16[4,192,768]{2,1,0:T(8,128)(2,1)}), bf16[4,192,768]{2,1,0:T(8,128)(2,1)S(1)}, u32[]{:S(2)}, u32[]{:S(2)}) async-start(bf16[4,192,768]{2,1,0:T(8,128)(2,1)} %broadcast_in_dim.17), calls=%async_computation.1 | async-start | bytes 2359296 | tf_op jit(solution)/shard_map/all_to_all | solution.py:29
  46.4 0.3 fusion.order_ref
  46.7 0.0 collective-permute-done.2.up2_ref.up2
  46.7 2.9 %collective-permute-done.3.up3_ref.up3 = bf16[256,768]{1,0:T(8,128)(2,1)} collective-permute-done((bf16[256,768]{1,0:T(8,128)(2,1)S(1)}, bf16[256,768]{1,0:T(8,128)(2,1)}, u32[]{:S(2)}, u32[]{:S(2)}) %collective-permute-start.3) | collective-permute-done | bytes 393248 | tf_op jit(solution)/shard_map/ppermute | solution.py:23
  49.7 0.0 collective-permute-done.5.down2_ref.down2
  49.7 16.2 %collective-permute-done.6.down3_ref.down3 = bf16[256,768]{1,0:T(8,128)(2,1)} collective-permute-done((bf16[256,768]{1,0:T(8,128)(2,1)S(1)}, bf16[256,768]{1,0:T(8,128)(2,1)}, u32[]{:S(2)}, u32[]{:S(2)}) %collective-permute-start.6) | collective-permute-done | bytes 393248 | tf_op jit(solution)/shard_map/ppermute | solution.py:23
  65.8 0.6 shard_map.93.arrived_ref
  66.4 0.0 all-to-all-done.1
  66.4 0.0 copy-start
  66.4 0.7 copy-done
  67.1 3.9 %shard_map.95 = (bf16[1024,768]{1,0:T(8,128)(2,1)S(1)}, f32[1024,768]{1,0:T(8,128)S(1)}, f32[1024,1]{1,0:T(8,128)S(1)}, bf16[1024,768]{1,0:T(8,128)(2,1)S(1)}) custom-call(s32[1]{0:T(128)} %bitcast.place, f32[8,128]{1,0:T(8,128)S(1)} %copy-done, bf16[768,768]{1,0:T(8,128)(2,1)S(1)} %fusion.order_ref, bf16[768,768]{1,0:T(8,128)(2,1)S(1)} %bitcast.8, ...), custom_call_target="tpu_custom_call" | custom-call | flops 2113929216 | bytes 8388608 | tf_op jit(solution)/shard_map/pallas_call | solution.py:154
  71.0 4.2 %collective-permute-start.8 = (bf16[1024,768]{1,0:T(8,128)(2,1)S(1)}, bf16[1024,768]{1,0:T(8,128)(2,1)S(1)}, u32[]{:S(2)}, u32[]{:S(2)}) collective-permute-start(bf16[1024,768]{1,0:T(8,128)(2,1)S(1)} %get-tuple-element.10.half_ref), channel_id=1, source_target_pairs={{0,64},{64,0},{1,65},{65,1},{2,66},{66,2},{3,67},{67,3},{4,68},{68... | collective-permute-start | bytes 4718600 | tf_op jit(solution)/shard_map/ppermute | solution.py:170
  76.6 0.1 pad_maximum_fusion.1.scalars
  76.6 1.6 %collective-permute-done.8.partner_ref = bf16[1024,768]{1,0:T(8,128)(2,1)S(1)} collective-permute-done((bf16[1024,768]{1,0:T(8,128)(2,1)S(1)}, bf16[1024,768]{1,0:T(8,128)(2,1)S(1)}, u32[]{:S(2)}, u32[]{:S(2)}) %collective-permute-start.8) | collective-permute-done | bytes 1572896 | tf_op jit(solution)/shard_map/ppermute | solution.py:170
  78.3 5.9 %shard_map.96 = (bf16[32,24,192]{2,1,0:T(8,128)(2,1)S(1)}, f32[256,1]{1,0:T(8,128)S(1)}) custom-call(f32[2]{0:T(128)S(1)} %pad_maximum_fusion.1.scalars, s32[1]{0:T(128)} %bitcast.place, bf16[1024,768]{1,0:T(8,128)(2,1)S(1)} %get-tuple-element.10.half_ref, bf16[1024,768]{1,0:T(8,128)(2,1)S(1)} %collective-permute-done.8.partner_ref, ...), custom_call_target="tpu_custom_call" | custom-call | flops 3221225472 | bytes 8388608 | tf_op jit(solution)/shard_map/pallas_call | solution.py:172
  84.2 23.2 %all_to_all.20 = bf16[32,24,192]{2,1,0:T(8,128)(2,1)S(1)} all-to-all(bf16[32,24,192]{2,1,0:T(8,128)(2,1)S(1)} %get-tuple-element.14), channel_id=1, replica_groups=mesh['zlo'=4,'core'=2,'y'=8,'zhi'=2,'x'=4] {'y','x'}, dimensions={0} | all-to-all | bytes 589824 | tf_op jit(solution)/shard_map/all_to_all | solution.py:194
  107.4 0.1 convert_reduce_fusion
  107.4 0.7 broadcast_in_dim.19
  108.2 5.7 %all-to-all-start.3 = ((f32[16,12,192]{2,1,0:T(8,128)}), f32[16,12,192]{2,1,0:T(8,128)S(1)}, u32[]{:S(2)}, u32[]{:S(2)}) async-start(f32[16,12,192]{2,1,0:T(8,128)} %bitcast.3), calls=%async_computation.3 | async-start | bytes 524288 | tf_op jit(solution)/shard_map/all_to_all | solution.py:197
  113.8 0.1 slice_reduce_fusion
  113.9 2.1 %collective-permute-start.9 = (f32[128]{0:T(128)S(1)}, f32[128]{0:T(128)S(1)}, u32[]{:S(2)}, u32[]{:S(2)}) collective-permute-start(f32[128]{0:T(128)S(1)} %get-tuple-element.16), channel_id=1, source_target_pairs={{0,64},{64,0},{1,65},{65,1},{2,66},{66,2},{3,67},{67,3},{4,68},{68... | collective-permute-start | bytes 1544 | tf_op jit(solution)/shard_map/ppermute | solution.py:208
  116.1 0.9 collective-permute-done.9
  117.0 0.5 broadcast_select_fusion.3
  117.5 8.2 %all-to-all-done.3 = f32[16,12,192]{2,1,0:T(8,128)S(1)} async-done(((f32[16,12,192]{2,1,0:T(8,128)}), f32[16,12,192]{2,1,0:T(8,128)S(1)}, u32[]{:S(2)}, u32[]{:S(2)}) %all-to-all-start.3) | async-done | bytes 147488 | tf_op jit(solution)/shard_map/all_to_all | solution.py:197
  125.7 0.1 copy.18
  125.8 0.7 squeeze.6
  126.5 0.7 squeeze.7
  (5 shorter events, 0.1 us)
Async XLA Ops:
  1.7 14.8 %collective-permute-start = (bf16[128,768]{1,0:T(8,128)(2,1)S(1)}, bf16[128,768]{1,0:T(8,128)(2,1)S(1)}, u32[]{:S(2)}, u32[]{:S(2)}) collective-permute-start(bf16[128,768]{1,0:T(8,128)(2,1)S(1)} %get-tuple-element.19), channel_id=1, source_target_pairs={{0,64},{64,0},{1,65},{65,1},{2,66},{66,2},{3,67},{67,3},{4,68},{68... | collective-permute-start | bytes 589832 | tf_op jit(solution)/shard_map/ppermute | solution.py:125
  11.2 9.7 %copy-start.1 = (bf16[12,768]{1,0:T(8,128)(2,1)}, bf16[12,768]{1,0:T(8,128)(2,1)S(1)}, u32[]{:S(2)}) copy-start(bf16[12,768]{1,0:T(8,128)(2,1)S(1)} %broadcast_select_fusion.2.own_ref) | copy-start | bytes 55300
  11.2 9.7 %collective-permute-start.7 = (bf16[12,768]{1,0:T(8,128)(2,1)S(1)}, bf16[12,768]{1,0:T(8,128)(2,1)S(1)}, u32[]{:S(2)}, u32[]{:S(2)}) collective-permute-start(bf16[12,768]{1,0:T(8,128)(2,1)S(1)} %broadcast_select_fusion.2.own_ref), channel_id=1, source_target_pairs={{0,4},{4,0},{1,5},{5,1},{2,6},{6,2},{3,7},{7,3},{8,12},{12,8},{9,1... | collective-permute-start | bytes 55304 | tf_op jit(solution)/shard_map/ppermute | solution.py:122
  16.6 13.4 %collective-permute-start.1 = (bf16[256,768]{1,0:T(8,128)(2,1)S(1)}, bf16[256,768]{1,0:T(8,128)(2,1)S(1)}, u32[]{:S(2)}, u32[]{:S(2)}) collective-permute-start(bf16[256,768]{1,0:T(8,128)(2,1)S(1)} %pad_maximum_fusion.x0), channel_id=1, source_target_pairs={{0,128},{128,256},{256,384},{1,129},{129,257},{257,385},{2,130},{1... | collective-permute-start | bytes 1179656 | tf_op jit(solution)/shard_map/ppermute | solution.py:23
  19.7 19.0 %collective-permute-start.4 = (bf16[256,768]{1,0:T(8,128)(2,1)S(1)}, bf16[256,768]{1,0:T(8,128)(2,1)S(1)}, u32[]{:S(2)}, u32[]{:S(2)}) collective-permute-start(bf16[256,768]{1,0:T(8,128)(2,1)S(1)} %pad_maximum_fusion.x0), channel_id=1, source_target_pairs={{128,0},{256,128},{384,256},{129,1},{257,129},{385,257},{130,2},{2... | collective-permute-start | bytes 1179656 | tf_op jit(solution)/shard_map/ppermute | solution.py:23
  21.0 0.6 copy-start.2
  23.1 18.2 %all-to-all-start = ((bf16[8,24,768]{2,1,0:T(8,128)(2,1)}), bf16[8,24,768]{2,1,0:T(8,128)(2,1)S(1)}, u32[]{:S(2)}, u32[]{:S(2)}) async-start(bf16[8,24,768]{2,1,0:T(8,128)(2,1)} %shard_map.94), calls=%async_computation | async-start | bytes 589824 | tf_op jit(solution)/shard_map/all_to_all | solution.py:144
  29.9 16.8 %collective-permute-start.2 = (bf16[256,768]{1,0:T(8,128)(2,1)S(1)}, bf16[256,768]{1,0:T(8,128)(2,1)}, u32[]{:S(2)}, u32[]{:S(2)}) collective-permute-start(bf16[256,768]{1,0:T(8,128)(2,1)S(1)} %collective-permute-done.1.up1), channel_id=1, source_target_pairs={{0,128},{128,256},{256,384},{1,129},{129,257},{257,385},{2,130},{1... | collective-permute-start | bytes 1179656 | tf_op jit(solution)/shard_map/ppermute | solution.py:23
  34.7 15.0 %collective-permute-start.3 = (bf16[256,768]{1,0:T(8,128)(2,1)S(1)}, bf16[256,768]{1,0:T(8,128)(2,1)}, u32[]{:S(2)}, u32[]{:S(2)}) collective-permute-start(bf16[256,768]{1,0:T(8,128)(2,1)S(1)} %collective-permute-done.1.up1), channel_id=1, source_target_pairs={{0,256},{128,384},{1,257},{129,385},{2,258},{130,386},{3,259},{131... | collective-permute-start | bytes 1179656 | tf_op jit(solution)/shard_map/ppermute | solution.py:23
  38.7 11.0 %collective-permute-start.5 = (bf16[256,768]{1,0:T(8,128)(2,1)S(1)}, bf16[256,768]{1,0:T(8,128)(2,1)}, u32[]{:S(2)}, u32[]{:S(2)}) collective-permute-start(bf16[256,768]{1,0:T(8,128)(2,1)S(1)} %collective-permute-done.4.down1), channel_id=1, source_target_pairs={{128,0},{256,128},{384,256},{129,1},{257,129},{385,257},{130,2},{2... | collective-permute-start | bytes 1179656 | tf_op jit(solution)/shard_map/ppermute | solution.py:23
  40.0 25.8 %collective-permute-start.6 = (bf16[256,768]{1,0:T(8,128)(2,1)S(1)}, bf16[256,768]{1,0:T(8,128)(2,1)}, u32[]{:S(2)}, u32[]{:S(2)}) collective-permute-start(bf16[256,768]{1,0:T(8,128)(2,1)S(1)} %collective-permute-done.4.down1), channel_id=1, source_target_pairs={{256,0},{384,128},{257,1},{385,129},{258,2},{386,130},{259,3},{387... | collective-permute-start | bytes 1179656 | tf_op jit(solution)/shard_map/ppermute | solution.py:23
  42.4 24.0 %all-to-all-start.1 = ((bf16[4,192,768]{2,1,0:T(8,128)(2,1)}), bf16[4,192,768]{2,1,0:T(8,128)(2,1)S(1)}, u32[]{:S(2)}, u32[]{:S(2)}) async-start(bf16[4,192,768]{2,1,0:T(8,128)(2,1)} %broadcast_in_dim.17), calls=%async_computation.1 | async-start | bytes 2359296 | tf_op jit(solution)/shard_map/all_to_all | solution.py:29
  66.4 0.7 copy-start
  71.0 7.3 %collective-permute-start.8 = (bf16[1024,768]{1,0:T(8,128)(2,1)S(1)}, bf16[1024,768]{1,0:T(8,128)(2,1)S(1)}, u32[]{:S(2)}, u32[]{:S(2)}) collective-permute-start(bf16[1024,768]{1,0:T(8,128)(2,1)S(1)} %get-tuple-element.10.half_ref), channel_id=1, source_target_pairs={{0,64},{64,0},{1,65},{65,1},{2,66},{66,2},{3,67},{67,3},{4,68},{68... | collective-permute-start | bytes 4718600 | tf_op jit(solution)/shard_map/ppermute | solution.py:170
  108.2 17.5 %all-to-all-start.3 = ((f32[16,12,192]{2,1,0:T(8,128)}), f32[16,12,192]{2,1,0:T(8,128)S(1)}, u32[]{:S(2)}, u32[]{:S(2)}) async-start(f32[16,12,192]{2,1,0:T(8,128)} %bitcast.3), calls=%async_computation.3 | async-start | bytes 524288 | tf_op jit(solution)/shard_map/all_to_all | solution.py:197
  113.9 3.0 %collective-permute-start.9 = (f32[128]{0:T(128)S(1)}, f32[128]{0:T(128)S(1)}, u32[]{:S(2)}, u32[]{:S(2)}) collective-permute-start(f32[128]{0:T(128)S(1)} %get-tuple-element.16), channel_id=1, source_target_pairs={{0,64},{64,0},{1,65},{65,1},{2,66},{66,2},{3,67},{67,3},{4,68},{68... | collective-permute-start | bytes 1544 | tf_op jit(solution)/shard_map/ppermute | solution.py:208

commit v10 on v9

--- a/solution.py
+++ b/solution.py
@@ -18,9 +18,8 @@
 PARAMS = pltpu.CompilerParams(vmem_limit_bytes=40 * 1024 * 1024)
 
 
-def passed_on(value, axis, by):
-    count = lax.axis_size(axis)
-    return lax.ppermute(value, axis, [(i, i + by) for i in range(count) if 0 <= i + by < count])
+def passed_on(value, *hops):
+    return lax.ppermute(value, "zlo", hops)
 
 
 def spread(value, axis):
@@ -36,18 +35,18 @@
         out_ref[k, share:] = other_ref[...]
 
 
-def arrived_kernel(up2_ref, up3_ref, down2_ref, down3_ref, out_ref):
+def arrived_kernel(far_ref, up_ref, down_ref, out_ref):
     out_ref[...] = jnp.zeros_like(out_ref)
 
 
 def embed_kernel(
-    place, arrived_ref, order_ref, gathered_ref, x0, up1, up2, up3, down1, down2, down3,
+    place, arrived_ref, order_ref, gathered_ref, x0, up1, up2, far, down1, down2,
     half_ref, unit_ref, radius_ref, rows_ref, mapping,
 ):
     mapping[...] = jnp.dot(
         order_ref[...], gathered_ref[...], preferred_element_type=F32
     ).astype(BF16)
-    blocks = ((x0, None), (up1, down3), (up2, down2), (up3, down1))
+    blocks = ((x0, None), (up1, far), (up2, down2), (far, down1))
     for k, (low, high) in enumerate(blocks):
         rows = low.shape[0]
         at = pl.ds(k * rows, rows)
@@ -123,23 +122,26 @@
     mine = jnp.where(first, picture_inputs, caption_inputs)
     sent = jnp.where(first, caption_inputs, picture_inputs)
     chunk = jnp.concatenate([mine, lax.ppermute(sent, "core", SWAP)], axis=0)
-    up1, down1 = passed_on(chunk, "zlo", 1), passed_on(chunk, "zlo", -1)
-    up = [chunk, up1] + [passed_on(up1, "zlo", k) for k in range(1, chips - 1)]
-    down = [chunk, down1] + [passed_on(down1, "zlo", -k) for k in range(1, chips - 1)]
+    at_line = lax.axis_index("zlo")
+    up1 = passed_on(chunk, (0, 1), (1, 2), (2, 3))
+    down1 = passed_on(chunk, (1, 0), (2, 1), (3, 2))
+    far = passed_on(jnp.where(at_line == 1, up1, down1), (1, 3), (2, 0))
+    up2 = passed_on(up1, (1, 2), (2, 3))
+    down2 = passed_on(down1, (1, 0), (2, 1))
     arrived = pl.pallas_call(
         arrived_kernel,
         out_shape=jax.ShapeDtypeStruct((8, 128), F32),
-        in_specs=[ANY] * 4,
+        in_specs=[ANY] * 3,
         out_specs=VMEM,
         cost_estimate=pl.CostEstimate(flops=ARRIVED, bytes_accessed=2**12, transcendentals=0),
-    )(*up[2:], *down[2:])
-    at_chip = lax.axis_index("zlo").astype(jnp.int32).reshape(1)
+    )(far, up2, down2)
+    at_chip = at_line.astype(jnp.int32).reshape(1)
     copies = pl.pallas_call(
         copies_kernel,
         out_shape=jax.ShapeDtypeStruct((n_y, n_zhi * share, embed), BF16),
         in_specs=[VMEM] * 2,
         out_specs=VMEM,
-        cost_estimate=pl.CostEstimate(flops=0, bytes_accessed=2**19, transcendentals=0),
+        cost_estimate=pl.CostEstimate(flops=4 * 10**9, bytes_accessed=2**19, transcendentals=0),
     )(piece, other)
     near = lax.all_to_all(copies, "y", split_axis=0, concat_axis=0)
     near = near.reshape(n_y * n_zhi * share, embed)
@@ -159,14 +161,16 @@
             jax.ShapeDtypeStruct((rows, 1), F32),
             jax.ShapeDtypeStruct((rows, width), BF16),
         ),
-        in_specs=[SMEM, ANY] + [VMEM] * 9,
+        in_specs=[SMEM, ANY] + [VMEM] * 8,
         out_specs=(VMEM,) * 4,
         scratch_shapes=[pltpu.VMEM((width, embed), BF16)],
         compiler_params=PARAMS,
         cost_estimate=pl.CostEstimate(
             flops=2 * (rows + width) * width * embed, bytes_accessed=8 * 2**20, transcendentals=0
         ),
-    )(at_chip, arrived, order, gathered, *up, *down[1:])
+    )(
+        at_chip, arrived, order, gathered, chunk, up1, up2, far, down1, down2
+    )
     partner = lax.ppermute(half, "core", SWAP)
     columns = embed // chips
     local, norms = pl.pallas_call(

time: 128 us -> 122 us (0.953)
  blocking collectives: 23.2 us -> 17.1 us
    ppermute x6 -> x5, waiting for transfers between devices: 19.1 us -> 9.65 us  [passed_on(): return lax.ppermute(value, 'zlo', hops)]
    ppermute x6 -> x5, starting transfers between devices: 15.7 us -> 8.38 us  [passed_on(): return lax.ppermute(value, 'zlo', hops)]
    all_to_all x1, blocking collectives: 23.2 us -> 17.1 us  [on_device(): lax.all_to_all(local, ('y', 'x'), split_axis=0, concat_axis=0, tiled=True)]
    all_to_all x1, starting transfers between devices: 5.67 us -> 11.4 us  [on_device(): lax.all_to_all(totals.reshape(2 * n_zhi * chips, share, columns), ('zhi',...]
    all_to_all x1, waiting for transfers between devices: 0.01 us -> 5.25 us  [spread(): return lax.all_to_all(copies, axis, split_axis=0, concat_axis=0)]
    all_to_all x1, waiting for transfers between devices: 0.01 us -> 4.78 us  [on_device(): near = lax.all_to_all(copies, 'y', split_axis=0, concat_axis=0)]
  transfers between devices with their start and end apart: 13 -> 12, of which waited for: 5 -> 7; matrix products, arithmetic and copies ran while one was open for 2% -> 3% of each run, Pallas kernels for 2% -> 2%
where the time goes in v10:
time: 122 us
  starting transfers between devices  52 us (43%)
  waiting for transfers between devices  30.4 us (25%)
  blocking collectives  17.1 us (14%)
  Pallas kernels  11.8 us (10%)
  local copies, waits for them, and re-layouts  4.74 us (4%)
  other arithmetic  3.6 us (3%)
  between operations  2.12 us (2%)
    all_to_all x1, blocking collectives, on_device(): lax.all_to_all(local, ('y', 'x'), split_axis=0, concat_axis=0, tiled=True)  17.1 us
    all_to_all x1, starting transfers between devices, on_device(): lax.all_to_all(totals.reshape(2 * n_zhi * chips, share, columns), ('zhi',...  11.4 us
    ppermute x5, waiting for transfers between devices, passed_on(): return lax.ppermute(value, 'zlo', hops)  9.65 us
    ppermute x1, starting transfers between devices, on_device(): chunk = jnp.concatenate([mine, lax.ppermute(sent, 'core', SWAP)], axis=0)  8.79 us
    ppermute x5, starting transfers between devices, passed_on(): return lax.ppermute(value, 'zlo', hops)  8.38 us
    all_to_all x1, waiting for transfers between devices, on_device(): lax.all_to_all(totals.reshape(2 * n_zhi * chips, share, columns), ('zhi',...  8.07 us
    all_to_all x1, starting transfers between devices, on_device(): near = lax.all_to_all(copies, 'y', split_axis=0, concat_axis=0)  6.82 us
    pallas_call x1, Pallas kernels, on_device(): pl.pallas_call(functools.partial(grad_kernel, own, (n_y, n_zhi, n_x)), ou...  5.91 us
  transfers between devices with their start and end apart: 12, of which 7 were waited for; matrix products, arithmetic and copies ran while one was open for 3% of the time, Pallas kernels for 2%

profile of v10, /device:TPU:1, one launch (start us, length us, event | category | flops | bytes accessed | tf_op | source)
XLA Modules:
  0.0 121.7 jit_solution(4886310137503441163)
XLA Ops:
  0.6 1.1 broadcast_select_fusion.2
  1.7 8.8 %collective-permute-start = (bf16[128,768]{1,0:T(8,128)(2,1)S(1)}, bf16[128,768]{1,0:T(8,128)(2,1)S(1)}, u32[]{:S(2)}, u32[]{:S(2)}) collective-permute-start(bf16[128,768]{1,0:T(8,128)(2,1)S(1)} %get-tuple-element.19), channel_id=1, source_target_pairs={{0,64},{64,0},{1,65},{65,1},{2,66},{66,2},{3,67},{67,3},{4,68},{68... | collective-permute-start | bytes 589832 | tf_op jit(solution)/shard_map/ppermute | solution.py:124
  10.5 0.8 broadcast_select_fusion.3.own_ref
  11.2 0.0 copy-start.1
  11.2 5.3 %collective-permute-start.6 = (bf16[12,768]{1,0:T(8,128)(2,1)S(1)}, bf16[12,768]{1,0:T(8,128)(2,1)S(1)}, u32[]{:S(2)}, u32[]{:S(2)}) collective-permute-start(bf16[12,768]{1,0:T(8,128)(2,1)S(1)} %broadcast_select_fusion.3.own_ref), channel_id=1, source_target_pairs={{0,4},{4,0},{1,5},{5,1},{2,6},{6,2},{3,7},{7,3},{8,12},{12,8},{9,1... | collective-permute-start | bytes 55304 | tf_op jit(solution)/shard_map/ppermute | solution.py:121
  16.5 0.0 collective-permute-done
  16.6 3.1 %collective-permute-start.1 = (bf16[256,768]{1,0:T(8,128)(2,1)S(1)}, bf16[256,768]{1,0:T(8,128)(2,1)S(1)}, u32[]{:S(2)}, u32[]{:S(2)}) collective-permute-start(bf16[256,768]{1,0:T(8,128)(2,1)S(1)} %pad_maximum_fusion.x0), channel_id=1, source_target_pairs={{0,128},{128,256},{256,384},{1,129},{129,257},{257,385},{2,130},{1... | collective-permute-start | bytes 1179656 | tf_op jit(solution)/shard_map/ppermute | solution.py:22
  19.7 1.3 %collective-permute-start.2 = (bf16[256,768]{1,0:T(8,128)(2,1)S(1)}, bf16[256,768]{1,0:T(8,128)(2,1)S(1)}, u32[]{:S(2)}, u32[]{:S(2)}) collective-permute-start(bf16[256,768]{1,0:T(8,128)(2,1)S(1)} %pad_maximum_fusion.x0), channel_id=1, source_target_pairs={{128,0},{256,128},{384,256},{129,1},{257,129},{385,257},{130,2},{2... | collective-permute-start | bytes 1179656 | tf_op jit(solution)/shard_map/ppermute | solution.py:22
  21.0 0.0 collective-permute-done.6.other_ref
  21.0 0.0 copy-done.1
  21.0 0.0 copy-start.2
  21.0 0.6 copy-done.2
  21.6 1.5 %shard_map.94 = bf16[8,24,768]{2,1,0:T(8,128)(2,1)} custom-call(bf16[12,768]{1,0:T(8,128)(2,1)} %copy-done.1, bf16[12,768]{1,0:T(8,128)(2,1)} %copy-done.2), custom_call_target="tpu_custom_call" | custom-call | flops 4000000000 | bytes 524288 | tf_op jit(solution)/shard_map/pallas_call | solution.py:139
  23.1 6.8 %all-to-all-start = ((bf16[8,24,768]{2,1,0:T(8,128)(2,1)}), bf16[8,24,768]{2,1,0:T(8,128)(2,1)S(1)}, u32[]{:S(2)}, u32[]{:S(2)}) async-start(bf16[8,24,768]{2,1,0:T(8,128)(2,1)} %shard_map.94), calls=%async_computation | async-start | bytes 589824 | tf_op jit(solution)/shard_map/all_to_all | solution.py:146
  29.9 0.0 collective-permute-done.1.up1
  29.9 1.7 %collective-permute-done.2.down1 = bf16[256,768]{1,0:T(8,128)(2,1)S(1)} collective-permute-done((bf16[256,768]{1,0:T(8,128)(2,1)S(1)}, bf16[256,768]{1,0:T(8,128)(2,1)S(1)}, u32[]{:S(2)}, u32[]{:S(2)}) %collective-permute-start.2) | collective-permute-done | bytes 393248 | tf_op jit(solution)/shard_map/ppermute | solution.py:22
  31.7 0.8 broadcast_select_fusion
  32.5 1.3 %collective-permute-start.3 = (bf16[256,768]{1,0:T(8,128)(2,1)}, bf16[256,768]{1,0:T(8,128)(2,1)}, u32[]{:S(2)}, u32[]{:S(2)}) collective-permute-start(bf16[256,768]{1,0:T(8,128)(2,1)} %broadcast_select_fusion), channel_id=1, source_target_pairs={{128,384},{256,0},{129,385},{257,1},{130,386},{258,2},{131,387},{2... | collective-permute-start | bytes 1179656 | tf_op jit(solution)/shard_map/ppermute | solution.py:22
  33.7 1.4 %collective-permute-start.4 = (bf16[256,768]{1,0:T(8,128)(2,1)S(1)}, bf16[256,768]{1,0:T(8,128)(2,1)}, u32[]{:S(2)}, u32[]{:S(2)}) collective-permute-start(bf16[256,768]{1,0:T(8,128)(2,1)S(1)} %collective-permute-done.1.up1), channel_id=1, source_target_pairs={{128,256},{256,384},{129,257},{257,385},{130,258},{258,386},{131,2... | collective-permute-start | bytes 1179656 | tf_op jit(solution)/shard_map/ppermute | solution.py:22
  35.2 1.3 %collective-permute-start.5 = (bf16[256,768]{1,0:T(8,128)(2,1)S(1)}, bf16[256,768]{1,0:T(8,128)(2,1)}, u32[]{:S(2)}, u32[]{:S(2)}) collective-permute-start(bf16[256,768]{1,0:T(8,128)(2,1)S(1)} %collective-permute-done.2.down1), channel_id=1, source_target_pairs={{128,0},{256,128},{129,1},{257,129},{130,2},{258,130},{131,3},{259... | collective-permute-start | bytes 1179656 | tf_op jit(solution)/shard_map/ppermute | solution.py:22
  36.5 4.8 %all-to-all-done = bf16[8,24,768]{2,1,0:T(8,128)(2,1)S(1)} async-done(((bf16[8,24,768]{2,1,0:T(8,128)(2,1)}), bf16[8,24,768]{2,1,0:T(8,128)(2,1)S(1)}, u32[]{:S(2)}, u32[]{:S(2)}) %all-to-all-start) | async-done | bytes 294944 | tf_op jit(solution)/shard_map/all_to_all | solution.py:146
  41.3 1.1 broadcast_in_dim.17
  42.4 4.0 %all-to-all-start.1 = ((bf16[4,192,768]{2,1,0:T(8,128)(2,1)}), bf16[4,192,768]{2,1,0:T(8,128)(2,1)S(1)}, u32[]{:S(2)}, u32[]{:S(2)}) async-start(bf16[4,192,768]{2,1,0:T(8,128)(2,1)} %broadcast_in_dim.17), calls=%async_computation.1 | async-start | bytes 2359296 | tf_op jit(solution)/shard_map/all_to_all | solution.py:28
  46.4 0.3 fusion.order_ref
  46.6 0.0 collective-permute-done.3.far_ref.far
  46.7 0.0 collective-permute-done.4.up_ref.up2
  46.7 7.9 %collective-permute-done.5.down_ref.down2 = bf16[256,768]{1,0:T(8,128)(2,1)} collective-permute-done((bf16[256,768]{1,0:T(8,128)(2,1)S(1)}, bf16[256,768]{1,0:T(8,128)(2,1)}, u32[]{:S(2)}, u32[]{:S(2)}) %collective-permute-start.5) | collective-permute-done | bytes 393248 | tf_op jit(solution)/shard_map/ppermute | solution.py:22
  54.6 0.6 shard_map.93.arrived_ref
  55.2 5.3 %all-to-all-done.1 = bf16[4,192,768]{2,1,0:T(8,128)(2,1)S(1)} async-done(((bf16[4,192,768]{2,1,0:T(8,128)(2,1)}), bf16[4,192,768]{2,1,0:T(8,128)(2,1)S(1)}, u32[]{:S(2)}, u32[]{:S(2)}) %all-to-all-start.1) | async-done | bytes 1179680 | tf_op jit(solution)/shard_map/all_to_all | solution.py:28
  60.4 0.0 copy-start
  60.4 0.7 copy-done
  61.1 3.8 %shard_map.95 = (bf16[1024,768]{1,0:T(8,128)(2,1)S(1)}, f32[1024,768]{1,0:T(8,128)S(1)}, f32[1024,1]{1,0:T(8,128)S(1)}, bf16[1024,768]{1,0:T(8,128)(2,1)S(1)}) custom-call(s32[1]{0:T(128)} %bitcast.place, f32[8,128]{1,0:T(8,128)S(1)} %copy-done, bf16[768,768]{1,0:T(8,128)(2,1)S(1)} %fusion.order_ref, bf16[768,768]{1,0:T(8,128)(2,1)S(1)} %bitcast.8, ...), custom_call_target="tpu_custom_call" | custom-call | flops 2113929216 | bytes 8388608 | tf_op jit(solution)/shard_map/pallas_call | solution.py:156
  64.9 5.3 %collective-permute-start.7 = (bf16[1024,768]{1,0:T(8,128)(2,1)S(1)}, bf16[1024,768]{1,0:T(8,128)(2,1)S(1)}, u32[]{:S(2)}, u32[]{:S(2)}) collective-permute-start(bf16[1024,768]{1,0:T(8,128)(2,1)S(1)} %get-tuple-element.10.half_ref), channel_id=1, source_target_pairs={{0,64},{64,0},{1,65},{65,1},{2,66},{66,2},{3,67},{67,3},{4,68},{68... | collective-permute-start | bytes 4718600 | tf_op jit(solution)/shard_map/ppermute | solution.py:174
  71.5 0.1 pad_maximum_fusion.1.scalars
  71.6 1.6 %collective-permute-done.7.partner_ref = bf16[1024,768]{1,0:T(8,128)(2,1)S(1)} collective-permute-done((bf16[1024,768]{1,0:T(8,128)(2,1)S(1)}, bf16[1024,768]{1,0:T(8,128)(2,1)S(1)}, u32[]{:S(2)}, u32[]{:S(2)}) %collective-permute-start.7) | collective-permute-done | bytes 1572896 | tf_op jit(solution)/shard_map/ppermute | solution.py:174
  73.2 5.9 %shard_map.96 = (bf16[32,24,192]{2,1,0:T(8,128)(2,1)S(1)}, f32[256,1]{1,0:T(8,128)S(1)}) custom-call(f32[2]{0:T(128)S(1)} %pad_maximum_fusion.1.scalars, s32[1]{0:T(128)} %bitcast.place, bf16[1024,768]{1,0:T(8,128)(2,1)S(1)} %get-tuple-element.10.half_ref, bf16[1024,768]{1,0:T(8,128)(2,1)S(1)} %collective-permute-done.7.partner_ref, ...), custom_call_target="tpu_custom_call" | custom-call | flops 3221225472 | bytes 8388608 | tf_op jit(solution)/shard_map/pallas_call | solution.py:176
  79.2 17.1 %all_to_all.20 = bf16[32,24,192]{2,1,0:T(8,128)(2,1)S(1)} all-to-all(bf16[32,24,192]{2,1,0:T(8,128)(2,1)S(1)} %get-tuple-element.14), channel_id=1, replica_groups=mesh['zlo'=4,'core'=2,'y'=8,'zhi'=2,'x'=4] {'y','x'}, dimensions={0} | all-to-all | bytes 589824 | tf_op jit(solution)/shard_map/all_to_all | solution.py:198
  96.2 0.1 convert_reduce_fusion
  96.3 0.7 broadcast_in_dim.19
  97.0 11.4 %all-to-all-start.3 = ((f32[16,12,192]{2,1,0:T(8,128)}), f32[16,12,192]{2,1,0:T(8,128)S(1)}, u32[]{:S(2)}, u32[]{:S(2)}) async-start(f32[16,12,192]{2,1,0:T(8,128)} %bitcast.3), calls=%async_computation.3 | async-start | bytes 524288 | tf_op jit(solution)/shard_map/all_to_all | solution.py:201
  108.4 0.1 slice_reduce_fusion
  108.5 2.0 %collective-permute-start.8 = (f32[128]{0:T(128)S(1)}, f32[128]{0:T(128)S(1)}, u32[]{:S(2)}, u32[]{:S(2)}) collective-permute-start(f32[128]{0:T(128)S(1)} %get-tuple-element.16), channel_id=1, source_target_pairs={{0,64},{64,0},{1,65},{65,1},{2,66},{66,2},{3,67},{67,3},{4,68},{68... | collective-permute-start | bytes 1544 | tf_op jit(solution)/shard_map/ppermute | solution.py:212
  110.5 1.0 collective-permute-done.8
  111.5 0.5 broadcast_select_fusion.4
  112.1 8.1 %all-to-all-done.3 = f32[16,12,192]{2,1,0:T(8,128)S(1)} async-done(((f32[16,12,192]{2,1,0:T(8,128)}), f32[16,12,192]{2,1,0:T(8,128)S(1)}, u32[]{:S(2)}, u32[]{:S(2)}) %all-to-all-start.3) | async-done | bytes 147488 | tf_op jit(solution)/shard_map/all_to_all | solution.py:201
  120.2 0.1 copy.18
  120.2 0.7 squeeze.6
  121.0 0.7 squeeze.7
  (5 shorter events, 0.1 us)
Async XLA Ops:
  1.7 14.8 %collective-permute-start = (bf16[128,768]{1,0:T(8,128)(2,1)S(1)}, bf16[128,768]{1,0:T(8,128)(2,1)S(1)}, u32[]{:S(2)}, u32[]{:S(2)}) collective-permute-start(bf16[128,768]{1,0:T(8,128)(2,1)S(1)} %get-tuple-element.19), channel_id=1, source_target_pairs={{0,64},{64,0},{1,65},{65,1},{2,66},{66,2},{3,67},{67,3},{4,68},{68... | collective-permute-start | bytes 589832 | tf_op jit(solution)/shard_map/ppermute | solution.py:124
  11.2 9.7 %copy-start.1 = (bf16[12,768]{1,0:T(8,128)(2,1)}, bf16[12,768]{1,0:T(8,128)(2,1)S(1)}, u32[]{:S(2)}) copy-start(bf16[12,768]{1,0:T(8,128)(2,1)S(1)} %broadcast_select_fusion.3.own_ref) | copy-start | bytes 55300
  11.2 9.7 %collective-permute-start.6 = (bf16[12,768]{1,0:T(8,128)(2,1)S(1)}, bf16[12,768]{1,0:T(8,128)(2,1)S(1)}, u32[]{:S(2)}, u32[]{:S(2)}) collective-permute-start(bf16[12,768]{1,0:T(8,128)(2,1)S(1)} %broadcast_select_fusion.3.own_ref), channel_id=1, source_target_pairs={{0,4},{4,0},{1,5},{5,1},{2,6},{6,2},{3,7},{7,3},{8,12},{12,8},{9,1... | collective-permute-start | bytes 55304 | tf_op jit(solution)/shard_map/ppermute | solution.py:121
  16.6 13.4 %collective-permute-start.1 = (bf16[256,768]{1,0:T(8,128)(2,1)S(1)}, bf16[256,768]{1,0:T(8,128)(2,1)S(1)}, u32[]{:S(2)}, u32[]{:S(2)}) collective-permute-start(bf16[256,768]{1,0:T(8,128)(2,1)S(1)} %pad_maximum_fusion.x0), channel_id=1, source_target_pairs={{0,128},{128,256},{256,384},{1,129},{129,257},{257,385},{2,130},{1... | collective-permute-start | bytes 1179656 | tf_op jit(solution)/shard_map/ppermute | solution.py:22
  19.7 12.0 %collective-permute-start.2 = (bf16[256,768]{1,0:T(8,128)(2,1)S(1)}, bf16[256,768]{1,0:T(8,128)(2,1)S(1)}, u32[]{:S(2)}, u32[]{:S(2)}) collective-permute-start(bf16[256,768]{1,0:T(8,128)(2,1)S(1)} %pad_maximum_fusion.x0), channel_id=1, source_target_pairs={{128,0},{256,128},{384,256},{129,1},{257,129},{385,257},{130,2},{2... | collective-permute-start | bytes 1179656 | tf_op jit(solution)/shard_map/ppermute | solution.py:22
  21.0 0.6 copy-start.2
  23.1 18.1 %all-to-all-start = ((bf16[8,24,768]{2,1,0:T(8,128)(2,1)}), bf16[8,24,768]{2,1,0:T(8,128)(2,1)S(1)}, u32[]{:S(2)}, u32[]{:S(2)}) async-start(bf16[8,24,768]{2,1,0:T(8,128)(2,1)} %shard_map.94), calls=%async_computation | async-start | bytes 589824 | tf_op jit(solution)/shard_map/all_to_all | solution.py:146
  32.5 14.2 %collective-permute-start.3 = (bf16[256,768]{1,0:T(8,128)(2,1)}, bf16[256,768]{1,0:T(8,128)(2,1)}, u32[]{:S(2)}, u32[]{:S(2)}) collective-permute-start(bf16[256,768]{1,0:T(8,128)(2,1)} %broadcast_select_fusion), channel_id=1, source_target_pairs={{128,384},{256,0},{129,385},{257,1},{130,386},{258,2},{131,387},{2... | collective-permute-start | bytes 1179656 | tf_op jit(solution)/shard_map/ppermute | solution.py:22
  33.7 12.9 %collective-permute-start.4 = (bf16[256,768]{1,0:T(8,128)(2,1)S(1)}, bf16[256,768]{1,0:T(8,128)(2,1)}, u32[]{:S(2)}, u32[]{:S(2)}) collective-permute-start(bf16[256,768]{1,0:T(8,128)(2,1)S(1)} %collective-permute-done.1.up1), channel_id=1, source_target_pairs={{128,256},{256,384},{129,257},{257,385},{130,258},{258,386},{131,2... | collective-permute-start | bytes 1179656 | tf_op jit(solution)/shard_map/ppermute | solution.py:22
  35.2 19.4 %collective-permute-start.5 = (bf16[256,768]{1,0:T(8,128)(2,1)S(1)}, bf16[256,768]{1,0:T(8,128)(2,1)}, u32[]{:S(2)}, u32[]{:S(2)}) collective-permute-start(bf16[256,768]{1,0:T(8,128)(2,1)S(1)} %collective-permute-done.2.down1), channel_id=1, source_target_pairs={{128,0},{256,128},{129,1},{257,129},{130,2},{258,130},{131,3},{259... | collective-permute-start | bytes 1179656 | tf_op jit(solution)/shard_map/ppermute | solution.py:22
  42.4 18.1 %all-to-all-start.1 = ((bf16[4,192,768]{2,1,0:T(8,128)(2,1)}), bf16[4,192,768]{2,1,0:T(8,128)(2,1)S(1)}, u32[]{:S(2)}, u32[]{:S(2)}) async-start(bf16[4,192,768]{2,1,0:T(8,128)(2,1)} %broadcast_in_dim.17), calls=%async_computation.1 | async-start | bytes 2359296 | tf_op jit(solution)/shard_map/all_to_all | solution.py:28
  60.4 0.7 copy-start
  64.9 8.3 %collective-permute-start.7 = (bf16[1024,768]{1,0:T(8,128)(2,1)S(1)}, bf16[1024,768]{1,0:T(8,128)(2,1)S(1)}, u32[]{:S(2)}, u32[]{:S(2)}) collective-permute-start(bf16[1024,768]{1,0:T(8,128)(2,1)S(1)} %get-tuple-element.10.half_ref), channel_id=1, source_target_pairs={{0,64},{64,0},{1,65},{65,1},{2,66},{66,2},{3,67},{67,3},{4,68},{68... | collective-permute-start | bytes 4718600 | tf_op jit(solution)/shard_map/ppermute | solution.py:174
  97.0 23.1 %all-to-all-start.3 = ((f32[16,12,192]{2,1,0:T(8,128)}), f32[16,12,192]{2,1,0:T(8,128)S(1)}, u32[]{:S(2)}, u32[]{:S(2)}) async-start(f32[16,12,192]{2,1,0:T(8,128)} %bitcast.3), calls=%async_computation.3 | async-start | bytes 524288 | tf_op jit(solution)/shard_map/all_to_all | solution.py:201
  108.5 3.0 %collective-permute-start.8 = (f32[128]{0:T(128)S(1)}, f32[128]{0:T(128)S(1)}, u32[]{:S(2)}, u32[]{:S(2)}) collective-permute-start(f32[128]{0:T(128)S(1)} %get-tuple-element.16), channel_id=1, source_target_pairs={{0,64},{64,0},{1,65},{65,1},{2,66},{66,2},{3,67},{67,3},{4,68},{68... | collective-permute-start | bytes 1544 | tf_op jit(solution)/shard_map/ppermute | solution.py:212

commit v11 on v10

--- a/solution.py
+++ b/solution.py
@@ -62,7 +62,7 @@
 
 def grad_kernel(
     own, grid, scalars, place, half_ref, partner_ref, unit_ref, radius_ref, rows_ref,
-    local_ref, norms_ref, pre_ref,
+    local_ref, norms_ref, pre_ref, weights_ref,
 ):
     multiplier, offset = scalars[0], scalars[1]
     peers, held, columns = local_ref.shape
@@ -74,11 +74,13 @@
         logits = multiplier * lax.dot_general(
             half_ref[at, :], partner_ref[...], (((1,), (1,)), ((), ())), preferred_element_type=F32
         ) + offset
-        i = lax.broadcasted_iota(jnp.int32, logits.shape, 0) + k * rows
-        j = lax.broadcasted_iota(jnp.int32, logits.shape, 1)
-        sign = jnp.where(j == jnp.where(i % rows < own, i + own, i - own), 1.0, -1.0)
-        weights = (-multiplier * sign) * jax.nn.sigmoid(-sign * logits)
-        grad = jnp.dot(weights.astype(BF16), partner_ref[...], preferred_element_type=F32)
+        weights_ref[...] = (multiplier * jax.nn.sigmoid(logits)).astype(BF16)
+        square = logits[:, k * rows : (k + 1) * rows]
+        i = lax.broadcasted_iota(jnp.int32, square.shape, 0)
+        j = lax.broadcasted_iota(jnp.int32, square.shape, 1)
+        sign = jnp.where(j == jnp.where(i < own, i + own, i - own), 1.0, -1.0)
+        weights_ref[:, at] = ((-multiplier * sign) * jax.nn.sigmoid(-sign * square)).astype(BF16)
+        grad = jnp.dot(weights_ref[...], partner_ref[...], preferred_element_type=F32)
         unit = unit_ref[at, :]
         pre = (grad - unit * jnp.sum(unit * grad, axis=-1, keepdims=True)) / radius_ref[at, :]
         pre_ref[...] = pre
@@ -181,7 +183,7 @@
         ),
         in_specs=[SMEM] * 2 + [VMEM] * 5,
         out_specs=(VMEM,) * 2,
-        scratch_shapes=[pltpu.VMEM((2 * own, embed), F32)],
+        scratch_shapes=[pltpu.VMEM((2 * own, embed), F32), pltpu.VMEM((2 * own, rows), BF16)],
         compiler_params=PARAMS,
         cost_estimate=pl.CostEstimate(
             flops=4 * rows * rows * embed, bytes_accessed=8 * 2**20, transcendentals=rows * rows
@@ -205,14 +207,17 @@
         concat_axis=0,
         tiled=True,
     )
-    whole = jnp.sum(parts.reshape(n_zhi, chips, 2, share, columns), axis=0)
-    whole = whole.transpose(1, 2, 0, 3).reshape(2, share, embed)
+    parts = parts.reshape(n_zhi, chips, 2, share, columns)
+    img_proj_grad, txt_proj_grad = (
+        jnp.concatenate([jnp.sum(parts[:, z, side], axis=0) for z in range(chips)], axis=1)
+        for side in range(2)
+    )
     norms = norms.reshape(2 * own)
     own_norms = norms[:own]
     their_norms = lax.ppermute(norms[own:], "core", SWAP)
     img_norms = jnp.where(first, own_norms, their_norms)
     txt_norms = jnp.where(first, their_norms, own_norms)
-    return (whole[0], whole[1], img_norms, txt_norms)
+    return (img_proj_grad, txt_proj_grad, img_norms, txt_norms)
 
 
 def build(fine):

time: 122 us -> 122 us (level)
  local copies, waits for them, and re-layouts: 4.74 us -> 3.2 us
    squeeze x2 -> x0, local copies, waits for them, and re-layouts: 1.43 us -> none  [on_device(): return (whole[0], whole[1], img_norms, txt_norms)]
where the time goes in v11:
time: 122 us; the launch traced here: 121 us
  starting transfers between devices  52 us (43%)
  waiting for transfers between devices  30.4 us (25%)
  blocking collectives  17.1 us (14%)
  Pallas kernels  11.7 us (10%)
  other arithmetic  4.33 us (4%)
  local copies, waits for them, and re-layouts  3.2 us (3%)
  between operations  2.11 us (2%)
    all_to_all x1, blocking collectives, on_device(): lax.all_to_all(local, ('y', 'x'), split_axis=0, concat_axis=0, tiled=True)  17.1 us
    all_to_all x1, starting transfers between devices, on_device(): lax.all_to_all(totals.reshape(2 * n_zhi * chips, share, columns), ('zhi',...  11.4 us
    ppermute x5, waiting for transfers between devices, passed_on(): return lax.ppermute(value, 'zlo', hops)  9.71 us
    ppermute x1, starting transfers between devices, on_device(): chunk = jnp.concatenate([mine, lax.ppermute(sent, 'core', SWAP)], axis=0)  8.79 us
    ppermute x5, starting transfers between devices, passed_on(): return lax.ppermute(value, 'zlo', hops)  8.38 us
    all_to_all x1, waiting for transfers between devices, on_device(): lax.all_to_all(totals.reshape(2 * n_zhi * chips, share, columns), ('zhi',...  8.07 us
    all_to_all x1, starting transfers between devices, on_device(): near = lax.all_to_all(copies, 'y', split_axis=0, concat_axis=0)  6.82 us
    pallas_call x1, Pallas kernels, on_device(): pl.pallas_call(functools.partial(grad_kernel, own, (n_y, n_zhi, n_x)), ou...  5.85 us
  transfers between devices with their start and end apart: 12, of which 7 were waited for; matrix products, arithmetic and copies ran while one was open for 3% of the time, Pallas kernels for 2%

profile of v11, /device:TPU:1, one launch (start us, length us, event | category | flops | bytes accessed | tf_op | source)
XLA Modules:
  0.0 120.8 jit_solution(6017621981411125811)
XLA Ops:
  0.6 1.1 broadcast_select_fusion.2
  1.7 8.8 %collective-permute-start = (bf16[128,768]{1,0:T(8,128)(2,1)S(1)}, bf16[128,768]{1,0:T(8,128)(2,1)S(1)}, u32[]{:S(2)}, u32[]{:S(2)}) collective-permute-start(bf16[128,768]{1,0:T(8,128)(2,1)S(1)} %get-tuple-element.27), channel_id=1, source_target_pairs={{0,64},{64,0},{1,65},{65,1},{2,66},{66,2},{3,67},{67,3},{4,68},{68... | collective-permute-start | bytes 589832 | tf_op jit(solution)/shard_map/ppermute | solution.py:126
  10.5 0.8 broadcast_select_fusion.3.own_ref
  11.2 0.0 copy-start.1
  11.2 5.3 %collective-permute-start.6 = (bf16[12,768]{1,0:T(8,128)(2,1)S(1)}, bf16[12,768]{1,0:T(8,128)(2,1)S(1)}, u32[]{:S(2)}, u32[]{:S(2)}) collective-permute-start(bf16[12,768]{1,0:T(8,128)(2,1)S(1)} %broadcast_select_fusion.3.own_ref), channel_id=1, source_target_pairs={{0,4},{4,0},{1,5},{5,1},{2,6},{6,2},{3,7},{7,3},{8,12},{12,8},{9,1... | collective-permute-start | bytes 55304 | tf_op jit(solution)/shard_map/ppermute | solution.py:123
  16.5 0.0 collective-permute-done
  16.6 3.1 %collective-permute-start.1 = (bf16[256,768]{1,0:T(8,128)(2,1)S(1)}, bf16[256,768]{1,0:T(8,128)(2,1)S(1)}, u32[]{:S(2)}, u32[]{:S(2)}) collective-permute-start(bf16[256,768]{1,0:T(8,128)(2,1)S(1)} %pad_maximum_fusion.x0), channel_id=1, source_target_pairs={{0,128},{128,256},{256,384},{1,129},{129,257},{257,385},{2,130},{1... | collective-permute-start | bytes 1179656 | tf_op jit(solution)/shard_map/ppermute | solution.py:22
  19.7 1.3 %collective-permute-start.2 = (bf16[256,768]{1,0:T(8,128)(2,1)S(1)}, bf16[256,768]{1,0:T(8,128)(2,1)S(1)}, u32[]{:S(2)}, u32[]{:S(2)}) collective-permute-start(bf16[256,768]{1,0:T(8,128)(2,1)S(1)} %pad_maximum_fusion.x0), channel_id=1, source_target_pairs={{128,0},{256,128},{384,256},{129,1},{257,129},{385,257},{130,2},{2... | collective-permute-start | bytes 1179656 | tf_op jit(solution)/shard_map/ppermute | solution.py:22
  21.0 0.0 collective-permute-done.6.other_ref
  21.0 0.0 copy-done.1
  21.0 0.0 copy-start.2
  21.0 0.6 copy-done.2
  21.6 1.5 %shard_map.94 = bf16[8,24,768]{2,1,0:T(8,128)(2,1)} custom-call(bf16[12,768]{1,0:T(8,128)(2,1)} %copy-done.1, bf16[12,768]{1,0:T(8,128)(2,1)} %copy-done.2), custom_call_target="tpu_custom_call" | custom-call | flops 4000000000 | bytes 524288 | tf_op jit(solution)/shard_map/pallas_call | solution.py:141
  23.1 6.8 %all-to-all-start = ((bf16[8,24,768]{2,1,0:T(8,128)(2,1)}), bf16[8,24,768]{2,1,0:T(8,128)(2,1)S(1)}, u32[]{:S(2)}, u32[]{:S(2)}) async-start(bf16[8,24,768]{2,1,0:T(8,128)(2,1)} %shard_map.94), calls=%async_computation | async-start | bytes 589824 | tf_op jit(solution)/shard_map/all_to_all | solution.py:148
  29.9 0.0 collective-permute-done.1.up1
  29.9 1.7 %collective-permute-done.2.down1 = bf16[256,768]{1,0:T(8,128)(2,1)S(1)} collective-permute-done((bf16[256,768]{1,0:T(8,128)(2,1)S(1)}, bf16[256,768]{1,0:T(8,128)(2,1)S(1)}, u32[]{:S(2)}, u32[]{:S(2)}) %collective-permute-start.2) | collective-permute-done | bytes 393248 | tf_op jit(solution)/shard_map/ppermute | solution.py:22
  31.7 0.8 broadcast_select_fusion
  32.5 1.3 %collective-permute-start.3 = (bf16[256,768]{1,0:T(8,128)(2,1)}, bf16[256,768]{1,0:T(8,128)(2,1)}, u32[]{:S(2)}, u32[]{:S(2)}) collective-permute-start(bf16[256,768]{1,0:T(8,128)(2,1)} %broadcast_select_fusion), channel_id=1, source_target_pairs={{128,384},{256,0},{129,385},{257,1},{130,386},{258,2},{131,387},{2... | collective-permute-start | bytes 1179656 | tf_op jit(solution)/shard_map/ppermute | solution.py:22
  33.8 1.4 %collective-permute-start.4 = (bf16[256,768]{1,0:T(8,128)(2,1)S(1)}, bf16[256,768]{1,0:T(8,128)(2,1)}, u32[]{:S(2)}, u32[]{:S(2)}) collective-permute-start(bf16[256,768]{1,0:T(8,128)(2,1)S(1)} %collective-permute-done.1.up1), channel_id=1, source_target_pairs={{128,256},{256,384},{129,257},{257,385},{130,258},{258,386},{131,2... | collective-permute-start | bytes 1179656 | tf_op jit(solution)/shard_map/ppermute | solution.py:22
  35.2 1.3 %collective-permute-start.5 = (bf16[256,768]{1,0:T(8,128)(2,1)S(1)}, bf16[256,768]{1,0:T(8,128)(2,1)}, u32[]{:S(2)}, u32[]{:S(2)}) collective-permute-start(bf16[256,768]{1,0:T(8,128)(2,1)S(1)} %collective-permute-done.2.down1), channel_id=1, source_target_pairs={{128,0},{256,128},{129,1},{257,129},{130,2},{258,130},{131,3},{259... | collective-permute-start | bytes 1179656 | tf_op jit(solution)/shard_map/ppermute | solution.py:22
  36.5 4.8 %all-to-all-done = bf16[8,24,768]{2,1,0:T(8,128)(2,1)S(1)} async-done(((bf16[8,24,768]{2,1,0:T(8,128)(2,1)}), bf16[8,24,768]{2,1,0:T(8,128)(2,1)S(1)}, u32[]{:S(2)}, u32[]{:S(2)}) %all-to-all-start) | async-done | bytes 294944 | tf_op jit(solution)/shard_map/all_to_all | solution.py:148
  41.2 1.1 broadcast_in_dim.17
  42.3 4.0 %all-to-all-start.1 = ((bf16[4,192,768]{2,1,0:T(8,128)(2,1)}), bf16[4,192,768]{2,1,0:T(8,128)(2,1)S(1)}, u32[]{:S(2)}, u32[]{:S(2)}) async-start(bf16[4,192,768]{2,1,0:T(8,128)(2,1)} %broadcast_in_dim.17), calls=%async_computation.1 | async-start | bytes 2359296 | tf_op jit(solution)/shard_map/all_to_all | solution.py:28
  46.3 0.3 fusion.order_ref
  46.6 0.0 collective-permute-done.3.far_ref.far
  46.6 0.0 collective-permute-done.4.up_ref.up2
  46.6 8.0 %collective-permute-done.5.down_ref.down2 = bf16[256,768]{1,0:T(8,128)(2,1)} collective-permute-done((bf16[256,768]{1,0:T(8,128)(2,1)S(1)}, bf16[256,768]{1,0:T(8,128)(2,1)}, u32[]{:S(2)}, u32[]{:S(2)}) %collective-permute-start.5) | collective-permute-done | bytes 393248 | tf_op jit(solution)/shard_map/ppermute | solution.py:22
  54.6 0.6 shard_map.93.arrived_ref
  55.2 5.2 %all-to-all-done.1 = bf16[4,192,768]{2,1,0:T(8,128)(2,1)S(1)} async-done(((bf16[4,192,768]{2,1,0:T(8,128)(2,1)}), bf16[4,192,768]{2,1,0:T(8,128)(2,1)S(1)}, u32[]{:S(2)}, u32[]{:S(2)}) %all-to-all-start.1) | async-done | bytes 1179680 | tf_op jit(solution)/shard_map/all_to_all | solution.py:28
  60.4 0.0 copy-start
  60.4 0.7 copy-done
  61.1 3.8 %shard_map.95 = (bf16[1024,768]{1,0:T(8,128)(2,1)S(1)}, f32[1024,768]{1,0:T(8,128)S(1)}, f32[1024,1]{1,0:T(8,128)S(1)}, bf16[1024,768]{1,0:T(8,128)(2,1)S(1)}) custom-call(s32[1]{0:T(128)} %bitcast.place, f32[8,128]{1,0:T(8,128)S(1)} %copy-done, bf16[768,768]{1,0:T(8,128)(2,1)S(1)} %fusion.order_ref, bf16[768,768]{1,0:T(8,128)(2,1)S(1)} %bitcast.5, ...), custom_call_target="tpu_custom_call" | custom-call | flops 2113929216 | bytes 8388608 | tf_op jit(solution)/shard_map/pallas_call | solution.py:158
  64.9 5.3 %collective-permute-start.7 = (bf16[1024,768]{1,0:T(8,128)(2,1)S(1)}, bf16[1024,768]{1,0:T(8,128)(2,1)S(1)}, u32[]{:S(2)}, u32[]{:S(2)}) collective-permute-start(bf16[1024,768]{1,0:T(8,128)(2,1)S(1)} %get-tuple-element.10.half_ref), channel_id=1, source_target_pairs={{0,64},{64,0},{1,65},{65,1},{2,66},{66,2},{3,67},{67,3},{4,68},{68... | collective-permute-start | bytes 4718600 | tf_op jit(solution)/shard_map/ppermute | solution.py:176
  71.5 0.1 pad_maximum_fusion.3.scalars
  71.5 1.6 %collective-permute-done.7.partner_ref = bf16[1024,768]{1,0:T(8,128)(2,1)S(1)} collective-permute-done((bf16[1024,768]{1,0:T(8,128)(2,1)S(1)}, bf16[1024,768]{1,0:T(8,128)(2,1)S(1)}, u32[]{:S(2)}, u32[]{:S(2)}) %collective-permute-start.7) | collective-permute-done | bytes 1572896 | tf_op jit(solution)/shard_map/ppermute | solution.py:176
  73.2 5.9 %shard_map.96 = (bf16[32,24,192]{2,1,0:T(8,128)(2,1)S(1)}, f32[256,1]{1,0:T(8,128)S(1)}) custom-call(f32[2]{0:T(128)S(1)} %pad_maximum_fusion.3.scalars, s32[1]{0:T(128)} %bitcast.place, bf16[1024,768]{1,0:T(8,128)(2,1)S(1)} %get-tuple-element.10.half_ref, bf16[1024,768]{1,0:T(8,128)(2,1)S(1)} %collective-permute-done.7.partner_ref, ...), custom_call_target="tpu_custom_call" | custom-call | flops 3221225472 | bytes 8388608 | tf_op jit(solution)/shard_map/pallas_call | solution.py:178
  79.1 17.1 %all_to_all.20 = bf16[32,24,192]{2,1,0:T(8,128)(2,1)S(1)} all-to-all(bf16[32,24,192]{2,1,0:T(8,128)(2,1)S(1)} %get-tuple-element.14), channel_id=1, replica_groups=mesh['zlo'=4,'core'=2,'y'=8,'zhi'=2,'x'=4] {'y','x'}, dimensions={0} | all-to-all | bytes 589824 | tf_op jit(solution)/shard_map/all_to_all | solution.py:200
  96.1 0.1 convert_reduce_fusion
  96.2 0.7 broadcast_in_dim.19
  96.9 11.4 %all-to-all-start.3 = ((f32[16,12,192]{2,1,0:T(8,128)}), f32[16,12,192]{2,1,0:T(8,128)S(1)}, u32[]{:S(2)}, u32[]{:S(2)}) async-start(f32[16,12,192]{2,1,0:T(8,128)} %bitcast.3), calls=%async_computation.3 | async-start | bytes 524288 | tf_op jit(solution)/shard_map/all_to_all | solution.py:203
  108.4 0.1 slice_reduce_fusion
  108.5 2.0 %collective-permute-start.8 = (f32[128]{0:T(128)S(1)}, f32[128]{0:T(128)S(1)}, u32[]{:S(2)}, u32[]{:S(2)}) collective-permute-start(f32[128]{0:T(128)S(1)} %get-tuple-element.24), channel_id=1, source_target_pairs={{0,64},{64,0},{1,65},{65,1},{2,66},{66,2},{3,67},{67,3},{4,68},{68... | collective-permute-start | bytes 1544 | tf_op jit(solution)/shard_map/ppermute | solution.py:217
  110.5 1.0 collective-permute-done.8
  111.5 0.5 broadcast_select_fusion.4
  112.0 8.1 %all-to-all-done.3 = f32[16,12,192]{2,1,0:T(8,128)S(1)} async-done(((f32[16,12,192]{2,1,0:T(8,128)}), f32[16,12,192]{2,1,0:T(8,128)S(1)}, u32[]{:S(2)}, u32[]{:S(2)}) %all-to-all-start.3) | async-done | bytes 147488 | tf_op jit(solution)/shard_map/all_to_all | solution.py:203
  120.1 0.7 pad_maximum_fusion.1
  (4 shorter events, 0.1 us)
Async XLA Ops:
  1.7 14.8 %collective-permute-start = (bf16[128,768]{1,0:T(8,128)(2,1)S(1)}, bf16[128,768]{1,0:T(8,128)(2,1)S(1)}, u32[]{:S(2)}, u32[]{:S(2)}) collective-permute-start(bf16[128,768]{1,0:T(8,128)(2,1)S(1)} %get-tuple-element.27), channel_id=1, source_target_pairs={{0,64},{64,0},{1,65},{65,1},{2,66},{66,2},{3,67},{67,3},{4,68},{68... | collective-permute-start | bytes 589832 | tf_op jit(solution)/shard_map/ppermute | solution.py:126
  11.2 9.7 %copy-start.1 = (bf16[12,768]{1,0:T(8,128)(2,1)}, bf16[12,768]{1,0:T(8,128)(2,1)S(1)}, u32[]{:S(2)}) copy-start(bf16[12,768]{1,0:T(8,128)(2,1)S(1)} %broadcast_select_fusion.3.own_ref) | copy-start | bytes 55300
  11.2 9.7 %collective-permute-start.6 = (bf16[12,768]{1,0:T(8,128)(2,1)S(1)}, bf16[12,768]{1,0:T(8,128)(2,1)S(1)}, u32[]{:S(2)}, u32[]{:S(2)}) collective-permute-start(bf16[12,768]{1,0:T(8,128)(2,1)S(1)} %broadcast_select_fusion.3.own_ref), channel_id=1, source_target_pairs={{0,4},{4,0},{1,5},{5,1},{2,6},{6,2},{3,7},{7,3},{8,12},{12,8},{9,1... | collective-permute-start | bytes 55304 | tf_op jit(solution)/shard_map/ppermute | solution.py:123
  16.6 13.4 %collective-permute-start.1 = (bf16[256,768]{1,0:T(8,128)(2,1)S(1)}, bf16[256,768]{1,0:T(8,128)(2,1)S(1)}, u32[]{:S(2)}, u32[]{:S(2)}) collective-permute-start(bf16[256,768]{1,0:T(8,128)(2,1)S(1)} %pad_maximum_fusion.x0), channel_id=1, source_target_pairs={{0,128},{128,256},{256,384},{1,129},{129,257},{257,385},{2,130},{1... | collective-permute-start | bytes 1179656 | tf_op jit(solution)/shard_map/ppermute | solution.py:22
  19.7 12.0 %collective-permute-start.2 = (bf16[256,768]{1,0:T(8,128)(2,1)S(1)}, bf16[256,768]{1,0:T(8,128)(2,1)S(1)}, u32[]{:S(2)}, u32[]{:S(2)}) collective-permute-start(bf16[256,768]{1,0:T(8,128)(2,1)S(1)} %pad_maximum_fusion.x0), channel_id=1, source_target_pairs={{128,0},{256,128},{384,256},{129,1},{257,129},{385,257},{130,2},{2... | collective-permute-start | bytes 1179656 | tf_op jit(solution)/shard_map/ppermute | solution.py:22
  21.0 0.6 copy-start.2
  23.1 18.1 %all-to-all-start = ((bf16[8,24,768]{2,1,0:T(8,128)(2,1)}), bf16[8,24,768]{2,1,0:T(8,128)(2,1)S(1)}, u32[]{:S(2)}, u32[]{:S(2)}) async-start(bf16[8,24,768]{2,1,0:T(8,128)(2,1)} %shard_map.94), calls=%async_computation | async-start | bytes 589824 | tf_op jit(solution)/shard_map/all_to_all | solution.py:148
  32.5 14.2 %collective-permute-start.3 = (bf16[256,768]{1,0:T(8,128)(2,1)}, bf16[256,768]{1,0:T(8,128)(2,1)}, u32[]{:S(2)}, u32[]{:S(2)}) collective-permute-start(bf16[256,768]{1,0:T(8,128)(2,1)} %broadcast_select_fusion), channel_id=1, source_target_pairs={{128,384},{256,0},{129,385},{257,1},{130,386},{258,2},{131,387},{2... | collective-permute-start | bytes 1179656 | tf_op jit(solution)/shard_map/ppermute | solution.py:22
  33.8 12.9 %collective-permute-start.4 = (bf16[256,768]{1,0:T(8,128)(2,1)S(1)}, bf16[256,768]{1,0:T(8,128)(2,1)}, u32[]{:S(2)}, u32[]{:S(2)}) collective-permute-start(bf16[256,768]{1,0:T(8,128)(2,1)S(1)} %collective-permute-done.1.up1), channel_id=1, source_target_pairs={{128,256},{256,384},{129,257},{257,385},{130,258},{258,386},{131,2... | collective-permute-start | bytes 1179656 | tf_op jit(solution)/shard_map/ppermute | solution.py:22
  35.2 19.4 %collective-permute-start.5 = (bf16[256,768]{1,0:T(8,128)(2,1)S(1)}, bf16[256,768]{1,0:T(8,128)(2,1)}, u32[]{:S(2)}, u32[]{:S(2)}) collective-permute-start(bf16[256,768]{1,0:T(8,128)(2,1)S(1)} %collective-permute-done.2.down1), channel_id=1, source_target_pairs={{128,0},{256,128},{129,1},{257,129},{130,2},{258,130},{131,3},{259... | collective-permute-start | bytes 1179656 | tf_op jit(solution)/shard_map/ppermute | solution.py:22
  42.3 18.1 %all-to-all-start.1 = ((bf16[4,192,768]{2,1,0:T(8,128)(2,1)}), bf16[4,192,768]{2,1,0:T(8,128)(2,1)S(1)}, u32[]{:S(2)}, u32[]{:S(2)}) async-start(bf16[4,192,768]{2,1,0:T(8,128)(2,1)} %broadcast_in_dim.17), calls=%async_computation.1 | async-start | bytes 2359296 | tf_op jit(solution)/shard_map/all_to_all | solution.py:28
  60.4 0.7 copy-start
  64.9 8.3 %collective-permute-start.7 = (bf16[1024,768]{1,0:T(8,128)(2,1)S(1)}, bf16[1024,768]{1,0:T(8,128)(2,1)S(1)}, u32[]{:S(2)}, u32[]{:S(2)}) collective-permute-start(bf16[1024,768]{1,0:T(8,128)(2,1)S(1)} %get-tuple-element.10.half_ref), channel_id=1, source_target_pairs={{0,64},{64,0},{1,65},{65,1},{2,66},{66,2},{3,67},{67,3},{4,68},{68... | collective-permute-start | bytes 4718600 | tf_op jit(solution)/shard_map/ppermute | solution.py:176
  96.9 23.1 %all-to-all-start.3 = ((f32[16,12,192]{2,1,0:T(8,128)}), f32[16,12,192]{2,1,0:T(8,128)S(1)}, u32[]{:S(2)}, u32[]{:S(2)}) async-start(f32[16,12,192]{2,1,0:T(8,128)} %bitcast.3), calls=%async_computation.3 | async-start | bytes 524288 | tf_op jit(solution)/shard_map/all_to_all | solution.py:203
  108.5 3.0 %collective-permute-start.8 = (f32[128]{0:T(128)S(1)}, f32[128]{0:T(128)S(1)}, u32[]{:S(2)}, u32[]{:S(2)}) collective-permute-start(f32[128]{0:T(128)S(1)} %get-tuple-element.24), channel_id=1, source_target_pairs={{0,64},{64,0},{1,65},{65,1},{2,66},{66,2},{3,67},{67,3},{4,68},{68... | collective-permute-start | bytes 1544 | tf_op jit(solution)/shard_map/ppermute | solution.py:217

commit v12 on v11

--- a/solution.py
+++ b/solution.py
@@ -35,7 +35,7 @@
         out_ref[k, share:] = other_ref[...]
 
 
-def arrived_kernel(far_ref, up_ref, down_ref, out_ref):
+def arrived_kernel(far_ref, up_ref, out_ref):
     out_ref[...] = jnp.zeros_like(out_ref)
 
 
@@ -133,10 +133,10 @@
     arrived = pl.pallas_call(
         arrived_kernel,
         out_shape=jax.ShapeDtypeStruct((8, 128), F32),
-        in_specs=[ANY] * 3,
+        in_specs=[ANY] * 2,
         out_specs=VMEM,
         cost_estimate=pl.CostEstimate(flops=ARRIVED, bytes_accessed=2**12, transcendentals=0),
-    )(far, up2, down2)
+    )(far, up2)
     at_chip = at_line.astype(jnp.int32).reshape(1)
     copies = pl.pallas_call(
         copies_kernel,

time: 122 us -> 118 us (0.967)
  starting transfers between devices: 52 us -> 47.7 us
    all_to_all x1, starting transfers between devices: 11.4 us -> 7.15 us  [on_device(): lax.all_to_all(totals.reshape(2 * n_zhi * chips, share, columns), ('zhi',...]
    all_to_all x1, waiting for transfers between devices: 5.21 us -> 3.82 us  [spread(): return lax.all_to_all(copies, axis, split_axis=0, concat_axis=0)]
    all_to_all x1, waiting for transfers between devices: 4.77 us -> 6.03 us  [on_device(): near = lax.all_to_all(copies, 'y', split_axis=0, concat_axis=0)]
where the time goes in v12:
time: 118 us; the launch traced here: 117 us
  starting transfers between devices  47.7 us (40%)
  waiting for transfers between devices  30.4 us (26%)
  blocking collectives  17.7 us (15%)
  Pallas kernels  11.7 us (10%)
  other arithmetic  4.36 us (4%)
  local copies, waits for them, and re-layouts  3.2 us (3%)
  between operations  2.1 us (2%)
    all_to_all x1, blocking collectives, on_device(): lax.all_to_all(local, ('y', 'x'), split_axis=0, concat_axis=0, tiled=True)  17.7 us
    ppermute x5, waiting for transfers between devices, passed_on(): return lax.ppermute(value, 'zlo', hops)  9.8 us
    ppermute x1, starting transfers between devices, on_device(): chunk = jnp.concatenate([mine, lax.ppermute(sent, 'core', SWAP)], axis=0)  8.79 us
    ppermute x5, starting transfers between devices, passed_on(): return lax.ppermute(value, 'zlo', hops)  8.39 us
    all_to_all x1, waiting for transfers between devices, on_device(): lax.all_to_all(totals.reshape(2 * n_zhi * chips, share, columns), ('zhi',...  8.07 us
    all_to_all x1, starting transfers between devices, on_device(): lax.all_to_all(totals.reshape(2 * n_zhi * chips, share, columns), ('zhi',...  7.15 us
    all_to_all x1, starting transfers between devices, on_device(): near = lax.all_to_all(copies, 'y', split_axis=0, concat_axis=0)  6.82 us
    all_to_all x1, waiting for transfers between devices, on_device(): near = lax.all_to_all(copies, 'y', split_axis=0, concat_axis=0)  6.03 us
  transfers between devices with their start and end apart: 12, of which 7 were waited for; matrix products, arithmetic and copies ran while one was open for 3% of the time, Pallas kernels for 2%

profile of v12, /device:TPU:1, one launch (start us, length us, event | category | flops | bytes accessed | tf_op | source)
XLA Modules:
  0.0 117.2 jit_solution(1933409134295103721)
XLA Ops:
  0.6 1.1 broadcast_select_fusion.2
  1.7 8.8 %collective-permute-start = (bf16[128,768]{1,0:T(8,128)(2,1)S(1)}, bf16[128,768]{1,0:T(8,128)(2,1)S(1)}, u32[]{:S(2)}, u32[]{:S(2)}) collective-permute-start(bf16[128,768]{1,0:T(8,128)(2,1)S(1)} %get-tuple-element.27), channel_id=1, source_target_pairs={{0,64},{64,0},{1,65},{65,1},{2,66},{66,2},{3,67},{67,3},{4,68},{68... | collective-permute-start | bytes 589832 | tf_op jit(solution)/shard_map/ppermute | solution.py:126
  10.5 0.8 broadcast_select_fusion.3.own_ref
  11.2 0.0 copy-start.1
  11.2 5.3 %collective-permute-start.5 = (bf16[12,768]{1,0:T(8,128)(2,1)S(1)}, bf16[12,768]{1,0:T(8,128)(2,1)S(1)}, u32[]{:S(2)}, u32[]{:S(2)}) collective-permute-start(bf16[12,768]{1,0:T(8,128)(2,1)S(1)} %broadcast_select_fusion.3.own_ref), channel_id=1, source_target_pairs={{0,4},{4,0},{1,5},{5,1},{2,6},{6,2},{3,7},{7,3},{8,12},{12,8},{9,1... | collective-permute-start | bytes 55304 | tf_op jit(solution)/shard_map/ppermute | solution.py:123
  16.5 0.0 collective-permute-done
  16.6 3.1 %collective-permute-start.1 = (bf16[256,768]{1,0:T(8,128)(2,1)S(1)}, bf16[256,768]{1,0:T(8,128)(2,1)S(1)}, u32[]{:S(2)}, u32[]{:S(2)}) collective-permute-start(bf16[256,768]{1,0:T(8,128)(2,1)S(1)} %pad_maximum_fusion.x0), channel_id=1, source_target_pairs={{0,128},{128,256},{256,384},{1,129},{129,257},{257,385},{2,130},{1... | collective-permute-start | bytes 1179656 | tf_op jit(solution)/shard_map/ppermute | solution.py:22
  19.7 1.3 %collective-permute-start.2 = (bf16[256,768]{1,0:T(8,128)(2,1)S(1)}, bf16[256,768]{1,0:T(8,128)(2,1)S(1)}, u32[]{:S(2)}, u32[]{:S(2)}) collective-permute-start(bf16[256,768]{1,0:T(8,128)(2,1)S(1)} %pad_maximum_fusion.x0), channel_id=1, source_target_pairs={{128,0},{256,128},{384,256},{129,1},{257,129},{385,257},{130,2},{2... | collective-permute-start | bytes 1179656 | tf_op jit(solution)/shard_map/ppermute | solution.py:22
  21.0 0.0 collective-permute-done.5.other_ref
  21.0 0.0 copy-done.1
  21.0 0.0 copy-start.2
  21.0 0.6 copy-done.2
  21.6 1.5 %shard_map.94 = bf16[8,24,768]{2,1,0:T(8,128)(2,1)} custom-call(bf16[12,768]{1,0:T(8,128)(2,1)} %copy-done.1, bf16[12,768]{1,0:T(8,128)(2,1)} %copy-done.2), custom_call_target="tpu_custom_call" | custom-call | flops 4000000000 | bytes 524288 | tf_op jit(solution)/shard_map/pallas_call | solution.py:141
  23.1 6.8 %all-to-all-start = ((bf16[8,24,768]{2,1,0:T(8,128)(2,1)}), bf16[8,24,768]{2,1,0:T(8,128)(2,1)S(1)}, u32[]{:S(2)}, u32[]{:S(2)}) async-start(bf16[8,24,768]{2,1,0:T(8,128)(2,1)} %shard_map.94), calls=%async_computation | async-start | bytes 589824 | tf_op jit(solution)/shard_map/all_to_all | solution.py:148
  29.9 0.0 collective-permute-done.1.up1
  29.9 1.7 %collective-permute-done.2.down1 = bf16[256,768]{1,0:T(8,128)(2,1)S(1)} collective-permute-done((bf16[256,768]{1,0:T(8,128)(2,1)S(1)}, bf16[256,768]{1,0:T(8,128)(2,1)S(1)}, u32[]{:S(2)}, u32[]{:S(2)}) %collective-permute-start.2) | collective-permute-done | bytes 393248 | tf_op jit(solution)/shard_map/ppermute | solution.py:22
  31.7 0.8 broadcast_select_fusion
  32.5 1.3 %collective-permute-start.3 = (bf16[256,768]{1,0:T(8,128)(2,1)}, bf16[256,768]{1,0:T(8,128)(2,1)}, u32[]{:S(2)}, u32[]{:S(2)}) collective-permute-start(bf16[256,768]{1,0:T(8,128)(2,1)} %broadcast_select_fusion), channel_id=1, source_target_pairs={{128,384},{256,0},{129,385},{257,1},{130,386},{258,2},{131,387},{2... | collective-permute-start | bytes 1179656 | tf_op jit(solution)/shard_map/ppermute | solution.py:22
  33.8 1.4 %collective-permute-start.4 = (bf16[256,768]{1,0:T(8,128)(2,1)S(1)}, bf16[256,768]{1,0:T(8,128)(2,1)}, u32[]{:S(2)}, u32[]{:S(2)}) collective-permute-start(bf16[256,768]{1,0:T(8,128)(2,1)S(1)} %collective-permute-done.1.up1), channel_id=1, source_target_pairs={{128,256},{256,384},{129,257},{257,385},{130,258},{258,386},{131,2... | collective-permute-start | bytes 1179656 | tf_op jit(solution)/shard_map/ppermute | solution.py:22
  35.2 6.0 %all-to-all-done = bf16[8,24,768]{2,1,0:T(8,128)(2,1)S(1)} async-done(((bf16[8,24,768]{2,1,0:T(8,128)(2,1)}), bf16[8,24,768]{2,1,0:T(8,128)(2,1)S(1)}, u32[]{:S(2)}, u32[]{:S(2)}) %all-to-all-start) | async-done | bytes 294944 | tf_op jit(solution)/shard_map/all_to_all | solution.py:148
  41.2 1.1 broadcast_in_dim.17
  42.3 4.0 %all-to-all-start.1 = ((bf16[4,192,768]{2,1,0:T(8,128)(2,1)}), bf16[4,192,768]{2,1,0:T(8,128)(2,1)S(1)}, u32[]{:S(2)}, u32[]{:S(2)}) async-start(bf16[4,192,768]{2,1,0:T(8,128)(2,1)} %broadcast_in_dim.17), calls=%async_computation.1 | async-start | bytes 2359296 | tf_op jit(solution)/shard_map/all_to_all | solution.py:28
  46.3 0.3 fusion.order_ref
  46.6 1.3 %collective-permute-start.6 = (bf16[256,768]{1,0:T(8,128)(2,1)S(1)}, bf16[256,768]{1,0:T(8,128)(2,1)}, u32[]{:S(2)}, u32[]{:S(2)}) collective-permute-start(bf16[256,768]{1,0:T(8,128)(2,1)S(1)} %collective-permute-done.2.down1), channel_id=1, source_target_pairs={{128,0},{256,128},{129,1},{257,129},{130,2},{258,130},{131,3},{259... | collective-permute-start | bytes 1179656 | tf_op jit(solution)/shard_map/ppermute | solution.py:22
  47.9 0.0 collective-permute-done.3.far_ref.far
  47.9 0.0 collective-permute-done.4.up_ref.up2
  47.9 0.6 shard_map.93.arrived_ref
  48.5 8.0 %collective-permute-done.6.down2 = bf16[256,768]{1,0:T(8,128)(2,1)} collective-permute-done((bf16[256,768]{1,0:T(8,128)(2,1)S(1)}, bf16[256,768]{1,0:T(8,128)(2,1)}, u32[]{:S(2)}, u32[]{:S(2)}) %collective-permute-start.6) | collective-permute-done | bytes 393248 | tf_op jit(solution)/shard_map/ppermute | solution.py:22
  56.6 3.8 %all-to-all-done.1 = bf16[4,192,768]{2,1,0:T(8,128)(2,1)S(1)} async-done(((bf16[4,192,768]{2,1,0:T(8,128)(2,1)}), bf16[4,192,768]{2,1,0:T(8,128)(2,1)S(1)}, u32[]{:S(2)}, u32[]{:S(2)}) %all-to-all-start.1) | async-done | bytes 1179680 | tf_op jit(solution)/shard_map/all_to_all | solution.py:28
  60.4 0.0 copy-start
  60.4 0.7 copy-done
  61.1 3.8 %shard_map.95 = (bf16[1024,768]{1,0:T(8,128)(2,1)S(1)}, f32[1024,768]{1,0:T(8,128)S(1)}, f32[1024,1]{1,0:T(8,128)S(1)}, bf16[1024,768]{1,0:T(8,128)(2,1)S(1)}) custom-call(s32[1]{0:T(128)} %bitcast.place, f32[8,128]{1,0:T(8,128)S(1)} %copy-done, bf16[768,768]{1,0:T(8,128)(2,1)S(1)} %fusion.order_ref, bf16[768,768]{1,0:T(8,128)(2,1)S(1)} %bitcast.5, ...), custom_call_target="tpu_custom_call" | custom-call | flops 2113929216 | bytes 8388608 | tf_op jit(solution)/shard_map/pallas_call | solution.py:158
  64.9 5.3 %collective-permute-start.7 = (bf16[1024,768]{1,0:T(8,128)(2,1)S(1)}, bf16[1024,768]{1,0:T(8,128)(2,1)S(1)}, u32[]{:S(2)}, u32[]{:S(2)}) collective-permute-start(bf16[1024,768]{1,0:T(8,128)(2,1)S(1)} %get-tuple-element.10.half_ref), channel_id=1, source_target_pairs={{0,64},{64,0},{1,65},{65,1},{2,66},{66,2},{3,67},{67,3},{4,68},{68... | collective-permute-start | bytes 4718600 | tf_op jit(solution)/shard_map/ppermute | solution.py:176
  71.5 0.1 pad_maximum_fusion.3.scalars
  71.5 1.6 %collective-permute-done.7.partner_ref = bf16[1024,768]{1,0:T(8,128)(2,1)S(1)} collective-permute-done((bf16[1024,768]{1,0:T(8,128)(2,1)S(1)}, bf16[1024,768]{1,0:T(8,128)(2,1)S(1)}, u32[]{:S(2)}, u32[]{:S(2)}) %collective-permute-start.7) | collective-permute-done | bytes 1572896 | tf_op jit(solution)/shard_map/ppermute | solution.py:176
  73.2 5.9 %shard_map.96 = (bf16[32,24,192]{2,1,0:T(8,128)(2,1)S(1)}, f32[256,1]{1,0:T(8,128)S(1)}) custom-call(f32[2]{0:T(128)S(1)} %pad_maximum_fusion.3.scalars, s32[1]{0:T(128)} %bitcast.place, bf16[1024,768]{1,0:T(8,128)(2,1)S(1)} %get-tuple-element.10.half_ref, bf16[1024,768]{1,0:T(8,128)(2,1)S(1)} %collective-permute-done.7.partner_ref, ...), custom_call_target="tpu_custom_call" | custom-call | flops 3221225472 | bytes 8388608 | tf_op jit(solution)/shard_map/pallas_call | solution.py:178
  79.1 17.7 %all_to_all.20 = bf16[32,24,192]{2,1,0:T(8,128)(2,1)S(1)} all-to-all(bf16[32,24,192]{2,1,0:T(8,128)(2,1)S(1)} %get-tuple-element.14), channel_id=1, replica_groups=mesh['zlo'=4,'core'=2,'y'=8,'zhi'=2,'x'=4] {'y','x'}, dimensions={0} | all-to-all | bytes 589824 | tf_op jit(solution)/shard_map/all_to_all | solution.py:200
  96.8 0.1 convert_reduce_fusion
  96.8 0.7 broadcast_in_dim.19
  97.6 7.2 %all-to-all-start.3 = ((f32[16,12,192]{2,1,0:T(8,128)}), f32[16,12,192]{2,1,0:T(8,128)S(1)}, u32[]{:S(2)}, u32[]{:S(2)}) async-start(f32[16,12,192]{2,1,0:T(8,128)} %bitcast.3), calls=%async_computation.3 | async-start | bytes 524288 | tf_op jit(solution)/shard_map/all_to_all | solution.py:203
  104.7 0.1 slice_reduce_fusion
  104.8 2.0 %collective-permute-start.8 = (f32[128]{0:T(128)S(1)}, f32[128]{0:T(128)S(1)}, u32[]{:S(2)}, u32[]{:S(2)}) collective-permute-start(f32[128]{0:T(128)S(1)} %get-tuple-element.24), channel_id=1, source_target_pairs={{0,64},{64,0},{1,65},{65,1},{2,66},{66,2},{3,67},{67,3},{4,68},{68... | collective-permute-start | bytes 1544 | tf_op jit(solution)/shard_map/ppermute | solution.py:217
  106.8 1.0 collective-permute-done.8
  107.8 0.5 broadcast_select_fusion.4
  108.4 8.1 %all-to-all-done.3 = f32[16,12,192]{2,1,0:T(8,128)S(1)} async-done(((f32[16,12,192]{2,1,0:T(8,128)}), f32[16,12,192]{2,1,0:T(8,128)S(1)}, u32[]{:S(2)}, u32[]{:S(2)}) %all-to-all-start.3) | async-done | bytes 147488 | tf_op jit(solution)/shard_map/all_to_all | solution.py:203
  116.5 0.7 pad_maximum_fusion.1
  (4 shorter events, 0.1 us)
Async XLA Ops:
  1.7 14.8 %collective-permute-start = (bf16[128,768]{1,0:T(8,128)(2,1)S(1)}, bf16[128,768]{1,0:T(8,128)(2,1)S(1)}, u32[]{:S(2)}, u32[]{:S(2)}) collective-permute-start(bf16[128,768]{1,0:T(8,128)(2,1)S(1)} %get-tuple-element.27), channel_id=1, source_target_pairs={{0,64},{64,0},{1,65},{65,1},{2,66},{66,2},{3,67},{67,3},{4,68},{68... | collective-permute-start | bytes 589832 | tf_op jit(solution)/shard_map/ppermute | solution.py:126
  11.2 9.7 %copy-start.1 = (bf16[12,768]{1,0:T(8,128)(2,1)}, bf16[12,768]{1,0:T(8,128)(2,1)S(1)}, u32[]{:S(2)}) copy-start(bf16[12,768]{1,0:T(8,128)(2,1)S(1)} %broadcast_select_fusion.3.own_ref) | copy-start | bytes 55300
  11.2 9.7 %collective-permute-start.5 = (bf16[12,768]{1,0:T(8,128)(2,1)S(1)}, bf16[12,768]{1,0:T(8,128)(2,1)S(1)}, u32[]{:S(2)}, u32[]{:S(2)}) collective-permute-start(bf16[12,768]{1,0:T(8,128)(2,1)S(1)} %broadcast_select_fusion.3.own_ref), channel_id=1, source_target_pairs={{0,4},{4,0},{1,5},{5,1},{2,6},{6,2},{3,7},{7,3},{8,12},{12,8},{9,1... | collective-permute-start | bytes 55304 | tf_op jit(solution)/shard_map/ppermute | solution.py:123
  16.6 13.4 %collective-permute-start.1 = (bf16[256,768]{1,0:T(8,128)(2,1)S(1)}, bf16[256,768]{1,0:T(8,128)(2,1)S(1)}, u32[]{:S(2)}, u32[]{:S(2)}) collective-permute-start(bf16[256,768]{1,0:T(8,128)(2,1)S(1)} %pad_maximum_fusion.x0), channel_id=1, source_target_pairs={{0,128},{128,256},{256,384},{1,129},{129,257},{257,385},{2,130},{1... | collective-permute-start | bytes 1179656 | tf_op jit(solution)/shard_map/ppermute | solution.py:22
  19.7 12.0 %collective-permute-start.2 = (bf16[256,768]{1,0:T(8,128)(2,1)S(1)}, bf16[256,768]{1,0:T(8,128)(2,1)S(1)}, u32[]{:S(2)}, u32[]{:S(2)}) collective-permute-start(bf16[256,768]{1,0:T(8,128)(2,1)S(1)} %pad_maximum_fusion.x0), channel_id=1, source_target_pairs={{128,0},{256,128},{384,256},{129,1},{257,129},{385,257},{130,2},{2... | collective-permute-start | bytes 1179656 | tf_op jit(solution)/shard_map/ppermute | solution.py:22
  21.0 0.6 copy-start.2
  23.1 18.1 %all-to-all-start = ((bf16[8,24,768]{2,1,0:T(8,128)(2,1)}), bf16[8,24,768]{2,1,0:T(8,128)(2,1)S(1)}, u32[]{:S(2)}, u32[]{:S(2)}) async-start(bf16[8,24,768]{2,1,0:T(8,128)(2,1)} %shard_map.94), calls=%async_computation | async-start | bytes 589824 | tf_op jit(solution)/shard_map/all_to_all | solution.py:148
  32.5 15.4 %collective-permute-start.3 = (bf16[256,768]{1,0:T(8,128)(2,1)}, bf16[256,768]{1,0:T(8,128)(2,1)}, u32[]{:S(2)}, u32[]{:S(2)}) collective-permute-start(bf16[256,768]{1,0:T(8,128)(2,1)} %broadcast_select_fusion), channel_id=1, source_target_pairs={{128,384},{256,0},{129,385},{257,1},{130,386},{258,2},{131,387},{2... | collective-permute-start | bytes 1179656 | tf_op jit(solution)/shard_map/ppermute | solution.py:22
  33.8 14.1 %collective-permute-start.4 = (bf16[256,768]{1,0:T(8,128)(2,1)S(1)}, bf16[256,768]{1,0:T(8,128)(2,1)}, u32[]{:S(2)}, u32[]{:S(2)}) collective-permute-start(bf16[256,768]{1,0:T(8,128)(2,1)S(1)} %collective-permute-done.1.up1), channel_id=1, source_target_pairs={{128,256},{256,384},{129,257},{257,385},{130,258},{258,386},{131,2... | collective-permute-start | bytes 1179656 | tf_op jit(solution)/shard_map/ppermute | solution.py:22
  42.3 18.1 %all-to-all-start.1 = ((bf16[4,192,768]{2,1,0:T(8,128)(2,1)}), bf16[4,192,768]{2,1,0:T(8,128)(2,1)S(1)}, u32[]{:S(2)}, u32[]{:S(2)}) async-start(bf16[4,192,768]{2,1,0:T(8,128)(2,1)} %broadcast_in_dim.17), calls=%async_computation.1 | async-start | bytes 2359296 | tf_op jit(solution)/shard_map/all_to_all | solution.py:28
  46.6 10.0 %collective-permute-start.6 = (bf16[256,768]{1,0:T(8,128)(2,1)S(1)}, bf16[256,768]{1,0:T(8,128)(2,1)}, u32[]{:S(2)}, u32[]{:S(2)}) collective-permute-start(bf16[256,768]{1,0:T(8,128)(2,1)S(1)} %collective-permute-done.2.down1), channel_id=1, source_target_pairs={{128,0},{256,128},{129,1},{257,129},{130,2},{258,130},{131,3},{259... | collective-permute-start | bytes 1179656 | tf_op jit(solution)/shard_map/ppermute | solution.py:22
  60.4 0.7 copy-start
  64.9 8.3 %collective-permute-start.7 = (bf16[1024,768]{1,0:T(8,128)(2,1)S(1)}, bf16[1024,768]{1,0:T(8,128)(2,1)S(1)}, u32[]{:S(2)}, u32[]{:S(2)}) collective-permute-start(bf16[1024,768]{1,0:T(8,128)(2,1)S(1)} %get-tuple-element.10.half_ref), channel_id=1, source_target_pairs={{0,64},{64,0},{1,65},{65,1},{2,66},{66,2},{3,67},{67,3},{4,68},{68... | collective-permute-start | bytes 4718600 | tf_op jit(solution)/shard_map/ppermute | solution.py:176
  97.6 18.9 %all-to-all-start.3 = ((f32[16,12,192]{2,1,0:T(8,128)}), f32[16,12,192]{2,1,0:T(8,128)S(1)}, u32[]{:S(2)}, u32[]{:S(2)}) async-start(f32[16,12,192]{2,1,0:T(8,128)} %bitcast.3), calls=%async_computation.3 | async-start | bytes 524288 | tf_op jit(solution)/shard_map/all_to_all | solution.py:203
  104.8 3.0 %collective-permute-start.8 = (f32[128]{0:T(128)S(1)}, f32[128]{0:T(128)S(1)}, u32[]{:S(2)}, u32[]{:S(2)}) collective-permute-start(f32[128]{0:T(128)S(1)} %get-tuple-element.24), channel_id=1, source_target_pairs={{0,64},{64,0},{1,65},{65,1},{2,66},{66,2},{3,67},{67,3},{4,68},{68... | collective-permute-start | bytes 1544 | tf_op jit(solution)/shard_map/ppermute | solution.py:217

commit v13 on v12

--- a/solution.py
+++ b/solution.py
@@ -41,7 +41,7 @@
 
 def embed_kernel(
     place, arrived_ref, order_ref, gathered_ref, x0, up1, up2, far, down1, down2,
-    half_ref, unit_ref, radius_ref, rows_ref, mapping,
+    half_ref, unit_ref, inverse_ref, rows_ref, mapping,
 ):
     mapping[...] = jnp.dot(
         order_ref[...], gathered_ref[...], preferred_element_type=F32
@@ -54,14 +54,15 @@
         rows_ref[at, :] = block
         out = jnp.dot(block, mapping[...], preferred_element_type=F32)
         radius = jnp.sqrt(jnp.sum(out * out, axis=-1, keepdims=True) + 1e-06)
-        unit = out / radius
-        radius_ref[at, :] = radius
+        inverse = 1.0 / radius
+        unit = out * inverse
+        inverse_ref[at, :] = inverse
         unit_ref[at, :] = unit
         half_ref[at, :] = unit.astype(BF16)
 
 
 def grad_kernel(
-    own, grid, scalars, place, half_ref, partner_ref, unit_ref, radius_ref, rows_ref,
+    own, grid, scalars, place, half_ref, partner_ref, unit_ref, inverse_ref, rows_ref,
     local_ref, norms_ref, pre_ref, weights_ref,
 ):
     multiplier, offset = scalars[0], scalars[1]
@@ -82,7 +83,7 @@
         weights_ref[:, at] = ((-multiplier * sign) * jax.nn.sigmoid(-sign * square)).astype(BF16)
         grad = jnp.dot(weights_ref[...], partner_ref[...], preferred_element_type=F32)
         unit = unit_ref[at, :]
-        pre = (grad - unit * jnp.sum(unit * grad, axis=-1, keepdims=True)) / radius_ref[at, :]
+        pre = (grad - unit * jnp.sum(unit * grad, axis=-1, keepdims=True)) * inverse_ref[at, :]
         pre_ref[...] = pre
         if k == 0:
             wide = rows_ref[at, :].astype(F32)
@@ -155,7 +156,7 @@
     from_row = (((owner % n_x) * n_y + owner // (n_x * n_zhi)) * n_zhi + at_half) * share + row
     order = (from_row[:, None] == at[None, :]).astype(BF16)
     rows = chips * chunk.shape[0]
-    half, unit, radius, set_rows = pl.pallas_call(
+    half, unit, inverse, set_rows = pl.pallas_call(
         embed_kernel,
         out_shape=(
             jax.ShapeDtypeStruct((rows, embed), BF16),
@@ -194,7 +195,7 @@
         half,
         partner,
         unit,
-        radius,
+        inverse,
         set_rows,
     )
     pieces = lax.all_to_all(local, ("y", "x"), split_axis=0, concat_axis=0, tiled=True)

time: 118 us -> 118 us (level)
  no operation moved by 1% of the time
where the time goes in v13:
time: 118 us; the launch traced here: 117 us
  starting transfers between devices  47.8 us (41%)
  waiting for transfers between devices  30.4 us (26%)
  blocking collectives  17.7 us (15%)
  Pallas kernels  11.7 us (10%)
  other arithmetic  4.36 us (4%)
  local copies, waits for them, and re-layouts  3.2 us (3%)
  between operations  2.1 us (2%)
    all_to_all x1, blocking collectives, on_device(): lax.all_to_all(local, ('y', 'x'), split_axis=0, concat_axis=0, tiled=True)  17.7 us
    ppermute x5, waiting for transfers between devices, passed_on(): return lax.ppermute(value, 'zlo', hops)  9.8 us
    ppermute x1, starting transfers between devices, on_device(): chunk = jnp.concatenate([mine, lax.ppermute(sent, 'core', SWAP)], axis=0)  8.79 us
    ppermute x5, starting transfers between devices, passed_on(): return lax.ppermute(value, 'zlo', hops)  8.39 us
    all_to_all x1, waiting for transfers between devices, on_device(): lax.all_to_all(totals.reshape(2 * n_zhi * chips, share, columns), ('zhi',...  8.07 us
    all_to_all x1, starting transfers between devices, on_device(): lax.all_to_all(totals.reshape(2 * n_zhi * chips, share, columns), ('zhi',...  7.15 us
    all_to_all x1, starting transfers between devices, on_device(): near = lax.all_to_all(copies, 'y', split_axis=0, concat_axis=0)  6.82 us
    all_to_all x1, waiting for transfers between devices, on_device(): near = lax.all_to_all(copies, 'y', split_axis=0, concat_axis=0)  6.03 us
  transfers between devices with their start and end apart: 12, of which 7 were waited for; matrix products, arithmetic and copies ran while one was open for 3% of the time, Pallas kernels for 2%

profile of v13, /device:TPU:1, one launch (start us, length us, event | category | flops | bytes accessed | tf_op | source)
XLA Modules:
  0.0 117.2 jit_solution(2480600882233731548)
XLA Ops:
  0.6 1.1 broadcast_select_fusion.2
  1.7 8.8 %collective-permute-start = (bf16[128,768]{1,0:T(8,128)(2,1)S(1)}, bf16[128,768]{1,0:T(8,128)(2,1)S(1)}, u32[]{:S(2)}, u32[]{:S(2)}) collective-permute-start(bf16[128,768]{1,0:T(8,128)(2,1)S(1)} %get-tuple-element.27), channel_id=1, source_target_pairs={{0,64},{64,0},{1,65},{65,1},{2,66},{66,2},{3,67},{67,3},{4,68},{68... | collective-permute-start | bytes 589832 | tf_op jit(solution)/shard_map/ppermute | solution.py:127
  10.5 0.8 broadcast_select_fusion.3.own_ref
  11.2 0.0 copy-start.1
  11.2 5.3 %collective-permute-start.5 = (bf16[12,768]{1,0:T(8,128)(2,1)S(1)}, bf16[12,768]{1,0:T(8,128)(2,1)S(1)}, u32[]{:S(2)}, u32[]{:S(2)}) collective-permute-start(bf16[12,768]{1,0:T(8,128)(2,1)S(1)} %broadcast_select_fusion.3.own_ref), channel_id=1, source_target_pairs={{0,4},{4,0},{1,5},{5,1},{2,6},{6,2},{3,7},{7,3},{8,12},{12,8},{9,1... | collective-permute-start | bytes 55304 | tf_op jit(solution)/shard_map/ppermute | solution.py:124
  16.5 0.0 collective-permute-done
  16.6 3.1 %collective-permute-start.1 = (bf16[256,768]{1,0:T(8,128)(2,1)S(1)}, bf16[256,768]{1,0:T(8,128)(2,1)S(1)}, u32[]{:S(2)}, u32[]{:S(2)}) collective-permute-start(bf16[256,768]{1,0:T(8,128)(2,1)S(1)} %pad_maximum_fusion.x0), channel_id=1, source_target_pairs={{0,128},{128,256},{256,384},{1,129},{129,257},{257,385},{2,130},{1... | collective-permute-start | bytes 1179656 | tf_op jit(solution)/shard_map/ppermute | solution.py:22
  19.7 1.3 %collective-permute-start.2 = (bf16[256,768]{1,0:T(8,128)(2,1)S(1)}, bf16[256,768]{1,0:T(8,128)(2,1)S(1)}, u32[]{:S(2)}, u32[]{:S(2)}) collective-permute-start(bf16[256,768]{1,0:T(8,128)(2,1)S(1)} %pad_maximum_fusion.x0), channel_id=1, source_target_pairs={{128,0},{256,128},{384,256},{129,1},{257,129},{385,257},{130,2},{2... | collective-permute-start | bytes 1179656 | tf_op jit(solution)/shard_map/ppermute | solution.py:22
  21.0 0.0 collective-permute-done.5.other_ref
  21.0 0.0 copy-done.1
  21.0 0.0 copy-start.2
  21.0 0.6 copy-done.2
  21.6 1.5 %shard_map.94 = bf16[8,24,768]{2,1,0:T(8,128)(2,1)} custom-call(bf16[12,768]{1,0:T(8,128)(2,1)} %copy-done.1, bf16[12,768]{1,0:T(8,128)(2,1)} %copy-done.2), custom_call_target="tpu_custom_call" | custom-call | flops 4000000000 | bytes 524288 | tf_op jit(solution)/shard_map/pallas_call | solution.py:142
  23.1 6.8 %all-to-all-start = ((bf16[8,24,768]{2,1,0:T(8,128)(2,1)}), bf16[8,24,768]{2,1,0:T(8,128)(2,1)S(1)}, u32[]{:S(2)}, u32[]{:S(2)}) async-start(bf16[8,24,768]{2,1,0:T(8,128)(2,1)} %shard_map.94), calls=%async_computation | async-start | bytes 589824 | tf_op jit(solution)/shard_map/all_to_all | solution.py:149
  29.9 0.0 collective-permute-done.1.up1
  29.9 1.7 %collective-permute-done.2.down1 = bf16[256,768]{1,0:T(8,128)(2,1)S(1)} collective-permute-done((bf16[256,768]{1,0:T(8,128)(2,1)S(1)}, bf16[256,768]{1,0:T(8,128)(2,1)S(1)}, u32[]{:S(2)}, u32[]{:S(2)}) %collective-permute-start.2) | collective-permute-done | bytes 393248 | tf_op jit(solution)/shard_map/ppermute | solution.py:22
  31.7 0.8 broadcast_select_fusion
  32.5 1.3 %collective-permute-start.3 = (bf16[256,768]{1,0:T(8,128)(2,1)}, bf16[256,768]{1,0:T(8,128)(2,1)}, u32[]{:S(2)}, u32[]{:S(2)}) collective-permute-start(bf16[256,768]{1,0:T(8,128)(2,1)} %broadcast_select_fusion), channel_id=1, source_target_pairs={{128,384},{256,0},{129,385},{257,1},{130,386},{258,2},{131,387},{2... | collective-permute-start | bytes 1179656 | tf_op jit(solution)/shard_map/ppermute | solution.py:22
  33.8 1.4 %collective-permute-start.4 = (bf16[256,768]{1,0:T(8,128)(2,1)S(1)}, bf16[256,768]{1,0:T(8,128)(2,1)}, u32[]{:S(2)}, u32[]{:S(2)}) collective-permute-start(bf16[256,768]{1,0:T(8,128)(2,1)S(1)} %collective-permute-done.1.up1), channel_id=1, source_target_pairs={{128,256},{256,384},{129,257},{257,385},{130,258},{258,386},{131,2... | collective-permute-start | bytes 1179656 | tf_op jit(solution)/shard_map/ppermute | solution.py:22
  35.2 6.0 %all-to-all-done = bf16[8,24,768]{2,1,0:T(8,128)(2,1)S(1)} async-done(((bf16[8,24,768]{2,1,0:T(8,128)(2,1)}), bf16[8,24,768]{2,1,0:T(8,128)(2,1)S(1)}, u32[]{:S(2)}, u32[]{:S(2)}) %all-to-all-start) | async-done | bytes 294944 | tf_op jit(solution)/shard_map/all_to_all | solution.py:149
  41.2 1.1 broadcast_in_dim.17
  42.3 4.0 %all-to-all-start.1 = ((bf16[4,192,768]{2,1,0:T(8,128)(2,1)}), bf16[4,192,768]{2,1,0:T(8,128)(2,1)S(1)}, u32[]{:S(2)}, u32[]{:S(2)}) async-start(bf16[4,192,768]{2,1,0:T(8,128)(2,1)} %broadcast_in_dim.17), calls=%async_computation.1 | async-start | bytes 2359296 | tf_op jit(solution)/shard_map/all_to_all | solution.py:28
  46.3 0.3 fusion.order_ref
  46.6 1.3 %collective-permute-start.6 = (bf16[256,768]{1,0:T(8,128)(2,1)S(1)}, bf16[256,768]{1,0:T(8,128)(2,1)}, u32[]{:S(2)}, u32[]{:S(2)}) collective-permute-start(bf16[256,768]{1,0:T(8,128)(2,1)S(1)} %collective-permute-done.2.down1), channel_id=1, source_target_pairs={{128,0},{256,128},{129,1},{257,129},{130,2},{258,130},{131,3},{259... | collective-permute-start | bytes 1179656 | tf_op jit(solution)/shard_map/ppermute | solution.py:22
  47.9 0.0 collective-permute-done.3.far_ref.far
  47.9 0.0 collective-permute-done.4.up_ref.up2
  47.9 0.6 shard_map.93.arrived_ref
  48.5 8.0 %collective-permute-done.6.down2 = bf16[256,768]{1,0:T(8,128)(2,1)} collective-permute-done((bf16[256,768]{1,0:T(8,128)(2,1)S(1)}, bf16[256,768]{1,0:T(8,128)(2,1)}, u32[]{:S(2)}, u32[]{:S(2)}) %collective-permute-start.6) | collective-permute-done | bytes 393248 | tf_op jit(solution)/shard_map/ppermute | solution.py:22
  56.6 3.8 %all-to-all-done.1 = bf16[4,192,768]{2,1,0:T(8,128)(2,1)S(1)} async-done(((bf16[4,192,768]{2,1,0:T(8,128)(2,1)}), bf16[4,192,768]{2,1,0:T(8,128)(2,1)S(1)}, u32[]{:S(2)}, u32[]{:S(2)}) %all-to-all-start.1) | async-done | bytes 1179680 | tf_op jit(solution)/shard_map/all_to_all | solution.py:28
  60.4 0.0 copy-start
  60.4 0.7 copy-done
  61.1 3.8 %shard_map.95 = (bf16[1024,768]{1,0:T(8,128)(2,1)S(1)}, f32[1024,768]{1,0:T(8,128)S(1)}, f32[1024,1]{1,0:T(8,128)S(1)}, bf16[1024,768]{1,0:T(8,128)(2,1)S(1)}) custom-call(s32[1]{0:T(128)} %bitcast.place, f32[8,128]{1,0:T(8,128)S(1)} %copy-done, bf16[768,768]{1,0:T(8,128)(2,1)S(1)} %fusion.order_ref, bf16[768,768]{1,0:T(8,128)(2,1)S(1)} %bitcast.5, ...), custom_call_target="tpu_custom_call" | custom-call | flops 2113929216 | bytes 8388608 | tf_op jit(solution)/shard_map/pallas_call | solution.py:159
  64.9 5.3 %collective-permute-start.7 = (bf16[1024,768]{1,0:T(8,128)(2,1)S(1)}, bf16[1024,768]{1,0:T(8,128)(2,1)S(1)}, u32[]{:S(2)}, u32[]{:S(2)}) collective-permute-start(bf16[1024,768]{1,0:T(8,128)(2,1)S(1)} %get-tuple-element.10.half_ref), channel_id=1, source_target_pairs={{0,64},{64,0},{1,65},{65,1},{2,66},{66,2},{3,67},{67,3},{4,68},{68... | collective-permute-start | bytes 4718600 | tf_op jit(solution)/shard_map/ppermute | solution.py:177
  71.5 0.1 pad_maximum_fusion.3.scalars
  71.6 1.6 %collective-permute-done.7.partner_ref = bf16[1024,768]{1,0:T(8,128)(2,1)S(1)} collective-permute-done((bf16[1024,768]{1,0:T(8,128)(2,1)S(1)}, bf16[1024,768]{1,0:T(8,128)(2,1)S(1)}, u32[]{:S(2)}, u32[]{:S(2)}) %collective-permute-start.7) | collective-permute-done | bytes 1572896 | tf_op jit(solution)/shard_map/ppermute | solution.py:177
  73.2 5.9 %shard_map.96 = (bf16[32,24,192]{2,1,0:T(8,128)(2,1)S(1)}, f32[256,1]{1,0:T(8,128)S(1)}) custom-call(f32[2]{0:T(128)S(1)} %pad_maximum_fusion.3.scalars, s32[1]{0:T(128)} %bitcast.place, bf16[1024,768]{1,0:T(8,128)(2,1)S(1)} %get-tuple-element.10.half_ref, bf16[1024,768]{1,0:T(8,128)(2,1)S(1)} %collective-permute-done.7.partner_ref, ...), custom_call_target="tpu_custom_call" | custom-call | flops 3221225472 | bytes 8388608 | tf_op jit(solution)/shard_map/pallas_call | solution.py:179
  79.1 17.7 %all_to_all.20 = bf16[32,24,192]{2,1,0:T(8,128)(2,1)S(1)} all-to-all(bf16[32,24,192]{2,1,0:T(8,128)(2,1)S(1)} %get-tuple-element.14), channel_id=1, replica_groups=mesh['zlo'=4,'core'=2,'y'=8,'zhi'=2,'x'=4] {'y','x'}, dimensions={0} | all-to-all | bytes 589824 | tf_op jit(solution)/shard_map/all_to_all | solution.py:201
  96.8 0.1 convert_reduce_fusion
  96.9 0.7 broadcast_in_dim.19
  97.6 7.2 %all-to-all-start.3 = ((f32[16,12,192]{2,1,0:T(8,128)}), f32[16,12,192]{2,1,0:T(8,128)S(1)}, u32[]{:S(2)}, u32[]{:S(2)}) async-start(f32[16,12,192]{2,1,0:T(8,128)} %bitcast.3), calls=%async_computation.3 | async-start | bytes 524288 | tf_op jit(solution)/shard_map/all_to_all | solution.py:204
  104.8 0.1 slice_reduce_fusion
  104.9 2.0 %collective-permute-start.8 = (f32[128]{0:T(128)S(1)}, f32[128]{0:T(128)S(1)}, u32[]{:S(2)}, u32[]{:S(2)}) collective-permute-start(f32[128]{0:T(128)S(1)} %get-tuple-element.24), channel_id=1, source_target_pairs={{0,64},{64,0},{1,65},{65,1},{2,66},{66,2},{3,67},{67,3},{4,68},{68... | collective-permute-start | bytes 1544 | tf_op jit(solution)/shard_map/ppermute | solution.py:218
  106.9 1.0 collective-permute-done.8
  107.9 0.5 broadcast_select_fusion.4
  108.4 8.1 %all-to-all-done.3 = f32[16,12,192]{2,1,0:T(8,128)S(1)} async-done(((f32[16,12,192]{2,1,0:T(8,128)}), f32[16,12,192]{2,1,0:T(8,128)S(1)}, u32[]{:S(2)}, u32[]{:S(2)}) %all-to-all-start.3) | async-done | bytes 147488 | tf_op jit(solution)/shard_map/all_to_all | solution.py:204
  116.5 0.7 pad_maximum_fusion.1
  (4 shorter events, 0.1 us)
Async XLA Ops:
  1.7 14.8 %collective-permute-start = (bf16[128,768]{1,0:T(8,128)(2,1)S(1)}, bf16[128,768]{1,0:T(8,128)(2,1)S(1)}, u32[]{:S(2)}, u32[]{:S(2)}) collective-permute-start(bf16[128,768]{1,0:T(8,128)(2,1)S(1)} %get-tuple-element.27), channel_id=1, source_target_pairs={{0,64},{64,0},{1,65},{65,1},{2,66},{66,2},{3,67},{67,3},{4,68},{68... | collective-permute-start | bytes 589832 | tf_op jit(solution)/shard_map/ppermute | solution.py:127
  11.2 9.7 %copy-start.1 = (bf16[12,768]{1,0:T(8,128)(2,1)}, bf16[12,768]{1,0:T(8,128)(2,1)S(1)}, u32[]{:S(2)}) copy-start(bf16[12,768]{1,0:T(8,128)(2,1)S(1)} %broadcast_select_fusion.3.own_ref) | copy-start | bytes 55300
  11.2 9.7 %collective-permute-start.5 = (bf16[12,768]{1,0:T(8,128)(2,1)S(1)}, bf16[12,768]{1,0:T(8,128)(2,1)S(1)}, u32[]{:S(2)}, u32[]{:S(2)}) collective-permute-start(bf16[12,768]{1,0:T(8,128)(2,1)S(1)} %broadcast_select_fusion.3.own_ref), channel_id=1, source_target_pairs={{0,4},{4,0},{1,5},{5,1},{2,6},{6,2},{3,7},{7,3},{8,12},{12,8},{9,1... | collective-permute-start | bytes 55304 | tf_op jit(solution)/shard_map/ppermute | solution.py:124
  16.6 13.4 %collective-permute-start.1 = (bf16[256,768]{1,0:T(8,128)(2,1)S(1)}, bf16[256,768]{1,0:T(8,128)(2,1)S(1)}, u32[]{:S(2)}, u32[]{:S(2)}) collective-permute-start(bf16[256,768]{1,0:T(8,128)(2,1)S(1)} %pad_maximum_fusion.x0), channel_id=1, source_target_pairs={{0,128},{128,256},{256,384},{1,129},{129,257},{257,385},{2,130},{1... | collective-permute-start | bytes 1179656 | tf_op jit(solution)/shard_map/ppermute | solution.py:22
  19.7 12.0 %collective-permute-start.2 = (bf16[256,768]{1,0:T(8,128)(2,1)S(1)}, bf16[256,768]{1,0:T(8,128)(2,1)S(1)}, u32[]{:S(2)}, u32[]{:S(2)}) collective-permute-start(bf16[256,768]{1,0:T(8,128)(2,1)S(1)} %pad_maximum_fusion.x0), channel_id=1, source_target_pairs={{128,0},{256,128},{384,256},{129,1},{257,129},{385,257},{130,2},{2... | collective-permute-start | bytes 1179656 | tf_op jit(solution)/shard_map/ppermute | solution.py:22
  21.0 0.6 copy-start.2
  23.1 18.1 %all-to-all-start = ((bf16[8,24,768]{2,1,0:T(8,128)(2,1)}), bf16[8,24,768]{2,1,0:T(8,128)(2,1)S(1)}, u32[]{:S(2)}, u32[]{:S(2)}) async-start(bf16[8,24,768]{2,1,0:T(8,128)(2,1)} %shard_map.94), calls=%async_computation | async-start | bytes 589824 | tf_op jit(solution)/shard_map/all_to_all | solution.py:149
  32.5 15.4 %collective-permute-start.3 = (bf16[256,768]{1,0:T(8,128)(2,1)}, bf16[256,768]{1,0:T(8,128)(2,1)}, u32[]{:S(2)}, u32[]{:S(2)}) collective-permute-start(bf16[256,768]{1,0:T(8,128)(2,1)} %broadcast_select_fusion), channel_id=1, source_target_pairs={{128,384},{256,0},{129,385},{257,1},{130,386},{258,2},{131,387},{2... | collective-permute-start | bytes 1179656 | tf_op jit(solution)/shard_map/ppermute | solution.py:22
  33.8 14.1 %collective-permute-start.4 = (bf16[256,768]{1,0:T(8,128)(2,1)S(1)}, bf16[256,768]{1,0:T(8,128)(2,1)}, u32[]{:S(2)}, u32[]{:S(2)}) collective-permute-start(bf16[256,768]{1,0:T(8,128)(2,1)S(1)} %collective-permute-done.1.up1), channel_id=1, source_target_pairs={{128,256},{256,384},{129,257},{257,385},{130,258},{258,386},{131,2... | collective-permute-start | bytes 1179656 | tf_op jit(solution)/shard_map/ppermute | solution.py:22
  42.3 18.1 %all-to-all-start.1 = ((bf16[4,192,768]{2,1,0:T(8,128)(2,1)}), bf16[4,192,768]{2,1,0:T(8,128)(2,1)S(1)}, u32[]{:S(2)}, u32[]{:S(2)}) async-start(bf16[4,192,768]{2,1,0:T(8,128)(2,1)} %broadcast_in_dim.17), calls=%async_computation.1 | async-start | bytes 2359296 | tf_op jit(solution)/shard_map/all_to_all | solution.py:28
  46.6 10.0 %collective-permute-start.6 = (bf16[256,768]{1,0:T(8,128)(2,1)S(1)}, bf16[256,768]{1,0:T(8,128)(2,1)}, u32[]{:S(2)}, u32[]{:S(2)}) collective-permute-start(bf16[256,768]{1,0:T(8,128)(2,1)S(1)} %collective-permute-done.2.down1), channel_id=1, source_target_pairs={{128,0},{256,128},{129,1},{257,129},{130,2},{258,130},{131,3},{259... | collective-permute-start | bytes 1179656 | tf_op jit(solution)/shard_map/ppermute | solution.py:22
  60.4 0.7 copy-start
  64.9 8.3 %collective-permute-start.7 = (bf16[1024,768]{1,0:T(8,128)(2,1)S(1)}, bf16[1024,768]{1,0:T(8,128)(2,1)S(1)}, u32[]{:S(2)}, u32[]{:S(2)}) collective-permute-start(bf16[1024,768]{1,0:T(8,128)(2,1)S(1)} %get-tuple-element.10.half_ref), channel_id=1, source_target_pairs={{0,64},{64,0},{1,65},{65,1},{2,66},{66,2},{3,67},{67,3},{4,68},{68... | collective-permute-start | bytes 4718600 | tf_op jit(solution)/shard_map/ppermute | solution.py:177
  97.6 18.9 %all-to-all-start.3 = ((f32[16,12,192]{2,1,0:T(8,128)}), f32[16,12,192]{2,1,0:T(8,128)S(1)}, u32[]{:S(2)}, u32[]{:S(2)}) async-start(f32[16,12,192]{2,1,0:T(8,128)} %bitcast.3), calls=%async_computation.3 | async-start | bytes 524288 | tf_op jit(solution)/shard_map/all_to_all | solution.py:204
  104.9 3.0 %collective-permute-start.8 = (f32[128]{0:T(128)S(1)}, f32[128]{0:T(128)S(1)}, u32[]{:S(2)}, u32[]{:S(2)}) collective-permute-start(f32[128]{0:T(128)S(1)} %get-tuple-element.24), channel_id=1, source_target_pairs={{0,64},{64,0},{1,65},{65,1},{2,66},{66,2},{3,67},{67,3},{4,68},{68... | collective-permute-start | bytes 1544 | tf_op jit(solution)/shard_map/ppermute | solution.py:218
